TPU v7x, 32 devices: a whole 2x2x4 slice. The times are simulated.
32 devices in a mesh: lat: 4 (over z), lon: 2 (over core), ens: 4 (over y, x).
Axes of the slice: x: 2, y: 2, z: 4, core: 2. Of those that a mesh axis runs over, the one named last changes fastest.
Arguments:
- fields: bfloat16 [128, 256, 256], P(('ens', 'lat'), 'lon'), parts along dimension 0, may hold values from -6 to 6
- lon_taps: float32 [32, 4, 9], replicated, may hold values from -2 to 2
- lat_taps: bfloat16 [32, 4, 6], P('lat'), may hold values from -2.5 to 2.5
- cycle_taps: bfloat16 [4, 8, 256], replicated, may hold values from -0.375 to 0.375
- band_start: int32 [32], P('lat'), may hold values from -4 to 30, as said below
- band_width: int32 [32], P('lat'), may hold values from 4 to 6, as said below
- mixing: bfloat16 [4, 256, 256], replicated, may hold values from -0.1875 to 0.1875
Outputs:
- layer_out: bfloat16 [128, 256, 256], P(('ens', 'lat'), 'lon'), parts along dimension 0
There are 4 independent parts, one for each index of `ens`. A program takes and returns all parts, laid end to end along the dimension named above; an argument that names none is the same for every part. Nothing has to cross between parts.
Inputs may be any that keep to these rules, and one draw needn't show every extreme that they name: band_start[i] = i - 4 + s with s in 0 .. 3; s = 0 where i % 8 == 0 and s = 3 where i % 8 == 7. band_width[i] = 6 where i % 8 is 0 or 7.
All inputs are finite; a program needn't handle non-finite values.
Results may differ from a plain program's by a relative error of at most 0.0052.
Values may be sent and summed in bfloat16 or wider, within the bound.
No kernel may reach another device: no remote copies, remote signals or barrier semaphores. Data moves between devices by JAX's collectives and lax.ppermute only.
A program may use at most 64 MiB of HBM per device.

v0:
```python
import jax
import jax.numpy as jnp
from jax import lax
from jax.sharding import PartitionSpec as P

HALO = 4


def extended_2(cells, sides, width, closed):
    for axis, dim in sides:
        count = lax.axis_size(axis)
        ends = count if closed else count - 1
        head = lax.slice_in_dim(cells, 0, width, axis=dim)
        tail = lax.slice_in_dim(cells, cells.shape[dim] - width, cells.shape[dim], axis=dim)
        cells = jnp.concatenate(
            [
                lax.ppermute(tail, axis, [(i, (i + 1) % count) for i in range(ends)]),
                cells,
                lax.ppermute(head, axis, [((i + 1) % count, i) for i in range(ends)]),
            ],
            axis=dim,
        )
    return cells


def toeplitz(coef, base, out_count, in_count, cycle_len):
    lead = coef.shape[:-1]
    window_len = out_count + in_count - 1
    tripled = jnp.concatenate([coef, coef, coef], axis=-1)
    begin = (base - in_count + 1) % cycle_len
    window = lax.dynamic_slice_in_dim(tripled, begin, window_len, len(lead))
    flipped = jnp.flip(window, axis=-1)
    rolled = jnp.roll(flipped, -(out_count - 1), axis=-1)
    tiled = jnp.tile(rolled, (1,) * len(lead) + (out_count,))
    cut = tiled[..., : out_count * (window_len - 1)]
    shaped = cut.reshape(lead + (out_count, window_len - 1))
    return shaped[..., :in_count]


def cycle_fold(coef, col_start, col_count, cycle_len, block_in):
    width_in = block_in.shape[1]
    circ = toeplitz(coef, col_start, col_count, width_in, cycle_len)
    return jnp.einsum("kpjm,pmc->kpjc", circ, block_in, preferred_element_type=jnp.float32)


def shards(fields, lon_taps, lat_taps, cycle_taps, band_start, band_width, mixing):
    row_count, col_count, chan_count = fields.shape
    basis_count = lon_taps.shape[1]
    reach_cells = (lon_taps.shape[2] - 1) // 2
    band_len = lat_taps.shape[2]
    polar_rows = row_count // 2
    lat_count = lax.axis_size("lat")
    lon_count = lax.axis_size("lon")
    cycle_len = lon_count * col_count
    lat_pos = lax.axis_index("lat")
    lon_pos = lax.axis_index("lon")
    leading = 0
    source_rows = fields.shape[0]
    padded = extended_2(fields, (("lon", 1),), reach_cells, True)
    taps_padded = jnp.pad(lon_taps, ((HALO, HALO), (0, 0), (0, 0)))
    taps_here = lax.dynamic_slice_in_dim(
        taps_padded, lat_pos * row_count + HALO - leading, source_rows, 0
    )
    accum = jnp.zeros((basis_count, source_rows, col_count, chan_count), jnp.float32)
    for offset in range(2 * reach_cells + 1):
        tap_now = jnp.transpose(taps_here[:, :, offset])
        accum = accum + tap_now[:, :, None, None] * padded[
            None, :, offset : offset + col_count, :
        ].astype(jnp.float32)
    near_rows = accum.astype(jnp.bfloat16)
    at_top = lat_pos == 0
    slot_start = jnp.where(at_top, 0, row_count - polar_rows).astype(jnp.int32)
    slot_rows = lax.dynamic_slice_in_dim(fields, slot_start, polar_rows, 0)
    col_start = lon_pos * col_count
    coef_start = jnp.where(at_top, 0, polar_rows).astype(jnp.int32)
    coef = lax.dynamic_slice_in_dim(cycle_taps, coef_start, polar_rows, 1)
    polar_sum = cycle_fold(
        coef, col_start, col_count, cycle_len, lax.all_gather(slot_rows, "lon", axis=1, tiled=True)
    )
    polar_z = polar_sum.astype(jnp.bfloat16)
    placed = lax.dynamic_update_slice_in_dim(
        jnp.zeros_like(near_rows), polar_z, slot_start + leading, 1
    )
    global_rows = lat_pos * row_count - leading + jnp.arange(source_rows, dtype=jnp.int32)
    is_polar = (global_rows < polar_rows) | (global_rows >= lat_count * row_count - polar_rows)
    filtered = jnp.where(is_polar[None, :, None, None], placed, near_rows)
    extended = extended_2(filtered, (("lat", 1),), HALO, False)
    ext_rows = row_count + 2 * HALO
    base_row = lat_pos * row_count
    steps_band = jnp.arange(band_len, dtype=jnp.int32)
    target = band_start[:, None] - base_row + HALO + steps_band[None, :]
    usable = steps_band[None, :] < band_width[:, None]
    ext_ids = jnp.arange(ext_rows, dtype=jnp.int32)
    select = ((target[:, :, None] == ext_ids[None, None, :]) & usable[:, :, None]).astype(
        jnp.float32
    )
    band_matrix = jnp.einsum("lkt,lte->kle", lat_taps.astype(jnp.float32), select).astype(
        jnp.bfloat16
    )
    hidden = jnp.einsum(
        "kle,kejc->ljkc", band_matrix, extended, preferred_element_type=jnp.float32
    ).astype(jnp.bfloat16)
    flat_hidden = hidden.reshape(row_count * col_count, basis_count * chan_count)
    flat_mix = mixing.reshape(basis_count * chan_count, chan_count)
    mixed = jnp.dot(flat_hidden, flat_mix, preferred_element_type=jnp.float32).reshape(
        row_count, col_count, chan_count
    )
    return (fields.astype(jnp.float32) + mixed).astype(jnp.bfloat16)


def solution(mesh):
    in_specs = (
        P(("ens", "lat"), "lon", None),
        P(),
        P("lat", None, None),
        P(),
        P("lat"),
        P("lat"),
        P(),
    )
    out_specs = P(("ens", "lat"), "lon", None)
    return jax.shard_map(shards, mesh=mesh, in_specs=in_specs, out_specs=out_specs, check_vma=False)
```

profile of v0, /device:TPU:0, one launch (start us, length us, event | category | flops | bytes accessed | tf_op | source)
XLA Modules:
  0.0 101.3 jit_solution(9050637405044125851)
XLA Ops:
  0.0 0.0 copy-start
  0.0 0.8 fusion.43
  0.9 0.5 collective-permute-start
  1.4 0.1 collective-permute-start.1
  1.5 0.7 constant_dynamic-slice_fusion.9
  2.2 0.1 fusion.32
  2.3 1.0 constant_dynamic-slice_fusion.10
  3.3 0.2 slice.92
  3.5 0.1 slice.94
  3.6 0.1 tile.4
  3.8 4.0 %tile.10 = bf16[4,4,49024]{2,1,0:T(4,128)(2,1)} reshape(bf16[4,4,128,383]{3,2,1,0:T(8,128)(2,1)S(1)} %tile.4) | data formatting | bytes 3137536 | tf_op jit(solution)/shard_map/tile | solution.py:34
  7.7 1.4 %slice-done = bf16[4,4,48896]{2,1,0:T(4,128)(2,1)S(1)} async-done(((bf16[4,4,49024]{2,1,0:T(4,128)(2,1)}), bf16[4,4,48896]{2,1,0:T(4,128)(2,1)S(1)}, s32[]{:S(2)}) %slice-start) | async-done | bytes 1564696 | tf_op jit(solution)/shard_map/slice | solution.py:35
  9.2 4.4 %reshape.90 = bf16[4,4,128,382]{3,2,1,0:T(8,128)(2,1)} reshape(bf16[4,4,48896]{2,1,0:T(4,128)(2,1)S(1)} %slice-done) | data formatting | bytes 3129344 | tf_op jit(solution)/shard_map/reshape | solution.py:36
  13.6 0.2 copy.54
  13.7 2.2 %all_gather.3 = bf16[4,256,256]{1,2,0:T(8,128)(2,1)S(1)} all-gather(bf16[4,128,256]{1,2,0:T(8,128)(2,1)S(1)} %copy.54), channel_id=1, replica_groups=mesh['lat'=4,'lon'=2,'ens'=4] {'lon'}, dimensions={1}, use_global_device_ids=true | all-gather | bytes 786432 | tf_op jit(solution)/shard_map/all_gather | solution.py:78
  16.0 1.8 %broadcast_in_dim.8 = bf16[4,8,128,256]{2,3,0,1:T(8,128)(2,1)} broadcast(bf16[]{:T(256)} %constant.37.clone.1), dimensions={} | broadcast | bytes 2097154 | tf_op jit(solution)/shard_map/broadcast_in_dim | solution.py:82
  17.8 2.7 %fusion.8 = bf16[4,8,128,256]{2,3,0,1:T(8,128)(2,1)} fusion(bf16[4,8,128,256]{2,3,0,1:T(8,128)(2,1)} %broadcast_in_dim.8, s32[]{:T(128)S(6)} %select_n.25, bf16[4,256,256]{1,2,0:T(8,128)(2,1)S(1)} %all_gather.3, bf16[4,4,128,382]{3,2,1,0:T(8,128)(2,1)} %reshape.90), kind=kOutput, calls=%fused_computation.9 | convolution fusion | flops 268959744 | bytes 2621444 | tf_op jit(solution)/shard_map/kpjm,pmc->kpjc/dot_general | solution.py:43
  20.5 0.0 copy-done.2
  20.5 0.1 fusion.35
  20.6 0.0 copy-done.1
  20.6 1.2 %copy.39 = f32[8,128,256]{1,2,0:T(8,128)} copy(bf16[8,128,256]{2,1,0:T(8,128)(2,1)S(1)} %copy-done.1) | data formatting | bytes 1572864 | tf_op jit(solution)/shard_map/convert_element_type | solution.py:108
  21.7 0.1 copy.30
  21.8 0.1 copy.32
  21.9 0.1 copy.34
  22.0 0.1 copy.36
  22.1 0.1 copy.38
  22.1 0.1 copy.40
  22.2 0.1 copy.42
  22.3 0.1 copy.44
  22.4 0.1 copy.46
  22.5 0.0 collective-permute-done
  22.5 1.9 %fusion.20 = (f32[8,128,256]{2,1,0:T(8,128)}, f32[8,128,256]{2,1,0:T(8,128)}, f32[8,128,256]{2,1,0:T(8,128)S(1)}, f32[8,128,256]{2,1,0:T(8,128)S(1)}, bf16[8,132,256]{2,1,0:T(8,128)(2,1)S(1)}) fusion(bf16[8,4,256]{2,1,0:T(4,128)(2,1)S(1)} %collective-permute-done, bf16[8,128,256]{2,1,0:T(8,128)(2,1)S(1)} %copy-done.1), kind=kLoop, calls=%fused_computation.21 | loop fusion | flops 4194303 | bytes 5259264 | tf_op jit(solution)/shard_map/convert_element_type | solution.py:69
  24.4 0.0 collective-permute-done.1
  24.4 2.2 %slice_convert_fusion.3 = (f32[8,128,256]{2,1,0:T(8,128)}, f32[8,128,256]{2,1,0:T(8,128)}, f32[8,128,256]{2,1,0:T(8,128)}, f32[8,128,256]{2,1,0:T(8,128)}) fusion(bf16[8,132,256]{2,1,0:T(8,128)(2,1)S(1)} %constant_dynamic-update-slice_fusion), kind=kLoop, calls=%fused_computation.27 | loop fusion | flops 1048576 | bytes 6291456 | tf_op jit(solution)/shard_map/convert_element_type | solution.py:69
  26.6 2.5 %copy.41 = f32[8,128,256]{1,2,0:T(8,128)} copy(f32[8,128,256]{2,1,0:T(8,128)} %get-tuple-element.7) | data formatting | bytes 2097152 | tf_op jit(solution)/shard_map/convert_element_type | solution.py:69
  29.1 2.6 %copy.43 = f32[8,128,256]{1,2,0:T(8,128)} copy(f32[8,128,256]{2,1,0:T(8,128)} %get-tuple-element.10) | data formatting | bytes 2097152 | tf_op jit(solution)/shard_map/convert_element_type | solution.py:69
  31.7 2.6 %copy.45 = f32[8,128,256]{1,2,0:T(8,128)} copy(f32[8,128,256]{2,1,0:T(8,128)} %get-tuple-element.9) | data formatting | bytes 2097152 | tf_op jit(solution)/shard_map/convert_element_type | solution.py:69
  34.3 2.6 %copy.47 = f32[8,128,256]{1,2,0:T(8,128)} copy(f32[8,128,256]{2,1,0:T(8,128)} %get-tuple-element.8) | data formatting | bytes 2097152 | tf_op jit(solution)/shard_map/convert_element_type | solution.py:69
  36.9 2.5 %copy.31 = f32[8,128,256]{1,2,0:T(8,128)} copy(f32[8,128,256]{2,1,0:T(8,128)} %get-tuple-element.11) | data formatting | bytes 2097152 | tf_op jit(solution)/shard_map/convert_element_type | solution.py:69
  39.4 2.6 %copy.33 = f32[8,128,256]{1,2,0:T(8,128)} copy(f32[8,128,256]{2,1,0:T(8,128)} %get-tuple-element.12) | data formatting | bytes 2097152 | tf_op jit(solution)/shard_map/convert_element_type | solution.py:69
  42.0 1.3 %copy.35 = f32[8,128,256]{1,2,0:T(8,128)} copy(f32[8,128,256]{2,1,0:T(8,128)S(1)} %get-tuple-element.14) | data formatting | bytes 2097152 | tf_op jit(solution)/shard_map/convert_element_type | solution.py:69
  43.3 1.3 %copy.37 = f32[8,128,256]{1,2,0:T(8,128)} copy(f32[8,128,256]{2,1,0:T(8,128)S(1)} %get-tuple-element.13) | data formatting | bytes 2097152 | tf_op jit(solution)/shard_map/convert_element_type | solution.py:69
  44.7 6.3 %fusion = bf16[4,8,128,256]{2,3,0,1:T(8,128)(2,1)S(1)} fusion(bf16[4,8,128,256]{2,3,0,1:T(8,128)(2,1)} %fusion.8, f32[8,128,256]{1,2,0:T(8,128)} %copy.47, f32[4,8]{0,1:T(8,128)S(1)} %copy.46, f32[8,128,256]{1,2,0:T(8,128)} %copy.45, f32[4,8]{0,1:T(8,128)S(1)} %copy.44, f32[8,128,256]{1,2,0:T(8,128)} %copy.43, f32[4,8]{0,1:T(8,128)S(1)} %copy.42, ...), kind=kLoop, calls=%fused_computation.3 | loop fusion | flops 19922944 | bytes 13632648 | tf_op jit(solution)/shard_map/jit(_where)/select_n | solution.py:86
  51.0 0.0 copy-start.3
  51.0 0.0 copy-start.4
  51.0 0.0 copy-start.5
  51.1 1.5 %fusion.42 = (bf16[4,4,128,256]{2,3,0,1:T(8,128)(2,1)}, bf16[4,4,128,256]{2,3,0,1:T(8,128)(2,1)}) fusion(bf16[4,8,128,256]{2,3,0,1:T(8,128)(2,1)S(1)} %fusion), kind=kLoop, calls=%fused_computation.69 | loop fusion | bytes 4194304 | tf_op jit(solution)/shard_map/slice | solution.py:14
  52.5 5.9 %collective-permute-start.2 = (bf16[4,4,128,256]{2,3,0,1:T(8,128)(2,1)}, bf16[4,4,128,256]{2,3,0,1:T(8,128)(2,1)}, u32[]{:S(2)}, u32[]{:S(2)}) collective-permute-start(bf16[4,4,128,256]{2,3,0,1:T(8,128)(2,1)} %get-tuple-element.5), channel_id=1, source_target_pairs={{0,8},{8,16},{16,24},{1,9},{9,17},{17,25},{2,10},{10,18},{18,26},{... | collective-permute-start | bytes 3145736 | tf_op jit(solution)/shard_map/ppermute | solution.py:17
  58.4 1.3 %collective-permute-start.3 = (bf16[4,4,128,256]{2,3,0,1:T(8,128)(2,1)}, bf16[4,4,128,256]{2,3,0,1:T(8,128)(2,1)}, u32[]{:S(2)}, u32[]{:S(2)}) collective-permute-start(bf16[4,4,128,256]{2,3,0,1:T(8,128)(2,1)} %get-tuple-element.6), channel_id=1, source_target_pairs={{8,0},{16,8},{24,16},{9,1},{17,9},{25,17},{10,2},{18,10},{26,18},{... | collective-permute-start | bytes 3145736 | tf_op jit(solution)/shard_map/ppermute | solution.py:19
  59.7 0.0 copy-done.3
  59.7 0.1 copy.49
  59.8 0.0 copy-done.4
  59.8 0.0 copy-done.5
  59.8 0.1 iota_compare_fusion.1
  59.9 0.1 iota_add_fusion
  60.0 0.3 fusion.15
  60.3 0.1 copy.51
  60.4 20.0 %collective-permute-done.2 = bf16[4,4,128,256]{2,3,0,1:T(8,128)(2,1)} collective-permute-done((bf16[4,4,128,256]{2,3,0,1:T(8,128)(2,1)}, bf16[4,4,128,256]{2,3,0,1:T(8,128)(2,1)}, u32[]{:S(2)}, u32[]{:S(2)}) %collective-permute-start.2) | collective-permute-done | bytes 1048608 | tf_op jit(solution)/shard_map/ppermute | solution.py:17
  80.4 5.1 %collective-permute-done.3 = bf16[4,4,128,256]{2,3,0,1:T(8,128)(2,1)} collective-permute-done((bf16[4,4,128,256]{2,3,0,1:T(8,128)(2,1)}, bf16[4,4,128,256]{2,3,0,1:T(8,128)(2,1)}, u32[]{:S(2)}, u32[]{:S(2)}) %collective-permute-start.3) | collective-permute-done | bytes 1048608 | tf_op jit(solution)/shard_map/ppermute | solution.py:19
  85.5 3.4 %pad_maximum_fusion = bf16[4,16,128,256]{2,3,0,1:T(8,128)(2,1)} fusion(bf16[4,4,128,256]{2,3,0,1:T(8,128)(2,1)} %collective-permute-done.3, bf16[4,8,128,256]{2,3,0,1:T(8,128)(2,1)S(1)} %fusion, bf16[4,4,128,256]{2,3,0,1:T(8,128)(2,1)} %collective-permute-done.2), kind=kLoop, calls=%fused_computation | loop fusion | flops 4194304 | bytes 8388608 | tf_op jit(solution)/shard_map/concatenate | solution.py:15
  88.9 7.9 %copy.50 = bf16[4,16,128,256]{3,1,2,0:T(8,128)(2,1)} copy(bf16[4,16,128,256]{2,3,0,1:T(8,128)(2,1)} %pad_maximum_fusion) | data formatting | bytes 8388608 | tf_op jit(solution)/shard_map/concatenate | solution.py:15
  96.9 2.9 %fusion.44 = bf16[4,128,256,8]{2,3,1,0:T(8,128)(2,1)S(1)} fusion(bf16[4,16,128,256]{3,1,2,0:T(8,128)(2,1)} %copy.50, bf16[4,8,16,1]{2,1,3,0:T(8,128)(2,1)S(1)} %copy.51), kind=kOutput, calls=%fused_computation.71 | convolution fusion | flops 33554432 | bytes 6292480 | tf_op jit(solution)/shard_map/kle,kejc->ljkc/dot_general | solution.py:100
  99.7 0.0 copy-done
  99.8 1.6 %fusion.12 = bf16[8,128,256]{2,1,0:T(8,128)(2,1)} fusion(bf16[4,128,256,8]{2,3,1,0:T(8,128)(2,1)S(1)} %fusion.44, bf16[4,256,256]{2,1,0:T(8,128)(2,1)S(1)} %copy-done, bf16[8,128,256]{2,1,0:T(8,128)(2,1)S(1)} %copy-done.1), kind=kOutput, calls=%fused_computation.11 | convolution fusion | flops 537657344 | bytes 3670016 | tf_op jit(solution)/shard_map/dot_general | solution.py:105
  (9 shorter events, 0.1 us)
Async XLA Ops:
  0.0 99.7 %copy-start = (bf16[4,256,256]{2,1,0:T(8,128)(2,1)S(1)}, bf16[4,256,256]{2,1,0:T(8,128)(2,1)}, u32[]{:S(2)}) copy-start(bf16[4,256,256]{2,1,0:T(8,128)(2,1)} %param.13) | copy-start | bytes 1572868
  0.9 21.6 %collective-permute-start = (bf16[8,4,256]{2,1,0:T(4,128)(2,1)S(1)}, bf16[8,4,256]{2,1,0:T(4,128)(2,1)S(1)}, u32[]{:S(2)}, u32[]{:S(2)}) collective-permute-start(bf16[8,4,256]{2,1,0:T(4,128)(2,1)S(1)} %get-tuple-element.16), channel_id=1, source_target_pairs={{0,4},{4,0},{1,5},{5,1},{2,6},{6,2},{3,7},{7,3},{8,12},{12,8},{9,1... | collective-permute-start | bytes 49160 | tf_op jit(solution)/shard_map/ppermute | solution.py:17
  1.4 23.0 %collective-permute-start.1 = (bf16[8,4,256]{2,1,0:T(4,128)(2,1)S(1)}, bf16[8,4,256]{2,1,0:T(4,128)(2,1)S(1)}, u32[]{:S(2)}, u32[]{:S(2)}) collective-permute-start(bf16[8,4,256]{2,1,0:T(4,128)(2,1)S(1)} %get-tuple-element.17), channel_id=1, source_target_pairs={{4,0},{0,4},{5,1},{1,5},{6,2},{2,6},{7,3},{3,7},{12,8},{8,12},{13,... | collective-permute-start | bytes 49160 | tf_op jit(solution)/shard_map/ppermute | solution.py:19
  7.7 1.4 %slice-start = ((bf16[4,4,49024]{2,1,0:T(4,128)(2,1)}), bf16[4,4,48896]{2,1,0:T(4,128)(2,1)S(1)}, s32[]{:S(2)}) async-start(bf16[4,4,49024]{2,1,0:T(4,128)(2,1)} %tile.10), calls=%async_computation | async-start | bytes 3129344 | tf_op jit(solution)/shard_map/slice | solution.py:35
  9.1 11.3 %copy-start.2 = (f32[32,4,9]{0,1,2:T(4,128)S(1)}, f32[32,4,9]{0,1,2:T(4,128)}, u32[]{:S(2)}) copy-start(f32[32,4,9]{0,1,2:T(4,128)} %param.8) | copy-start | bytes 13828
  9.2 11.4 %copy-start.1 = (bf16[8,128,256]{2,1,0:T(8,128)(2,1)S(1)}, bf16[8,128,256]{2,1,0:T(8,128)(2,1)}, u32[]{:S(2)}) copy-start(bf16[8,128,256]{2,1,0:T(8,128)(2,1)} %param.7) | copy-start | bytes 1572868
  51.0 8.7 %copy-start.3 = (bf16[8,4,6]{0,1,2:T(4,128)(2,1)S(1)}, bf16[8,4,6]{0,1,2:T(4,128)(2,1)}, u32[]{:S(2)}) copy-start(bf16[8,4,6]{0,1,2:T(4,128)(2,1)} %param.9) | copy-start | bytes 1156
  51.0 8.8 %copy-start.4 = (s32[8]{0:T(128)S(1)}, s32[8]{0:T(128)}, u32[]{:S(2)}) copy-start(s32[8]{0:T(128)} %param.11) | copy-start | bytes 100
  51.0 8.8 %copy-start.5 = (s32[8]{0:T(128)S(1)}, s32[8]{0:T(128)}, u32[]{:S(2)}) copy-start(s32[8]{0:T(128)} %param.12) | copy-start | bytes 100
  52.5 27.9 %collective-permute-start.2 = (bf16[4,4,128,256]{2,3,0,1:T(8,128)(2,1)}, bf16[4,4,128,256]{2,3,0,1:T(8,128)(2,1)}, u32[]{:S(2)}, u32[]{:S(2)}) collective-permute-start(bf16[4,4,128,256]{2,3,0,1:T(8,128)(2,1)} %get-tuple-element.5), channel_id=1, source_target_pairs={{0,8},{8,16},{16,24},{1,9},{9,17},{17,25},{2,10},{10,18},{18,26},{... | collective-permute-start | bytes 3145736 | tf_op jit(solution)/shard_map/ppermute | solution.py:17
  58.4 27.1 %collective-permute-start.3 = (bf16[4,4,128,256]{2,3,0,1:T(8,128)(2,1)}, bf16[4,4,128,256]{2,3,0,1:T(8,128)(2,1)}, u32[]{:S(2)}, u32[]{:S(2)}) collective-permute-start(bf16[4,4,128,256]{2,3,0,1:T(8,128)(2,1)} %get-tuple-element.6), channel_id=1, source_target_pairs={{8,0},{16,8},{24,16},{9,1},{17,9},{25,17},{10,2},{18,10},{26,18},{... | collective-permute-start | bytes 3145736 | tf_op jit(solution)/shard_map/ppermute | solution.py:19
where the time goes:
time: 102 us; the launch traced here: 101 us
  local copies, waits for them, and re-layouts  44.6 us (44%)
  waiting for transfers between devices  25.1 us (25%)
  other arithmetic  14.1 us (14%)
  starting transfers between devices  7.75 us (8%)
  matrix products  7.39 us (7%)
  blocking collectives  2.24 us (2%)
    ppermute x2, waiting for transfers between devices, extended_2(): lax.ppermute(tail, axis, [(i, (i + 1) % count) for i in range(ends)])  20 us
    convert_element_type x8, local copies, waits for them, and re-layouts, shards(): accum = accum + tap_now[:, :, None, None] * padded[None, :, offset:offset...  18.1 us
    concatenate x2, local copies, waits for them, and re-layouts, extended_2(): jnp.concatenate([lax.ppermute(tail, axis, [(i, (i + 1) % count) for i in...  7.95 us
    ppermute x2, starting transfers between devices, extended_2(): lax.ppermute(tail, axis, [(i, (i + 1) % count) for i in range(ends)])  6.39 us
    select_n x1, other arithmetic, shards(): filtered = jnp.where(is_polar[None, :, None, None], placed, near_rows)  6.33 us
    ppermute x2, waiting for transfers between devices, extended_2(): lax.ppermute(head, axis, [((i + 1) % count, i) for i in range(ends)])  5.12 us
    reshape x1, local copies, waits for them, and re-layouts, toeplitz(): shaped = cut.reshape(lead + (out_count, window_len - 1))  4.41 us
    another operation x2, local copies, waits for them, and re-layouts, toeplitz(): tiled = jnp.tile(rolled, (1,) * len(lead) + (out_count,))  4.11 us
  transfers between devices with their start and end apart: 4, of which 2 were waited for; matrix products, arithmetic and copies ran while one was open for 20% of the time, Pallas kernels for 0%

commit v1 on v0

v1 whole, which is shorter than its diff:
```python
import functools

import jax
import jax.numpy as jnp
from jax import lax
from jax.experimental import pallas as pl
from jax.experimental.pallas import tpu as pltpu
from jax.sharding import PartitionSpec as P

HALO = 4
SWAP = [(0, 1), (1, 0)]


def ring(lat_count, step):
    pairs = []
    for lat in range(lat_count):
        for core in range(2):
            to = lat + (step if core == 0 else -step)
            if 0 <= to < lat_count:
                pairs.append((lat * 2 + core, to * 2 + core))
            else:
                pairs.append((lat * 2 + core, lat * 2 + 1 - core))
    return pairs


def circulants(h, out_ref, basis):
    cycle = h.shape[1]
    count = out_ref.shape[0] // basis
    for k in range(basis):
        wide = jnp.broadcast_to(h[k : k + 1], (count, cycle))
        turned = pltpu.roll(wide, 0, 1, stride=1, stride_axis=0)
        out_ref[k * count : (k + 1) * count, :] = turned.astype(jnp.bfloat16)
    return None


def own_kernel(
    lat_taps, band_start, band_width, fields, other, lon_taps, cycle_taps, mixing,
    acc, halo_mats, lag, flipped, mats, filt, hidden,
):
    rows, cols, chans = fields.shape
    basis, taps = lon_taps.shape[1:]
    reach = taps // 2
    band = lat_taps.shape[2]
    cycle = cycle_taps.shape[2]
    half = rows // 2
    lat_pos = lax.axis_index("lat")
    lat_count = lax.axis_size("lat")
    base = lat_pos * rows
    row_total = lat_count * rows

    lag[...] = jnp.zeros_like(lag)
    for slot in range(rows + 2 * HALO):
        row = jnp.clip(base - HALO + slot, 0, row_total - 1)
        lag[slot, :, 0:taps] = lon_taps[row]
    lags = pltpu.roll(lag[...].reshape(-1, cycle), cycle - reach, 1)
    lag[...] = lags.reshape(lag.shape)

    ids = lax.broadcasted_iota(jnp.int32, (cycle, cycle), 0) + lax.broadcasted_iota(
        jnp.int32, (cycle, cycle), 1
    )
    turn = jnp.where((ids == 0) | (ids == cycle), 1.0, 0.0).astype(jnp.bfloat16)
    flat = cycle_taps[...].reshape(basis * rows, cycle)
    flipped[...] = jnp.dot(flat, turn, preferred_element_type=jnp.float32).reshape(flipped.shape)
    for r in range(rows):
        polar = (lat_pos == 0) if r < half else (lat_pos == lat_count - 1)
        lag[HALO + r] = jnp.where(polar, flipped[:, r, :], lag[HALO + r])

    def halo_step(s, carry):
        circulants(lag[jnp.where(s < HALO, s, s + rows)], halo_mats.at[s], basis)
        return carry

    def own_step(r, carry):
        circulants(lag[HALO + r], mats, basis)
        cells = jnp.concatenate([fields[r], other[r]], axis=0)
        filt[r] = jnp.dot(mats[...], cells, preferred_element_type=jnp.float32)
        return carry

    lax.fori_loop(0, rows, own_step, 0)

    def band_step(n, carry):
        i = n // basis
        k = n % basis
        first = band_start[i]
        width = band_width[i]
        chunk = 32
        sums = [jnp.zeros((chunk, chans), jnp.float32) for _ in range(cols // chunk)]
        for t in range(band):
            r = first + t - base
            used = (t < width) & (r >= 0) & (r < rows)
            weight = jnp.where(used, lat_taps[i, k, t], 0.0)
            source = jnp.clip(r, 0, rows - 1)
            for c in range(cols // chunk):
                at = pl.multiple_of(k * cols + c * chunk, chunk)
                sums[c] = sums[c] + weight * filt[source, pl.ds(at, chunk), :]
        for c in range(cols // chunk):
            at = pl.multiple_of(i * cols + c * chunk, chunk)
            hidden[k, pl.ds(at, chunk), :] = sums[c].astype(jnp.bfloat16)
        return carry

    lax.fori_loop(0, rows * basis, band_step, 0)
    total = fields[...].reshape(rows * cols, chans).astype(jnp.float32)
    for k in range(basis):
        total = total + jnp.dot(hidden[k], mixing[k], preferred_element_type=jnp.float32)
    acc[...] = total.reshape(acc.shape)
    lax.fori_loop(0, 2 * HALO, halo_step, 0)


def halo_kernel(
    lat_taps, band_start, band_width, first_in, second_in, edges, halo_mats, acc, mixing,
    out, cells, filt, hidden,
):
    rows, cols, chans = out.shape
    basis = mixing.shape[0]
    reach = edges.shape[1] // 2
    band = lat_taps.shape[2]
    cycle = 2 * cols
    lat_pos = lax.axis_index("lat")
    lat_count = lax.axis_size("lat")
    core = lax.axis_index("lon")
    base = lat_pos * rows
    row_total = lat_count * rows

    is_first = core == 0
    zeros = jnp.zeros((cycle - cols - 2 * reach, chans), jnp.bfloat16)
    for s in range(2 * HALO):
        p = s % HALO
        mine, his = (first_in, second_in) if s < HALO else (second_in, first_in)
        a, b = (p + HALO, p) if s < HALO else (p, p + HALO)
        body = jnp.where(is_first, mine[p], his[p])
        edge = jnp.where(is_first, edges[a], edges[b])
        cells[s] = jnp.concatenate([body, edge[:reach], zeros, edge[reach:]], axis=0)

    def filter_step(s, carry):
        filt[s] = jnp.dot(halo_mats[s], cells[s], preferred_element_type=jnp.float32)
        return carry

    lax.fori_loop(0, 2 * HALO, filter_step, 0)

    chunk = 32

    def band_step(k, carry):
        for i in range(rows):
            slots = range(i, HALO) if i < HALO else range(HALO, i + 1)
            weights = []
            for s in slots:
                row = base - HALO + s + (0 if s < HALO else rows)
                t = row - band_start[i]
                used = (t >= 0) & (t < band_width[i]) & (row >= 0) & (row < row_total)
                weights.append(jnp.where(used, lat_taps[i, k, jnp.clip(t, 0, band - 1)], 0.0))
            for c in range(cols // chunk):
                at = pl.multiple_of(k * cols + c * chunk, chunk)
                total = None
                for s, weight in zip(slots, weights):
                    term = weight * filt[s, pl.ds(at, chunk), :]
                    total = term if total is None else total + term
                hidden[k, i * cols + c * chunk : i * cols + (c + 1) * chunk, :] = total.astype(
                    jnp.bfloat16
                )
        return carry

    lax.fori_loop(0, basis, band_step, 0)
    total = acc[...].reshape(rows * cols, chans)
    for k in range(basis):
        total = total + jnp.dot(hidden[k], mixing[k], preferred_element_type=jnp.float32)
    out[...] = total.reshape(out.shape).astype(out.dtype)


def shards(fields, lon_taps, lat_taps, cycle_taps, band_start, band_width, mixing):
    rows, cols, chans = fields.shape
    basis = lon_taps.shape[1]
    reach = (lon_taps.shape[2] - 1) // 2
    lat_count = lax.axis_size("lat")
    cycle = 2 * cols
    core = lax.axis_index("lon")
    axes = ("lat", "lon")
    other = lax.ppermute(fields, "lon", SWAP)
    head, tail = fields[:HALO], fields[rows - HALO :]
    first = lax.ppermute(jnp.where(core == 0, tail, head), axes, ring(lat_count, 1))
    second = lax.ppermute(jnp.where(core == 0, head, tail), axes, ring(lat_count, -1))

    weights = lat_taps.astype(jnp.float32)
    vmem = pl.BlockSpec(memory_space=pltpu.VMEM)
    smem = pl.BlockSpec(memory_space=pltpu.SMEM)
    f32, bf16 = jnp.float32, jnp.bfloat16
    acc, halo_mats = pl.pallas_call(
        own_kernel,
        out_shape=(
            jax.ShapeDtypeStruct((rows, cols, chans), f32),
            jax.ShapeDtypeStruct((2 * HALO, basis * cols, cycle), bf16),
        ),
        in_specs=[smem] * 3 + [vmem] * 5,
        out_specs=(vmem, vmem),
        scratch_shapes=[
            pltpu.VMEM((rows + 2 * HALO, basis, cycle), f32),
            pltpu.VMEM((basis, rows, cycle), f32),
            pltpu.VMEM((basis * cols, cycle), bf16),
            pltpu.VMEM((rows, basis * cols, chans), f32),
            pltpu.VMEM((basis, rows * cols, chans), bf16),
        ],
        compiler_params=pltpu.CompilerParams(vmem_limit_bytes=32 * 1024 * 1024),
        cost_estimate=pl.CostEstimate(
            flops=2_000_000_000, bytes_accessed=6_000_000, transcendentals=0
        ),
        name="own_rows",
    )(weights, band_start, band_width, fields, other, lon_taps, cycle_taps, mixing)

    arrived = jnp.concatenate([first, second], axis=0)
    edges = jnp.concatenate([arrived[:, :reach], arrived[:, cols - reach :]], axis=1)
    edges = lax.ppermute(edges, "lon", SWAP)
    return pl.pallas_call(
        halo_kernel,
        out_shape=jax.ShapeDtypeStruct((rows, cols, chans), bf16),
        in_specs=[smem] * 3 + [vmem] * 6,
        out_specs=vmem,
        scratch_shapes=[
            pltpu.VMEM((2 * HALO, cycle, chans), bf16),
            pltpu.VMEM((2 * HALO, basis * cols, chans), f32),
            pltpu.VMEM((basis, rows * cols, chans), bf16),
        ],
        compiler_params=pltpu.CompilerParams(vmem_limit_bytes=32 * 1024 * 1024),
        name="halo_rows",
    )(weights, band_start, band_width, first, second, edges, halo_mats, acc, mixing)


def solution(mesh):
    in_specs = (
        P(("ens", "lat"), "lon", None),
        P(),
        P("lat", None, None),
        P(),
        P("lat"),
        P("lat"),
        P(),
    )
    out_specs = P(("ens", "lat"), "lon", None)
    return jax.shard_map(shards, mesh=mesh, in_specs=in_specs, out_specs=out_specs, check_vma=False)
```

time: 102 us -> 23.5 us (0.23)
  the two profiles are of different devices: /device:TPU:0 before, /device:TPU:1 now
where the time goes in v1:
time: 23.5 us; the launch traced here: 23.3 us
  Pallas kernels  12.4 us (53%)
  starting transfers between devices  5.46 us (23%)
  waiting for transfers between devices  2.42 us (10%)
  local copies, waits for them, and re-layouts  1.7 us (7%)
  other arithmetic  1.18 us (5%)
    pallas_call x1, Pallas kernels, shards(): pl.pallas_call(own_kernel, out_shape=(jax.ShapeDtypeStruct((rows, cols, c...  7.42 us
    pallas_call x1, Pallas kernels, shards(): pl.pallas_call(halo_kernel, out_shape=jax.ShapeDtypeStruct((rows, cols, c...  4.99 us
    ppermute x1, starting transfers between devices, shards(): edges = lax.ppermute(edges, 'lon', SWAP)  2.36 us
    ppermute x1, starting transfers between devices, shards(): lax.ppermute(jnp.where(core == 0, head, tail), axes, ring(lat_count, -1))  2.11 us
    unnamed x13, local copies, waits for them, and re-layouts  1.67 us
    ppermute x1, waiting for transfers between devices, shards(): lax.ppermute(jnp.where(core == 0, head, tail), axes, ring(lat_count, -1))  1.25 us
    ppermute x1, waiting for transfers between devices, shards(): lax.ppermute(jnp.where(core == 0, tail, head), axes, ring(lat_count, 1))  1.16 us
    select_n x1, other arithmetic, shards(): jnp.where(core == 0, head, tail)  1.15 us
  transfers between devices with their start and end apart: 4, of which 2 were waited for; matrix products, arithmetic and copies ran while one was open for 7% of the time, Pallas kernels for 32%

profile of v1, /device:TPU:1, one launch (start us, length us, event | category | flops | bytes accessed | tf_op | source)
XLA Modules:
  0.0 23.3 jit_solution(9986106274908277131)
XLA Ops:
  0.0 0.0 copy-start
  0.0 0.0 copy-start.1
  0.0 0.0 copy-start.3
  0.0 0.0 copy-start.2
  0.0 0.0 copy-start.4
  0.0 1.2 %broadcast_select_fusion = (bf16[4,128,256]{2,1,0:T(8,128)(2,1)S(1)}, bf16[4,128,256]{2,1,0:T(8,128)(2,1)S(1)}) fusion(pred[]{:T(512)S(6)} %eq.4, bf16[8,128,256]{2,1,0:T(8,128)(2,1)} %fields.1), kind=kLoop, calls=%fused_computation | loop fusion | flops 262144 | bytes 1048577 | tf_op jit(solution)/shard_map/jit(_where)/select_n | solution.py:179
  1.2 0.1 collective-permute-start
  1.3 2.1 %collective-permute-start.1 = (bf16[4,128,256]{2,1,0:T(8,128)(2,1)S(1)}, bf16[4,128,256]{2,1,0:T(8,128)(2,1)S(1)}, u32[]{:S(2)}, u32[]{:S(2)}) collective-permute-start(bf16[4,128,256]{2,1,0:T(8,128)(2,1)S(1)} %get-tuple-element.11), channel_id=1, source_target_pairs={{0,4},{4,12},{8,0},{12,20},{16,8},{20,28},{24,16},{28,24},{1,5},{5... | collective-permute-start | bytes 786440 | tf_op jit(solution)/shard_map/ppermute | solution.py:179
  3.4 0.9 %collective-permute-start.3 = (bf16[8,128,256]{2,1,0:T(8,128)(2,1)}, bf16[8,128,256]{2,1,0:T(8,128)(2,1)S(1)}, u32[]{:S(2)}, u32[]{:S(2)}) collective-permute-start(bf16[8,128,256]{2,1,0:T(8,128)(2,1)} %fields.1), channel_id=1, source_target_pairs={{0,4},{4,0},{1,5},{5,1},{2,6},{6,2},{3,7},{7,3},{8,12},{12,8},{9,1... | collective-permute-start | bytes 1572872 | tf_op jit(solution)/shard_map/ppermute | solution.py:176
  4.3 0.8 %copy.8 = bf16[8,4,6]{2,1,0:T(4,128)(2,1)S(1)} copy(bf16[8,4,6]{0,1,2:T(4,128)(2,1)} %param.9) | data formatting | bytes 768 | tf_op args[2]
  5.1 0.8 %copy.9.lon_taps = f32[32,4,9]{2,1,0:T(4,128)S(1)} copy(f32[32,4,9]{0,1,2:T(4,128)} %param.8) | data formatting | bytes 9216 | tf_op args[1]
  5.9 1.2 %collective-permute-done.first_in = bf16[4,128,256]{2,1,0:T(8,128)(2,1)S(1)} collective-permute-done((bf16[4,128,256]{2,1,0:T(8,128)(2,1)S(1)}, bf16[4,128,256]{2,1,0:T(8,128)(2,1)S(1)}, u32[]{:S(2)}, u32[]{:S(2)}) %collective-permute-start) | collective-permute-done | bytes 262176 | tf_op jit(solution)/shard_map/ppermute | solution.py:178
  7.1 1.3 %collective-permute-done.1.second_in = bf16[4,128,256]{2,1,0:T(8,128)(2,1)S(1)} collective-permute-done((bf16[4,128,256]{2,1,0:T(8,128)(2,1)S(1)}, bf16[4,128,256]{2,1,0:T(8,128)(2,1)S(1)}, u32[]{:S(2)}, u32[]{:S(2)}) %collective-permute-start.1) | collective-permute-done | bytes 262176 | tf_op jit(solution)/shard_map/ppermute | solution.py:179
  8.4 2.4 %collective-permute-start.2 = (bf16[8,8,256]{2,1,0:T(8,128)(2,1)S(1)}, bf16[8,8,256]{2,1,0:T(8,128)(2,1)S(1)}, u32[]{:S(2)}, u32[]{:S(2)}) collective-permute-start(bf16[8,8,256]{2,1,0:T(8,128)(2,1)S(1)} %pad_maximum_fusion), channel_id=1, source_target_pairs={{0,4},{4,0},{1,5},{5,1},{2,6},{6,2},{3,7},{7,3},{8,12},{12,8},{9,1... | collective-permute-start | bytes 98312 | tf_op jit(solution)/shard_map/ppermute | solution.py:209
  10.8 0.0 collective-permute-done.3.other
  10.8 0.0 copy-done
  10.8 0.0 copy-done.1
  10.8 0.0 copy-done.3
  10.8 0.0 copy-done.2
  10.8 0.0 copy-done.4
  10.8 7.4 %own_rows.1 = (f32[8,128,256]{2,1,0:T(8,128)S(1)}, bf16[8,512,256]{2,1,0:T(8,128)(2,1)S(1)}) custom-call(f32[8,4,6]{2,1,0:T(4,128)S(1)} %convert_element_type.3.lat_taps, s32[8]{0:T(128)S(1)} %copy-done.2, s32[8]{0:T(128)S(1)} %copy-done.3, bf16[8,128,256]{2,1,0:T(8,128)(2,1)S(1)} %copy-done, bf16[8,128,256]{2,1,0:T(8,128)(2,1)S(1)} %collective-permute-done.3.other, ...), custom_call_target="tpu_custom_call" | custom-call | flops 2000000000 | bytes 6000000 | tf_op jit(solution)/shard_map/own_rows/pallas_call | solution.py:185
  18.3 0.0 collective-permute-done.2.edges
  18.3 5.0 %halo_rows.1 = bf16[8,128,256]{2,1,0:T(8,128)(2,1)} custom-call(f32[8,4,6]{2,1,0:T(4,128)S(1)} %convert_element_type.3.lat_taps, s32[8]{0:T(128)S(1)} %copy-done.2, s32[8]{0:T(128)S(1)} %copy-done.3, bf16[4,128,256]{2,1,0:T(8,128)(2,1)S(1)} %collective-permute-done.first_in, bf16[4,128,256]{2,1,0:T(8,128)(2,1)S(1)} %collective-permute-done.1.second_in, ...), custom_call_target="tpu_custom_call" | custom-call | tf_op jit(solution)/shard_map/halo_rows/pallas_call | solution.py:210
  (5 shorter events, 0.1 us)
Async XLA Ops:
  0.0 10.8 %copy-start = (bf16[8,128,256]{2,1,0:T(8,128)(2,1)S(1)}, bf16[8,128,256]{2,1,0:T(8,128)(2,1)}, u32[]{:S(2)}) copy-start(bf16[8,128,256]{2,1,0:T(8,128)(2,1)} %fields.1) | copy-start | bytes 1572868
  0.0 10.8 %copy-start.1 = (bf16[4,256,256]{2,1,0:T(8,128)(2,1)S(1)}, bf16[4,256,256]{2,1,0:T(8,128)(2,1)}, u32[]{:S(2)}) copy-start(bf16[4,256,256]{2,1,0:T(8,128)(2,1)} %mixing.3) | copy-start | bytes 1572868
  0.0 10.8 %copy-start.3 = (s32[8]{0:T(128)S(1)}, s32[8]{0:T(128)}, u32[]{:S(2)}) copy-start(s32[8]{0:T(128)} %band_width.3) | copy-start | bytes 100
  0.0 10.8 %copy-start.2 = (s32[8]{0:T(128)S(1)}, s32[8]{0:T(128)}, u32[]{:S(2)}) copy-start(s32[8]{0:T(128)} %band_start.3) | copy-start | bytes 100
  0.0 10.8 %copy-start.4 = (bf16[4,8,256]{2,1,0:T(8,128)(2,1)S(1)}, bf16[4,8,256]{2,1,0:T(8,128)(2,1)}, u32[]{:S(2)}) copy-start(bf16[4,8,256]{2,1,0:T(8,128)(2,1)} %cycle_taps.1) | copy-start | bytes 49156
  1.2 5.9 %collective-permute-start = (bf16[4,128,256]{2,1,0:T(8,128)(2,1)S(1)}, bf16[4,128,256]{2,1,0:T(8,128)(2,1)S(1)}, u32[]{:S(2)}, u32[]{:S(2)}) collective-permute-start(bf16[4,128,256]{2,1,0:T(8,128)(2,1)S(1)} %get-tuple-element.12), channel_id=1, source_target_pairs={{0,8},{4,0},{8,16},{12,4},{16,24},{20,12},{24,28},{28,20},{1,9},{5... | collective-permute-start | bytes 786440 | tf_op jit(solution)/shard_map/ppermute | solution.py:178
  1.3 7.1 %collective-permute-start.1 = (bf16[4,128,256]{2,1,0:T(8,128)(2,1)S(1)}, bf16[4,128,256]{2,1,0:T(8,128)(2,1)S(1)}, u32[]{:S(2)}, u32[]{:S(2)}) collective-permute-start(bf16[4,128,256]{2,1,0:T(8,128)(2,1)S(1)} %get-tuple-element.11), channel_id=1, source_target_pairs={{0,4},{4,12},{8,0},{12,20},{16,8},{20,28},{24,16},{28,24},{1,5},{5... | collective-permute-start | bytes 786440 | tf_op jit(solution)/shard_map/ppermute | solution.py:179
  3.4 7.4 %collective-permute-start.3 = (bf16[8,128,256]{2,1,0:T(8,128)(2,1)}, bf16[8,128,256]{2,1,0:T(8,128)(2,1)S(1)}, u32[]{:S(2)}, u32[]{:S(2)}) collective-permute-start(bf16[8,128,256]{2,1,0:T(8,128)(2,1)} %fields.1), channel_id=1, source_target_pairs={{0,4},{4,0},{1,5},{5,1},{2,6},{6,2},{3,7},{7,3},{8,12},{12,8},{9,1... | collective-permute-start | bytes 1572872 | tf_op jit(solution)/shard_map/ppermute | solution.py:176
  8.4 9.8 %collective-permute-start.2 = (bf16[8,8,256]{2,1,0:T(8,128)(2,1)S(1)}, bf16[8,8,256]{2,1,0:T(8,128)(2,1)S(1)}, u32[]{:S(2)}, u32[]{:S(2)}) collective-permute-start(bf16[8,8,256]{2,1,0:T(8,128)(2,1)S(1)} %pad_maximum_fusion), channel_id=1, source_target_pairs={{0,4},{4,0},{1,5},{5,1},{2,6},{6,2},{3,7},{7,3},{8,12},{12,8},{9,1... | collective-permute-start | bytes 98312 | tf_op jit(solution)/shard_map/ppermute | solution.py:209

commit v2 on v1

--- a/solution.py
+++ b/solution.py
@@ -204,6 +204,7 @@
         name="own_rows",
     )(weights, band_start, band_width, fields, other, lon_taps, cycle_taps, mixing)
 
+    first, second, acc = lax.optimization_barrier((first, second, acc))
     arrived = jnp.concatenate([first, second], axis=0)
     edges = jnp.concatenate([arrived[:, :reach], arrived[:, cols - reach :]], axis=1)
     edges = lax.ppermute(edges, "lon", SWAP)

time: 23.5 us -> 24.1 us (1.026)
  the two profiles are of different devices: /device:TPU:1 before, /device:TPU:0 now
where the time goes in v2:
time: 24.1 us; the launch traced here: 23.7 us
  Pallas kernels  12.4 us (51%)
  local copies, waits for them, and re-layouts  5.79 us (24%)
  starting transfers between devices  3.35 us (14%)
  other arithmetic  1.1 us (5%)
  waiting for transfers between devices  1.01 us (4%)
    pallas_call x1, Pallas kernels, shards(): pl.pallas_call(own_kernel, out_shape=(jax.ShapeDtypeStruct((rows, cols, c...  7.42 us
    unnamed x13, local copies, waits for them, and re-layouts  5.75 us
    pallas_call x1, Pallas kernels, shards(): pl.pallas_call(halo_kernel, out_shape=jax.ShapeDtypeStruct((rows, cols, c...  4.98 us
    ppermute x1, starting transfers between devices, shards(): lax.ppermute(jnp.where(core == 0, tail, head), axes, ring(lat_count, 1))  2.55 us
    select_n x1, other arithmetic, shards(): jnp.where(core == 0, head, tail)  1.07 us
    ppermute x1, waiting for transfers between devices, shards(): edges = lax.ppermute(edges, 'lon', SWAP)  1 us
  transfers between devices with their start and end apart: 4, of which 1 were waited for; matrix products, arithmetic and copies ran while one was open for 11% of the time, Pallas kernels for 31%

profile of v2, /device:TPU:0, one launch (start us, length us, event | category | flops | bytes accessed | tf_op | source)
XLA Modules:
  0.0 23.7 jit_solution(4066452969641519133)
XLA Ops:
  0.0 0.5 %collective-permute-start.2 = (bf16[8,128,256]{2,1,0:T(8,128)(2,1)}, bf16[8,128,256]{2,1,0:T(8,128)(2,1)S(1)}, u32[]{:S(2)}, u32[]{:S(2)}) collective-permute-start(bf16[8,128,256]{2,1,0:T(8,128)(2,1)} %fields.1), channel_id=1, source_target_pairs={{0,4},{4,0},{1,5},{5,1},{2,6},{6,2},{3,7},{7,3},{8,12},{12,8},{9,1... | collective-permute-start | bytes 1572872 | tf_op jit(solution)/shard_map/ppermute | solution.py:176
  0.5 1.1 %broadcast_select_fusion = (bf16[4,128,256]{2,1,0:T(8,128)(2,1)S(1)}, bf16[4,128,256]{2,1,0:T(8,128)(2,1)S(1)}) fusion(pred[]{:T(512)S(6)} %eq.4, bf16[8,128,256]{2,1,0:T(8,128)(2,1)} %fields.1), kind=kLoop, calls=%fused_computation | loop fusion | flops 262144 | bytes 1048577 | tf_op jit(solution)/shard_map/jit(_where)/select_n | solution.py:179
  1.5 0.1 collective-permute-start.1
  1.6 2.5 %collective-permute-start = (bf16[4,128,256]{2,1,0:T(8,128)(2,1)S(1)}, bf16[4,128,256]{2,1,0:T(8,128)(2,1)S(1)}, u32[]{:S(2)}, u32[]{:S(2)}) collective-permute-start(bf16[4,128,256]{2,1,0:T(8,128)(2,1)S(1)} %get-tuple-element.18), channel_id=1, source_target_pairs={{0,8},{4,0},{8,16},{12,4},{16,24},{20,12},{24,28},{28,20},{1,9},{5... | collective-permute-start | bytes 786440 | tf_op jit(solution)/shard_map/ppermute | solution.py:178
  4.1 0.8 %copy.8 = bf16[8,4,6]{2,1,0:T(4,128)(2,1)S(1)} copy(bf16[8,4,6]{0,1,2:T(4,128)(2,1)} %param.9) | data formatting | bytes 768 | tf_op args[2]
  5.0 0.8 %copy.9.lon_taps = f32[32,4,9]{2,1,0:T(4,128)S(1)} copy(f32[32,4,9]{0,1,2:T(4,128)} %param.8) | data formatting | bytes 9216 | tf_op args[1]
  5.8 0.0 collective-permute-done.2.other
  5.8 0.0 copy-start
  5.8 1.0 %copy-done = bf16[8,128,256]{2,1,0:T(8,128)(2,1)S(1)} copy-done((bf16[8,128,256]{2,1,0:T(8,128)(2,1)S(1)}, bf16[8,128,256]{2,1,0:T(8,128)(2,1)}, u32[]{:S(2)}) %copy-start) | copy-done | bytes 524312
  6.8 0.0 copy-start.1
  6.8 1.0 %copy-done.1 = bf16[4,256,256]{2,1,0:T(8,128)(2,1)S(1)} copy-done((bf16[4,256,256]{2,1,0:T(8,128)(2,1)S(1)}, bf16[4,256,256]{2,1,0:T(8,128)(2,1)}, u32[]{:S(2)}) %copy-start.1) | copy-done | bytes 524312
  7.9 0.0 copy-start.2
  7.9 0.7 %copy-done.2 = s32[8]{0:T(128)S(1)} copy-done((s32[8]{0:T(128)S(1)}, s32[8]{0:T(128)}, u32[]{:S(2)}) %copy-start.2) | copy-done | bytes 56
  8.5 0.0 copy-start.3
  8.5 0.7 %copy-done.3 = s32[8]{0:T(128)S(1)} copy-done((s32[8]{0:T(128)S(1)}, s32[8]{0:T(128)}, u32[]{:S(2)}) %copy-start.3) | copy-done | bytes 56
  9.2 0.0 copy-start.4
  9.2 0.7 %copy-done.4 = bf16[4,8,256]{2,1,0:T(8,128)(2,1)S(1)} copy-done((bf16[4,8,256]{2,1,0:T(8,128)(2,1)S(1)}, bf16[4,8,256]{2,1,0:T(8,128)(2,1)}, u32[]{:S(2)}) %copy-start.4) | copy-done | bytes 16408
  9.9 7.4 %own_rows.1 = (f32[8,128,256]{2,1,0:T(8,128)S(1)}, bf16[8,512,256]{2,1,0:T(8,128)(2,1)S(1)}) custom-call(f32[8,4,6]{2,1,0:T(4,128)S(1)} %convert_element_type.3.lat_taps, s32[8]{0:T(128)S(1)} %copy-done.2, s32[8]{0:T(128)S(1)} %copy-done.3, bf16[8,128,256]{2,1,0:T(8,128)(2,1)S(1)} %copy-done, bf16[8,128,256]{2,1,0:T(8,128)(2,1)S(1)} %collective-permute-done.2.other, ...), custom_call_target="tpu_custom_call" | custom-call | flops 2000000000 | bytes 6000000 | tf_op jit(solution)/shard_map/own_rows/pallas_call | solution.py:185
  17.3 0.0 collective-permute-done.1.second_in
  17.3 0.0 collective-permute-done.first_in
  17.5 0.3 %collective-permute-start.3 = (bf16[8,8,256]{2,1,0:T(8,128)(2,1)S(1)}, bf16[8,8,256]{2,1,0:T(8,128)(2,1)S(1)}, u32[]{:S(2)}, u32[]{:S(2)}) collective-permute-start(bf16[8,8,256]{2,1,0:T(8,128)(2,1)S(1)} %pad_maximum_fusion), channel_id=1, source_target_pairs={{0,4},{4,0},{1,5},{5,1},{2,6},{6,2},{3,7},{7,3},{8,12},{12,8},{9,1... | collective-permute-start | bytes 98312 | tf_op jit(solution)/shard_map/ppermute | solution.py:210
  17.7 1.0 %collective-permute-done.3.edges = bf16[8,8,256]{2,1,0:T(8,128)(2,1)S(1)} collective-permute-done((bf16[8,8,256]{2,1,0:T(8,128)(2,1)S(1)}, bf16[8,8,256]{2,1,0:T(8,128)(2,1)S(1)}, u32[]{:S(2)}, u32[]{:S(2)}) %collective-permute-start.3) | collective-permute-done | bytes 32800 | tf_op jit(solution)/shard_map/ppermute | solution.py:210
  18.7 5.0 %halo_rows.1 = bf16[8,128,256]{2,1,0:T(8,128)(2,1)} custom-call(f32[8,4,6]{2,1,0:T(4,128)S(1)} %convert_element_type.3.lat_taps, s32[8]{0:T(128)S(1)} %copy-done.2, s32[8]{0:T(128)S(1)} %copy-done.3, bf16[4,128,256]{2,1,0:T(8,128)(2,1)S(1)} %collective-permute-done.first_in, bf16[4,128,256]{2,1,0:T(8,128)(2,1)S(1)} %collective-permute-done.1.second_in, ...), custom_call_target="tpu_custom_call" | custom-call | tf_op jit(solution)/shard_map/halo_rows/pallas_call | solution.py:211
  (5 shorter events, 0.1 us)
Async XLA Ops:
  0.0 5.8 %collective-permute-start.2 = (bf16[8,128,256]{2,1,0:T(8,128)(2,1)}, bf16[8,128,256]{2,1,0:T(8,128)(2,1)S(1)}, u32[]{:S(2)}, u32[]{:S(2)}) collective-permute-start(bf16[8,128,256]{2,1,0:T(8,128)(2,1)} %fields.1), channel_id=1, source_target_pairs={{0,4},{4,0},{1,5},{5,1},{2,6},{6,2},{3,7},{7,3},{8,12},{12,8},{9,1... | collective-permute-start | bytes 1572872 | tf_op jit(solution)/shard_map/ppermute | solution.py:176
  1.5 15.8 %collective-permute-start.1 = (bf16[4,128,256]{2,1,0:T(8,128)(2,1)S(1)}, bf16[4,128,256]{2,1,0:T(8,128)(2,1)S(1)}, u32[]{:S(2)}, u32[]{:S(2)}) collective-permute-start(bf16[4,128,256]{2,1,0:T(8,128)(2,1)S(1)} %get-tuple-element.17), channel_id=1, source_target_pairs={{0,4},{4,12},{8,0},{12,20},{16,8},{20,28},{24,16},{28,24},{1,5},{5... | collective-permute-start | bytes 786440 | tf_op jit(solution)/shard_map/ppermute | solution.py:179
  1.6 15.7 %collective-permute-start = (bf16[4,128,256]{2,1,0:T(8,128)(2,1)S(1)}, bf16[4,128,256]{2,1,0:T(8,128)(2,1)S(1)}, u32[]{:S(2)}, u32[]{:S(2)}) collective-permute-start(bf16[4,128,256]{2,1,0:T(8,128)(2,1)S(1)} %get-tuple-element.18), channel_id=1, source_target_pairs={{0,8},{4,0},{8,16},{12,4},{16,24},{20,12},{24,28},{28,20},{1,9},{5... | collective-permute-start | bytes 786440 | tf_op jit(solution)/shard_map/ppermute | solution.py:178
  5.8 1.0 %copy-start = (bf16[8,128,256]{2,1,0:T(8,128)(2,1)S(1)}, bf16[8,128,256]{2,1,0:T(8,128)(2,1)}, u32[]{:S(2)}) copy-start(bf16[8,128,256]{2,1,0:T(8,128)(2,1)} %fields.1) | copy-start | bytes 1572868
  6.8 1.0 %copy-start.1 = (bf16[4,256,256]{2,1,0:T(8,128)(2,1)S(1)}, bf16[4,256,256]{2,1,0:T(8,128)(2,1)}, u32[]{:S(2)}) copy-start(bf16[4,256,256]{2,1,0:T(8,128)(2,1)} %mixing.3) | copy-start | bytes 1572868
  7.9 0.7 %copy-start.2 = (s32[8]{0:T(128)S(1)}, s32[8]{0:T(128)}, u32[]{:S(2)}) copy-start(s32[8]{0:T(128)} %band_start.3) | copy-start | bytes 100
  8.5 0.7 %copy-start.3 = (s32[8]{0:T(128)S(1)}, s32[8]{0:T(128)}, u32[]{:S(2)}) copy-start(s32[8]{0:T(128)} %band_width.3) | copy-start | bytes 100
  9.2 0.7 %copy-start.4 = (bf16[4,8,256]{2,1,0:T(8,128)(2,1)S(1)}, bf16[4,8,256]{2,1,0:T(8,128)(2,1)}, u32[]{:S(2)}) copy-start(bf16[4,8,256]{2,1,0:T(8,128)(2,1)} %cycle_taps.1) | copy-start | bytes 49156
  17.5 1.3 %collective-permute-start.3 = (bf16[8,8,256]{2,1,0:T(8,128)(2,1)S(1)}, bf16[8,8,256]{2,1,0:T(8,128)(2,1)S(1)}, u32[]{:S(2)}, u32[]{:S(2)}) collective-permute-start(bf16[8,8,256]{2,1,0:T(8,128)(2,1)S(1)} %pad_maximum_fusion), channel_id=1, source_target_pairs={{0,4},{4,0},{1,5},{5,1},{2,6},{6,2},{3,7},{7,3},{8,12},{12,8},{9,1... | collective-permute-start | bytes 98312 | tf_op jit(solution)/shard_map/ppermute | solution.py:210

commit v3 on v2

v3 whole, which is shorter than its diff:
```python
import jax
import jax.numpy as jnp
from jax import lax
from jax.experimental import pallas as pl
from jax.experimental.pallas import tpu as pltpu
from jax.sharding import PartitionSpec as P

HALO = 4
BLOCK = 16
SPAN = 32
SWAP = [(0, 1), (1, 0)]
F32, BF16 = jnp.float32, jnp.bfloat16


def ring(lat_count, step):
    pairs = []
    for lat in range(lat_count):
        for core in range(2):
            to = lat + (step if core == 0 else -step)
            if 0 <= to < lat_count:
                pairs.append((lat * 2 + core, to * 2 + core))
            else:
                pairs.append((lat * 2 + core, lat * 2 + 1 - core))
    return pairs


def matmul(a, b):
    return jnp.dot(a, b, preferred_element_type=F32)


def staircase(line, steps):
    wide = jnp.broadcast_to(line, (steps, line.shape[1]))
    return pltpu.roll(wide, 0, 1, stride=1, stride_axis=0).astype(BF16)


def chosen(terms):
    total = None
    for mask, value in terms:
        term = jnp.where(mask, value, 0.0)
        total = term if total is None else total + term
    return total


def window_products(weights, ext, hidden, blocks, rows, basis, cols, chans):
    for b in blocks:
        cells = ext[:, BLOCK * b : BLOCK * b + SPAN, :].reshape(-1, chans)
        part = matmul(weights[...], cells).astype(BF16)
        for k in range(basis):
            for i in range(rows):
                at = (k * rows + i) * BLOCK
                hidden[
                    i * cols + BLOCK * b : i * cols + BLOCK * (b + 1),
                    k * chans : (k + 1) * chans,
                ] = part[at : at + BLOCK]


def own_kernel(
    start_in, width_in, lon_in, lat_in, fields_in, cycle_in, mixing_in, other,
    acc, halo_weights, mix,
    start, width, lon, lat, fields, cycle_taps, lon_wide, lat_wide, own_weights, ext, hidden,
    turned, cycle_rows, mixed_rows, sems,
):
    rows, cols, chans = fields.shape
    taps, basis, row_total = lon.shape
    band = lat.shape[0]
    reach = taps // 2
    polar = cycle_taps.shape[1] // 2
    cycle = cycle_taps.shape[2]
    lat_pos = lax.axis_index("lat")
    base = lat_pos * rows
    at_top = base == 0
    at_bottom = base == row_total - rows

    copies = []
    for n, (source, target) in enumerate(
        [
            (lon_in, lon), (lat_in, lat), (start_in, start), (width_in, width),
            (fields_in, fields), (cycle_in, cycle_taps), (mixing_in, mix),
        ]
    ):
        copies.append(pltpu.make_async_copy(source, target, sems.at[n]))
        copies[-1].start()
    lon_wide[...] = jnp.zeros_like(lon_wide)
    lat_wide[...] = jnp.zeros_like(lat_wide)
    for n in range(4):
        copies[n].wait()

    for d in range(taps):
        for k in range(basis):
            lon_wide[k * 16 + d : k * 16 + d + 1, 0:row_total] = lon[d, k : k + 1, :]
    lanes = lon_wide.shape[1]
    slots = pltpu.roll(lon_wide[...], lax.rem(lanes + HALO - base, lanes), 1)[:, :128]
    slots = jnp.transpose(slots)[: rows + 2 * HALO]
    is_tap = lax.broadcasted_iota(jnp.int32, slots.shape, 1) < taps
    own_taps, halo_taps = [], []
    for k in range(basis):
        moved = slots if k == 0 else pltpu.roll(slots, 128 - 16 * k, 1)
        moved = jnp.where(is_tap, moved, 0.0)
        for _ in range(2):
            moved = pltpu.roll(moved, 0, 1, stride=SPAN // 2, stride_axis=0)
        quads = [jnp.sum(moved[4 * q : 4 * q + 4], axis=0, keepdims=True) for q in range(4)]
        own_taps.append(jnp.concatenate([quads[1], quads[2]], axis=1))
        halo_taps.append(jnp.concatenate([quads[0], quads[3]], axis=1))

    for t in range(band):
        lat_wide[t * basis : (t + 1) * basis, 0:rows] = lat[t].astype(F32)
    lat_cols = jnp.transpose(lat_wide[...])[:rows]
    shape = (rows, rows * SPAN)
    lane = lax.broadcasted_iota(jnp.int32, shape, 1)
    out_row = lax.broadcasted_iota(jnp.int32, shape, 0)
    first = jnp.zeros(shape, jnp.int32)
    count = jnp.zeros(shape, jnp.int32)
    for i in range(rows):
        first = jnp.where(out_row == i, start[i], first)
        count = jnp.where(out_row == i, width[i], count)
    spread = [
        [
            jnp.broadcast_to(lat_cols[:, t * basis + k : t * basis + k + 1], shape)
            for k in range(basis)
        ]
        for t in range(band)
    ]
    slot = lane // SPAN
    own_row = base + slot
    halo_row = jnp.where(slot < HALO, own_row - HALO, own_row + rows - HALO)
    is_polar = (own_row < polar) | (own_row >= row_total - polar)
    in_grid = (halo_row >= 0) & (halo_row < row_total)
    own_step, halo_step = own_row - first, halo_row - first
    own_used = [(own_step == t) & (count > t) & ~is_polar for t in range(band)]
    halo_used = [(halo_step == t) & (count > t) & in_grid for t in range(band)]
    for k in range(basis):
        own_line = own_taps[k] * chosen([(own_used[t], spread[t][k]) for t in range(band)])
        halo_line = halo_taps[k] * chosen([(halo_used[t], spread[t][k]) for t in range(band)])
        for i in range(rows):
            at = (k * rows + i) * BLOCK
            own_weights[at : at + BLOCK, :] = staircase(own_line[i : i + 1], BLOCK)
            halo_weights[at : at + BLOCK, :] = staircase(halo_line[i : i + 1], BLOCK)

    copies[4].wait()
    pad = jnp.zeros((ext.shape[1] - cols - 2 * reach, chans), BF16)
    for r in range(rows):
        ext[r] = jnp.concatenate(
            [other[r, cols - reach :], fields[r], other[r, :reach], pad], axis=0
        )
    window_products(
        own_weights, ext, hidden, range(cols // BLOCK), rows, basis, cols, chans
    )
    copies[5].wait()
    copies[6].wait()
    half = rows // 2
    for n in range(2):
        total = matmul(hidden[n * half * cols : (n + 1) * half * cols], mix[...])
        acc[n * half : (n + 1) * half] = (
            total.reshape(half, cols, chans)
            + fields[n * half : (n + 1) * half].astype(F32)
        )

    @pl.when(at_top | at_bottom)
    def polar_part():
        offset = jnp.where(at_top, 0, rows - polar)
        total = lax.broadcasted_iota(jnp.int32, (cycle, cycle), 0) + lax.broadcasted_iota(
            jnp.int32, (cycle, cycle), 1
        )
        turn = jnp.where((total == 0) | (total == cycle), 1.0, 0.0).astype(BF16)
        negated = matmul(cycle_taps[...].reshape(-1, cycle), turn)
        for p in range(polar):
            for k in range(basis):
                n = k * 2 * polar + p
                line = jnp.where(at_top, negated[n : n + 1], negated[n + polar : n + polar + 1])
                turned[p, k * cols : (k + 1) * cols, :] = staircase(line, cols)
        for p in range(polar):
            whole = jnp.concatenate([fields[offset + p], other[offset + p]], axis=0)
            part = matmul(turned[p], whole).astype(BF16)
            for k in range(basis):
                cycle_rows[k, p * cols : (p + 1) * cols, :] = part[k * cols : (k + 1) * cols]
        for k in range(basis):
            part = matmul(cycle_rows[k], mix[k * chans : (k + 1) * chans, :]).astype(BF16)
            mixed_rows[k * polar : (k + 1) * polar] = part.reshape(polar, cols, chans)
        of_basis = lane // (polar * BLOCK)
        step = base + offset + lax.rem(lane // BLOCK, polar) - first
        at_start = lax.rem(lane, BLOCK) == 0
        terms = []
        for t in range(band):
            value = spread[t][0]
            for k in range(1, basis):
                value = jnp.where(of_basis == k, spread[t][k], value)
            terms.append(((step == t) & (count > t) & at_start, value))
        line = chosen(terms)
        weights = jnp.concatenate(
            [staircase(line[i : i + 1], BLOCK) for i in range(rows)], axis=0
        )
        for b in range(cols // BLOCK):
            at = slice(BLOCK * b, BLOCK * (b + 1))
            cells = mixed_rows[:, at, :].reshape(-1, chans)
            acc[:, at, :] = acc[:, at, :] + matmul(weights, cells).reshape(rows, BLOCK, chans)


def halo_kernel(first_in, second_in, edges, weights, acc, mix, out, ext, hidden):
    rows, cols, chans = out.shape
    basis = mix.shape[0] // chans
    reach = edges.shape[1] // 2
    is_first = lax.axis_index("lon") == 0
    pad = jnp.zeros((ext.shape[1] - cols - 2 * reach, chans), BF16)
    for s in range(2 * HALO):
        p = s % HALO
        mine, his = (first_in, second_in) if s < HALO else (second_in, first_in)
        a, b = (p + HALO, p) if s < HALO else (p, p + HALO)
        body = jnp.where(is_first, mine[p], his[p])
        edge = jnp.where(is_first, edges[a], edges[b])
        ext[s] = jnp.concatenate([edge[reach:], body, edge[:reach], pad], axis=0)
    window_products(weights, ext, hidden, range(cols // BLOCK), rows, basis, cols, chans)
    half = rows // 2
    for n in range(2):
        total = matmul(hidden[n * half * cols : (n + 1) * half * cols], mix[...])
        at = slice(n * half, (n + 1) * half)
        out[at] = (total.reshape(half, cols, chans) + acc[at]).astype(BF16)


def shards(fields, lon_taps, lat_taps, cycle_taps, band_start, band_width, mixing):
    rows, cols, chans = fields.shape
    row_total, basis, taps = lon_taps.shape
    band = lat_taps.shape[2]
    reach = (taps - 1) // 2
    polar = cycle_taps.shape[1] // 2
    cycle = cycle_taps.shape[2]
    lat_count = lax.axis_size("lat")
    core = lax.axis_index("lon")
    axes = ("lat", "lon")
    assert cycle == 2 * cols and rows == 2 * HALO and basis * polar * BLOCK == rows * SPAN
    other = lax.ppermute(fields, "lon", SWAP)
    head, tail = fields[:HALO], fields[rows - HALO :]
    first = lax.ppermute(jnp.where(core == 0, tail, head), axes, ring(lat_count, 1))
    second = lax.ppermute(jnp.where(core == 0, head, tail), axes, ring(lat_count, -1))

    vmem = pl.BlockSpec(memory_space=pltpu.VMEM)
    hbm = pl.BlockSpec(memory_space=pltpu.HBM)
    sds = jax.ShapeDtypeStruct
    group = basis * rows * BLOCK
    ext_cols = cols + SPAN - BLOCK
    acc, halo_weights, mix = pl.pallas_call(
        own_kernel,
        out_shape=(
            sds((rows, cols, chans), F32),
            sds((group, rows * SPAN), BF16),
            sds((basis * chans, chans), BF16),
        ),
        in_specs=[hbm] * 7 + [vmem],
        out_specs=(vmem, vmem, vmem),
        scratch_shapes=[
            pltpu.SMEM((rows,), jnp.int32),
            pltpu.SMEM((rows,), jnp.int32),
            pltpu.VMEM((taps, basis, row_total), F32),
            pltpu.VMEM((band, basis, rows), BF16),
            pltpu.VMEM((rows, cols, chans), BF16),
            pltpu.VMEM((basis, 2 * polar, cycle), BF16),
            pltpu.VMEM((128, -(-row_total // 128) * 128), F32),
            pltpu.VMEM((128, 128), F32),
            pltpu.VMEM((group, rows * SPAN), BF16),
            pltpu.VMEM((rows, ext_cols, chans), BF16),
            pltpu.VMEM((rows * cols, basis * chans), BF16),
            pltpu.VMEM((polar, basis * cols, cycle), BF16),
            pltpu.VMEM((basis, polar * cols, chans), BF16),
            pltpu.VMEM((basis * polar, cols, chans), BF16),
            pltpu.SemaphoreType.DMA((7,)),
        ],
        compiler_params=pltpu.CompilerParams(vmem_limit_bytes=32 * 1024 * 1024),
        cost_estimate=pl.CostEstimate(
            flops=2_000_000_000, bytes_accessed=6_000_000, transcendentals=0
        ),
        name="own_rows",
    )(
        band_start, band_width, jnp.transpose(lon_taps, (2, 1, 0)),
        jnp.transpose(lat_taps, (2, 1, 0)), fields, cycle_taps,
        mixing.reshape(basis * chans, chans), other,
    )

    first, second, acc = lax.optimization_barrier((first, second, acc))
    edges = jnp.concatenate(
        [
            jnp.concatenate([got[:, :reach], got[:, cols - reach :]], axis=1)
            for got in (first, second)
        ],
        axis=0,
    )
    edges = lax.ppermute(edges, "lon", SWAP)
    return pl.pallas_call(
        halo_kernel,
        out_shape=sds((rows, cols, chans), BF16),
        in_specs=[vmem] * 6,
        out_specs=vmem,
        scratch_shapes=[
            pltpu.VMEM((rows, ext_cols, chans), BF16),
            pltpu.VMEM((rows * cols, basis * chans), BF16),
        ],
        compiler_params=pltpu.CompilerParams(vmem_limit_bytes=32 * 1024 * 1024),
        name="halo_rows",
    )(first, second, edges, halo_weights, acc, mix)


def solution(mesh):
    in_specs = (
        P(("ens", "lat"), "lon", None),
        P(),
        P("lat", None, None),
        P(),
        P("lat"),
        P("lat"),
        P(),
    )
    out_specs = P(("ens", "lat"), "lon", None)
    return jax.shard_map(shards, mesh=mesh, in_specs=in_specs, out_specs=out_specs, check_vma=False)
```

time: 24.1 us -> 14.5 us (0.60)
  Pallas kernels: 12.4 us -> 5.93 us
  local copies, waits for them, and re-layouts: 5.79 us -> 2.11 us
  starting transfers between devices: 3.35 us -> 3.89 us
    pallas_call x2, Pallas kernels: 12.4 us -> 5.93 us  [the longest x1 3.86 us: shards(): pl.pallas_call(own_kernel, out_shape=(sds((rows, cols, chans), F32), sds(...]
    unnamed x13 -> x14, local copies, waits for them, and re-layouts: 5.75 us -> 2.1 us
    ppermute x1, starting transfers between devices: 0.27 us -> 0.81 us  [shards(): edges = lax.ppermute(edges, 'lon', SWAP)]
  transfers between devices with their start and end apart: 4 -> 4, of which waited for: 1 -> 2; matrix products, arithmetic and copies ran while one was open for 11% -> 8% of each run, Pallas kernels for 31% -> 27%
where the time goes in v3:
time: 14.5 us; the launch traced here: 14.3 us
  Pallas kernels  5.93 us (41%)
  starting transfers between devices  3.89 us (27%)
  local copies, waits for them, and re-layouts  2.11 us (15%)
  other arithmetic  1.18 us (8%)
  waiting for transfers between devices  1.07 us (7%)
    pallas_call x1, Pallas kernels, shards(): pl.pallas_call(own_kernel, out_shape=(sds((rows, cols, chans), F32), sds(...  3.86 us
    ppermute x1, starting transfers between devices, shards(): lax.ppermute(jnp.where(core == 0, tail, head), axes, ring(lat_count, 1))  2.55 us
    unnamed x14, local copies, waits for them, and re-layouts  2.1 us
    pallas_call x1, Pallas kernels, shards(): pl.pallas_call(halo_kernel, out_shape=sds((rows, cols, chans), BF16), in_...  2.07 us
    select_n x1, other arithmetic, shards(): jnp.where(core == 0, head, tail)  1.16 us
    ppermute x1, waiting for transfers between devices, shards(): edges = lax.ppermute(edges, 'lon', SWAP)  0.86 us
    ppermute x1, starting transfers between devices, shards(): edges = lax.ppermute(edges, 'lon', SWAP)  0.81 us
    ppermute x1, starting transfers between devices, shards(): other = lax.ppermute(fields, 'lon', SWAP)  0.45 us
  transfers between devices with their start and end apart: 4, of which 2 were waited for; matrix products, arithmetic and copies ran while one was open for 8% of the time, Pallas kernels for 27%

profile of v3, /device:TPU:0, one launch (start us, length us, event | category | flops | bytes accessed | tf_op | source)
XLA Modules:
  0.0 14.3 jit_solution(2784208699935612915)
XLA Ops:
  0.0 0.5 %collective-permute-start.2 = (bf16[8,128,256]{2,1,0:T(8,128)(2,1)}, bf16[8,128,256]{2,1,0:T(8,128)(2,1)S(1)}, u32[]{:S(2)}, u32[]{:S(2)}) collective-permute-start(bf16[8,128,256]{2,1,0:T(8,128)(2,1)} %fields_in.1), channel_id=1, source_target_pairs={{0,4},{4,0},{1,5},{5,1},{2,6},{6,2},{3,7},{7,3},{8,12},{12,8},{9,1... | collective-permute-start | bytes 1572872 | tf_op jit(solution)/shard_map/ppermute | solution.py:230
  0.5 0.0 copy-start
  0.5 0.0 copy-start.1
  0.5 1.2 %broadcast_select_fusion = (bf16[4,128,256]{2,1,0:T(8,128)(2,1)S(1)}, bf16[4,128,256]{2,1,0:T(8,128)(2,1)S(1)}) fusion(pred[]{:T(512)S(6)} %eq.4, bf16[8,128,256]{2,1,0:T(8,128)(2,1)} %fields_in.1), kind=kLoop, calls=%fused_computation | loop fusion | flops 262144 | bytes 1048577 | tf_op jit(solution)/shard_map/jit(_where)/select_n | solution.py:233
  1.6 0.0 copy-start.4
  1.6 0.1 collective-permute-start.1
  1.7 2.5 %collective-permute-start = (bf16[4,128,256]{2,1,0:T(8,128)(2,1)S(1)}, bf16[4,128,256]{2,1,0:T(8,128)(2,1)S(1)}, u32[]{:S(2)}, u32[]{:S(2)}) collective-permute-start(bf16[4,128,256]{2,1,0:T(8,128)(2,1)S(1)} %get-tuple-element.18), channel_id=1, source_target_pairs={{0,8},{4,0},{8,16},{12,4},{16,24},{20,12},{24,28},{28,20},{1,9},{5... | collective-permute-start | bytes 786440 | tf_op jit(solution)/shard_map/ppermute | solution.py:232
  4.3 0.0 collective-permute-done.2.other
  4.3 0.0 copy-start.5
  4.3 0.0 copy-start.6
  4.3 0.0 copy-done
  4.3 0.0 copy-done.1
  4.3 0.0 copy-done.4
  4.3 0.6 %copy-done.5 = s32[8]{0:T(128)S(1)} copy-done((s32[8]{0:T(128)S(1)}, s32[8]{0:T(128)}, u32[]{:S(2)}) %copy-start.5) | copy-done | bytes 56
  4.9 0.0 copy-done.6
  4.9 0.0 copy-start.2
  4.9 0.7 %copy-done.2 = f32[32,4,9]{0,1,2:T(4,128)S(1)} copy-done((f32[32,4,9]{0,1,2:T(4,128)S(1)}, f32[32,4,9]{0,1,2:T(4,128)}, u32[]{:S(2)}) %copy-start.2) | copy-done | bytes 4632
  5.7 0.0 copy-start.3
  5.7 0.7 %copy-done.3 = bf16[4,8,256]{2,1,0:T(8,128)(2,1)S(1)} copy-done((bf16[4,8,256]{2,1,0:T(8,128)(2,1)S(1)}, bf16[4,8,256]{2,1,0:T(8,128)(2,1)}, u32[]{:S(2)}) %copy-start.3) | copy-done | bytes 16408
  6.4 3.9 %own_rows.1 = (f32[8,128,256]{2,1,0:T(8,128)S(1)}, bf16[512,256]{1,0:T(8,128)(2,1)S(1)}, bf16[1024,256]{1,0:T(8,128)(2,1)S(1)}) custom-call(s32[8]{0:T(128)S(1)} %copy-done.5, s32[8]{0:T(128)S(1)} %copy-done.6, f32[9,4,32]{2,1,0:T(4,128)S(1)} %bitcast.4, bf16[6,4,8]{2,1,0:T(4,128)(2,1)S(1)} %bitcast.5, bf16[8,128,256]{2,1,0:T(8,128)(2,1)S(1)} %copy-done, ...), custom_call_target="tpu_custom_call" | custom-call | flops 2000000000 | bytes 6000000 | tf_op jit(solution)/shard_map/own_rows/pallas_call | solution.py:240
  10.2 0.0 collective-permute-done.1.second_in
  10.2 0.2 %collective-permute-done.first_in = bf16[4,128,256]{2,1,0:T(8,128)(2,1)S(1)} collective-permute-done((bf16[4,128,256]{2,1,0:T(8,128)(2,1)S(1)}, bf16[4,128,256]{2,1,0:T(8,128)(2,1)S(1)}, u32[]{:S(2)}, u32[]{:S(2)}) %collective-permute-start) | collective-permute-done | bytes 262176 | tf_op jit(solution)/shard_map/ppermute | solution.py:232
  10.5 0.8 %collective-permute-start.3 = (bf16[8,8,256]{2,1,0:T(8,128)(2,1)S(1)}, bf16[8,8,256]{2,1,0:T(8,128)(2,1)S(1)}, u32[]{:S(2)}, u32[]{:S(2)}) collective-permute-start(bf16[8,8,256]{2,1,0:T(8,128)(2,1)S(1)} %maximum_maximum_fusion), channel_id=1, source_target_pairs={{0,4},{4,0},{1,5},{5,1},{2,6},{6,2},{3,7},{7,3},{8,12},{12,8},{9,1... | collective-permute-start | bytes 98312 | tf_op jit(solution)/shard_map/ppermute | solution.py:285
  11.3 0.9 %collective-permute-done.3.edges = bf16[8,8,256]{2,1,0:T(8,128)(2,1)S(1)} collective-permute-done((bf16[8,8,256]{2,1,0:T(8,128)(2,1)S(1)}, bf16[8,8,256]{2,1,0:T(8,128)(2,1)S(1)}, u32[]{:S(2)}, u32[]{:S(2)}) %collective-permute-start.3) | collective-permute-done | bytes 32800 | tf_op jit(solution)/shard_map/ppermute | solution.py:285
  12.2 2.1 %halo_rows.1 = bf16[8,128,256]{2,1,0:T(8,128)(2,1)} custom-call(bf16[4,128,256]{2,1,0:T(8,128)(2,1)S(1)} %collective-permute-done.first_in, bf16[4,128,256]{2,1,0:T(8,128)(2,1)S(1)} %collective-permute-done.1.second_in, bf16[8,8,256]{2,1,0:T(8,128)(2,1)S(1)} %collective-permute-done.3.edges, bf16[512,256]{1,0:T(8,128)(2,1)S(1)} %get-tuple-element.14.weights, ...), custom_call_target="tpu_custom_call" | custom-call | tf_op jit(solution)/shard_map/halo_rows/pallas_call | solution.py:286
  (2 shorter events, 0.0 us)
Async XLA Ops:
  0.0 4.3 %collective-permute-start.2 = (bf16[8,128,256]{2,1,0:T(8,128)(2,1)}, bf16[8,128,256]{2,1,0:T(8,128)(2,1)S(1)}, u32[]{:S(2)}, u32[]{:S(2)}) collective-permute-start(bf16[8,128,256]{2,1,0:T(8,128)(2,1)} %fields_in.1), channel_id=1, source_target_pairs={{0,4},{4,0},{1,5},{5,1},{2,6},{6,2},{3,7},{7,3},{8,12},{12,8},{9,1... | collective-permute-start | bytes 1572872 | tf_op jit(solution)/shard_map/ppermute | solution.py:230
  0.5 3.8 %copy-start = (bf16[8,128,256]{2,1,0:T(8,128)(2,1)S(1)}, bf16[8,128,256]{2,1,0:T(8,128)(2,1)}, u32[]{:S(2)}) copy-start(bf16[8,128,256]{2,1,0:T(8,128)(2,1)} %fields_in.1) | copy-start | bytes 1572868
  0.5 3.8 %copy-start.1 = (bf16[4,256,256]{2,1,0:T(8,128)(2,1)S(1)}, bf16[4,256,256]{2,1,0:T(8,128)(2,1)}, u32[]{:S(2)}) copy-start(bf16[4,256,256]{2,1,0:T(8,128)(2,1)} %param.13) | copy-start | bytes 1572868
  1.6 2.7 %copy-start.4 = (bf16[8,4,6]{0,1,2:T(4,128)(2,1)S(1)}, bf16[8,4,6]{0,1,2:T(4,128)(2,1)}, u32[]{:S(2)}) copy-start(bf16[8,4,6]{0,1,2:T(4,128)(2,1)} %param.9) | copy-start | bytes 1156
  1.6 8.6 %collective-permute-start.1 = (bf16[4,128,256]{2,1,0:T(8,128)(2,1)S(1)}, bf16[4,128,256]{2,1,0:T(8,128)(2,1)S(1)}, u32[]{:S(2)}, u32[]{:S(2)}) collective-permute-start(bf16[4,128,256]{2,1,0:T(8,128)(2,1)S(1)} %get-tuple-element.17), channel_id=1, source_target_pairs={{0,4},{4,12},{8,0},{12,20},{16,8},{20,28},{24,16},{28,24},{1,5},{5... | collective-permute-start | bytes 786440 | tf_op jit(solution)/shard_map/ppermute | solution.py:233
  1.7 8.8 %collective-permute-start = (bf16[4,128,256]{2,1,0:T(8,128)(2,1)S(1)}, bf16[4,128,256]{2,1,0:T(8,128)(2,1)S(1)}, u32[]{:S(2)}, u32[]{:S(2)}) collective-permute-start(bf16[4,128,256]{2,1,0:T(8,128)(2,1)S(1)} %get-tuple-element.18), channel_id=1, source_target_pairs={{0,8},{4,0},{8,16},{12,4},{16,24},{20,12},{24,28},{28,20},{1,9},{5... | collective-permute-start | bytes 786440 | tf_op jit(solution)/shard_map/ppermute | solution.py:232
  4.3 0.7 %copy-start.5 = (s32[8]{0:T(128)S(1)}, s32[8]{0:T(128)}, u32[]{:S(2)}) copy-start(s32[8]{0:T(128)} %start_in.1) | copy-start | bytes 100
  4.3 0.7 %copy-start.6 = (s32[8]{0:T(128)S(1)}, s32[8]{0:T(128)}, u32[]{:S(2)}) copy-start(s32[8]{0:T(128)} %width_in.1) | copy-start | bytes 100
  4.9 0.7 %copy-start.2 = (f32[32,4,9]{0,1,2:T(4,128)S(1)}, f32[32,4,9]{0,1,2:T(4,128)}, u32[]{:S(2)}) copy-start(f32[32,4,9]{0,1,2:T(4,128)} %param.8) | copy-start | bytes 13828
  5.7 0.7 %copy-start.3 = (bf16[4,8,256]{2,1,0:T(8,128)(2,1)S(1)}, bf16[4,8,256]{2,1,0:T(8,128)(2,1)}, u32[]{:S(2)}) copy-start(bf16[4,8,256]{2,1,0:T(8,128)(2,1)} %cycle_in.1) | copy-start | bytes 49156
  10.5 1.7 %collective-permute-start.3 = (bf16[8,8,256]{2,1,0:T(8,128)(2,1)S(1)}, bf16[8,8,256]{2,1,0:T(8,128)(2,1)S(1)}, u32[]{:S(2)}, u32[]{:S(2)}) collective-permute-start(bf16[8,8,256]{2,1,0:T(8,128)(2,1)S(1)} %maximum_maximum_fusion), channel_id=1, source_target_pairs={{0,4},{4,0},{1,5},{5,1},{2,6},{6,2},{3,7},{7,3},{8,12},{12,8},{9,1... | collective-permute-start | bytes 98312 | tf_op jit(solution)/shard_map/ppermute | solution.py:285

commit v4 on v3

--- a/solution.py
+++ b/solution.py
@@ -195,18 +195,20 @@
             acc[:, at, :] = acc[:, at, :] + matmul(weights, cells).reshape(rows, BLOCK, chans)
 
 
-def halo_kernel(first_in, second_in, edges, weights, acc, mix, out, ext, hidden):
+def halo_kernel(
+    first_in, second_in, first_edges, second_edges, weights, acc, mix, out, ext, hidden,
+):
     rows, cols, chans = out.shape
     basis = mix.shape[0] // chans
-    reach = edges.shape[1] // 2
+    reach = first_edges.shape[1] // 2
     is_first = lax.axis_index("lon") == 0
     pad = jnp.zeros((ext.shape[1] - cols - 2 * reach, chans), BF16)
     for s in range(2 * HALO):
         p = s % HALO
-        mine, his = (first_in, second_in) if s < HALO else (second_in, first_in)
-        a, b = (p + HALO, p) if s < HALO else (p, p + HALO)
-        body = jnp.where(is_first, mine[p], his[p])
-        edge = jnp.where(is_first, edges[a], edges[b])
+        by = (first_in, second_in) if s < HALO else (second_in, first_in)
+        body = jnp.where(is_first, by[0][p], by[1][p])
+        by = (first_edges, second_edges) if s < HALO else (second_edges, first_edges)
+        edge = jnp.where(is_first, by[0][p], by[1][p])
         ext[s] = jnp.concatenate([edge[reach:], body, edge[:reach], pad], axis=0)
     window_products(weights, ext, hidden, range(cols // BLOCK), rows, basis, cols, chans)
     half = rows // 2
@@ -227,10 +229,15 @@
     core = lax.axis_index("lon")
     axes = ("lat", "lon")
     assert cycle == 2 * cols and rows == 2 * HALO and basis * polar * BLOCK == rows * SPAN
+    ahead, back = ring(lat_count, 1), ring(lat_count, -1)
     other = lax.ppermute(fields, "lon", SWAP)
     head, tail = fields[:HALO], fields[rows - HALO :]
-    first = lax.ppermute(jnp.where(core == 0, tail, head), axes, ring(lat_count, 1))
-    second = lax.ppermute(jnp.where(core == 0, head, tail), axes, ring(lat_count, -1))
+    first = lax.ppermute(jnp.where(core == 0, tail, head), axes, ahead)
+    second = lax.ppermute(jnp.where(core == 0, head, tail), axes, back)
+    edges = jnp.concatenate([other[:, :reach], other[:, cols - reach :]], axis=1)
+    head, tail = edges[:HALO], edges[rows - HALO :]
+    first_edges = lax.ppermute(jnp.where(core == 0, tail, head), axes, ahead)
+    second_edges = lax.ppermute(jnp.where(core == 0, head, tail), axes, back)
 
     vmem = pl.BlockSpec(memory_space=pltpu.VMEM)
     hbm = pl.BlockSpec(memory_space=pltpu.HBM)
@@ -269,24 +276,24 @@
         ),
         name="own_rows",
     )(
-        band_start, band_width, jnp.transpose(lon_taps, (2, 1, 0)),
-        jnp.transpose(lat_taps, (2, 1, 0)), fields, cycle_taps,
-        mixing.reshape(basis * chans, chans), other,
+        *(
+            pltpu.with_memory_space_constraint(x, pltpu.HBM)
+            for x in (
+                band_start, band_width, jnp.transpose(lon_taps, (2, 1, 0)),
+                jnp.transpose(lat_taps, (2, 1, 0)), fields, cycle_taps,
+                mixing.reshape(basis * chans, chans),
+            )
+        ),
+        other,
     )
 
-    first, second, acc = lax.optimization_barrier((first, second, acc))
-    edges = jnp.concatenate(
-        [
-            jnp.concatenate([got[:, :reach], got[:, cols - reach :]], axis=1)
-            for got in (first, second)
-        ],
-        axis=0,
+    first, second, first_edges, second_edges, acc = lax.optimization_barrier(
+        (first, second, first_edges, second_edges, acc)
     )
-    edges = lax.ppermute(edges, "lon", SWAP)
     return pl.pallas_call(
         halo_kernel,
         out_shape=sds((rows, cols, chans), BF16),
-        in_specs=[vmem] * 6,
+        in_specs=[vmem] * 7,
         out_specs=vmem,
         scratch_shapes=[
             pltpu.VMEM((rows, ext_cols, chans), BF16),
@@ -294,7 +301,7 @@
         ],
         compiler_params=pltpu.CompilerParams(vmem_limit_bytes=32 * 1024 * 1024),
         name="halo_rows",
-    )(first, second, edges, halo_weights, acc, mix)
+    )(first, second, first_edges, second_edges, halo_weights, acc, mix)
 
 
 def solution(mesh):

time: 14.5 us -> 13.6 us (0.938); the launches traced: 14.3 us -> 13.5 us
  local copies, waits for them, and re-layouts: 2.11 us -> 0.02 us
  starting transfers between devices: 3.89 us -> 5.09 us
  Pallas kernels: 5.93 us -> 6.19 us
    unnamed x14 -> x0, local copies, waits for them, and re-layouts: 2.1 us -> none
    ppermute x3 -> x4, starting transfers between devices: 3.44 us -> 4.63 us  [the longest x1 2.59 us: shards(): first = lax.ppermute(jnp.where(core == 0, tail, head), axes, ahead)]
    pallas_call x1, Pallas kernels: 3.86 us -> 4.13 us  [shards(): pl.pallas_call(own_kernel, out_shape=(sds((rows, cols, chans), F32), sds(...]
    select_n x1 -> x2, other arithmetic: 1.16 us -> 1.09 us  [the longest x1 1.07 us: shards(): second = lax.ppermute(jnp.where(core == 0, head, tail), axes, back)]
    ppermute x3 -> x4, waiting for transfers between devices: 1.07 us -> 1.08 us  [the longest x1 0.71 us: shards(): second = lax.ppermute(jnp.where(core == 0, head, tail), axes, back)]
  transfers between devices with their start and end apart: 4 -> 5, of which waited for: 2 -> 3; matrix products, arithmetic and copies ran while one was open for 8% -> 8% of each run, Pallas kernels for 27% -> 31%
where the time goes in v4:
time: 13.6 us; the launch traced here: 13.5 us
  Pallas kernels  6.19 us (46%)
  starting transfers between devices  5.09 us (37%)
  other arithmetic  1.09 us (8%)
  waiting for transfers between devices  1.09 us (8%)
    pallas_call x1, Pallas kernels, shards(): pl.pallas_call(own_kernel, out_shape=(sds((rows, cols, chans), F32), sds(...  4.13 us
    ppermute x1, starting transfers between devices, shards(): first = lax.ppermute(jnp.where(core == 0, tail, head), axes, ahead)  2.59 us
    pallas_call x1, Pallas kernels, shards(): pl.pallas_call(halo_kernel, out_shape=sds((rows, cols, chans), BF16), in_...  2.06 us
    ppermute x1, starting transfers between devices, shards(): first_edges = lax.ppermute(jnp.where(core == 0, tail, head), axes, ahead)  2.04 us
    select_n x1, other arithmetic, shards(): second = lax.ppermute(jnp.where(core == 0, head, tail), axes, back)  1.07 us
    ppermute x1, waiting for transfers between devices, shards(): second = lax.ppermute(jnp.where(core == 0, head, tail), axes, back)  0.71 us
    ppermute x1, starting transfers between devices, shards(): other = lax.ppermute(fields, 'lon', SWAP)  0.45 us
  transfers between devices with their start and end apart: 5, of which 3 were waited for; matrix products, arithmetic and copies ran while one was open for 8% of the time, Pallas kernels for 31%

profile of v4, /device:TPU:0, one launch (start us, length us, event | category | flops | bytes accessed | tf_op | source)
XLA Modules:
  0.0 13.5 jit_solution(4596282380487954106)
XLA Ops:
  0.0 0.5 %collective-permute-start.2 = (bf16[8,128,256]{2,1,0:T(8,128)(2,1)}, bf16[8,128,256]{2,1,0:T(8,128)(2,1)S(1)}, u32[]{:S(2)}, u32[]{:S(2)}) collective-permute-start(bf16[8,128,256]{2,1,0:T(8,128)(2,1)} %fields_in.1), channel_id=1, source_target_pairs={{0,4},{4,0},{1,5},{5,1},{2,6},{6,2},{3,7},{7,3},{8,12},{12,8},{9,1... | collective-permute-start | bytes 1572872 | tf_op jit(solution)/shard_map/ppermute | solution.py:233
  0.5 1.1 %broadcast_select_fusion = (bf16[4,128,256]{2,1,0:T(8,128)(2,1)S(1)}, bf16[4,128,256]{2,1,0:T(8,128)(2,1)S(1)}) fusion(pred[]{:T(512)S(6)} %eq.2, bf16[8,128,256]{2,1,0:T(8,128)(2,1)} %fields_in.1), kind=kLoop, calls=%fused_computation | loop fusion | flops 262144 | bytes 1048577 | tf_op jit(solution)/shard_map/jit(_where)/select_n | solution.py:236
  1.5 2.6 %collective-permute-start = (bf16[4,128,256]{2,1,0:T(8,128)(2,1)S(1)}, bf16[4,128,256]{2,1,0:T(8,128)(2,1)S(1)}, u32[]{:S(2)}, u32[]{:S(2)}) collective-permute-start(bf16[4,128,256]{2,1,0:T(8,128)(2,1)S(1)} %get-tuple-element.24), channel_id=1, source_target_pairs={{0,8},{4,0},{8,16},{12,4},{16,24},{20,12},{24,28},{28,20},{1,9},{5... | collective-permute-start | bytes 786440 | tf_op jit(solution)/shard_map/ppermute | solution.py:235
  4.1 0.0 collective-permute-start.1
  4.1 0.0 collective-permute-done.2.other
  4.2 2.0 %collective-permute-start.3 = (bf16[4,8,256]{2,1,0:T(8,128)(2,1)S(1)}, bf16[4,8,256]{2,1,0:T(8,128)(2,1)S(1)}, u32[]{:S(2)}, u32[]{:S(2)}) collective-permute-start(bf16[4,8,256]{2,1,0:T(8,128)(2,1)S(1)} %get-tuple-element.26), channel_id=1, source_target_pairs={{0,8},{4,0},{8,16},{12,4},{16,24},{20,12},{24,28},{28,20},{1,9},{5... | collective-permute-start | bytes 49160 | tf_op jit(solution)/shard_map/ppermute | solution.py:239
  6.2 0.0 collective-permute-start.4
  6.2 4.1 %own_rows.1 = (f32[8,128,256]{2,1,0:T(8,128)S(1)}, bf16[512,256]{1,0:T(8,128)(2,1)S(1)}, bf16[1024,256]{1,0:T(8,128)(2,1)S(1)}) custom-call(s32[8]{0:T(128)} %start_in.1, s32[8]{0:T(128)} %width_in.1, f32[9,4,32]{2,1,0:T(4,128)} %bitcast.4, bf16[6,4,8]{2,1,0:T(4,128)(2,1)} %bitcast.5, bf16[8,128,256]{2,1,0:T(8,128)(2,1)} %fields_in.1, ...), custom_call_target="tpu_custom_call" | custom-call | flops 2000000000 | bytes 6000000 | tf_op jit(solution)/shard_map/own_rows/pallas_call | solution.py:247
  10.4 0.2 %collective-permute-done.first_in = bf16[4,128,256]{2,1,0:T(8,128)(2,1)S(1)} collective-permute-done((bf16[4,128,256]{2,1,0:T(8,128)(2,1)S(1)}, bf16[4,128,256]{2,1,0:T(8,128)(2,1)S(1)}, u32[]{:S(2)}, u32[]{:S(2)}) %collective-permute-start) | collective-permute-done | bytes 262176 | tf_op jit(solution)/shard_map/ppermute | solution.py:235
  10.6 0.7 %collective-permute-done.1.second_in = bf16[4,128,256]{2,1,0:T(8,128)(2,1)S(1)} collective-permute-done((bf16[4,128,256]{2,1,0:T(8,128)(2,1)S(1)}, bf16[4,128,256]{2,1,0:T(8,128)(2,1)S(1)}, u32[]{:S(2)}, u32[]{:S(2)}) %collective-permute-start.1) | collective-permute-done | bytes 262176 | tf_op jit(solution)/shard_map/ppermute | solution.py:236
  11.3 0.0 collective-permute-done.3.first_edges
  11.3 0.2 %collective-permute-done.4.second_edges = bf16[4,8,256]{2,1,0:T(8,128)(2,1)S(1)} collective-permute-done((bf16[4,8,256]{2,1,0:T(8,128)(2,1)S(1)}, bf16[4,8,256]{2,1,0:T(8,128)(2,1)S(1)}, u32[]{:S(2)}, u32[]{:S(2)}) %collective-permute-start.4) | collective-permute-done | bytes 16416 | tf_op jit(solution)/shard_map/ppermute | solution.py:240
  11.4 2.1 %halo_rows.1 = bf16[8,128,256]{2,1,0:T(8,128)(2,1)} custom-call(bf16[4,128,256]{2,1,0:T(8,128)(2,1)S(1)} %collective-permute-done.first_in, bf16[4,128,256]{2,1,0:T(8,128)(2,1)S(1)} %collective-permute-done.1.second_in, bf16[4,8,256]{2,1,0:T(8,128)(2,1)S(1)} %collective-permute-done.3.first_edges, ...), custom_call_target="tpu_custom_call" | custom-call | tf_op jit(solution)/shard_map/halo_rows/pallas_call | solution.py:293
  (2 shorter events, 0.0 us)
Async XLA Ops:
  0.0 4.1 %collective-permute-start.2 = (bf16[8,128,256]{2,1,0:T(8,128)(2,1)}, bf16[8,128,256]{2,1,0:T(8,128)(2,1)S(1)}, u32[]{:S(2)}, u32[]{:S(2)}) collective-permute-start(bf16[8,128,256]{2,1,0:T(8,128)(2,1)} %fields_in.1), channel_id=1, source_target_pairs={{0,4},{4,0},{1,5},{5,1},{2,6},{6,2},{3,7},{7,3},{8,12},{12,8},{9,1... | collective-permute-start | bytes 1572872 | tf_op jit(solution)/shard_map/ppermute | solution.py:233
  1.5 9.0 %collective-permute-start = (bf16[4,128,256]{2,1,0:T(8,128)(2,1)S(1)}, bf16[4,128,256]{2,1,0:T(8,128)(2,1)S(1)}, u32[]{:S(2)}, u32[]{:S(2)}) collective-permute-start(bf16[4,128,256]{2,1,0:T(8,128)(2,1)S(1)} %get-tuple-element.24), channel_id=1, source_target_pairs={{0,8},{4,0},{8,16},{12,4},{16,24},{20,12},{24,28},{28,20},{1,9},{5... | collective-permute-start | bytes 786440 | tf_op jit(solution)/shard_map/ppermute | solution.py:235
  4.1 7.2 %collective-permute-start.1 = (bf16[4,128,256]{2,1,0:T(8,128)(2,1)S(1)}, bf16[4,128,256]{2,1,0:T(8,128)(2,1)S(1)}, u32[]{:S(2)}, u32[]{:S(2)}) collective-permute-start(bf16[4,128,256]{2,1,0:T(8,128)(2,1)S(1)} %get-tuple-element.23), channel_id=1, source_target_pairs={{0,4},{4,12},{8,0},{12,20},{16,8},{20,28},{24,16},{28,24},{1,5},{5... | collective-permute-start | bytes 786440 | tf_op jit(solution)/shard_map/ppermute | solution.py:236
  4.2 7.1 %collective-permute-start.3 = (bf16[4,8,256]{2,1,0:T(8,128)(2,1)S(1)}, bf16[4,8,256]{2,1,0:T(8,128)(2,1)S(1)}, u32[]{:S(2)}, u32[]{:S(2)}) collective-permute-start(bf16[4,8,256]{2,1,0:T(8,128)(2,1)S(1)} %get-tuple-element.26), channel_id=1, source_target_pairs={{0,8},{4,0},{8,16},{12,4},{16,24},{20,12},{24,28},{28,20},{1,9},{5... | collective-permute-start | bytes 49160 | tf_op jit(solution)/shard_map/ppermute | solution.py:239
  6.2 5.2 %collective-permute-start.4 = (bf16[4,8,256]{2,1,0:T(8,128)(2,1)S(1)}, bf16[4,8,256]{2,1,0:T(8,128)(2,1)S(1)}, u32[]{:S(2)}, u32[]{:S(2)}) collective-permute-start(bf16[4,8,256]{2,1,0:T(8,128)(2,1)S(1)} %get-tuple-element.25), channel_id=1, source_target_pairs={{0,4},{4,12},{8,0},{12,20},{16,8},{20,28},{24,16},{28,24},{1,5},{5... | collective-permute-start | bytes 49160 | tf_op jit(solution)/shard_map/ppermute | solution.py:240

commit v5 on v4

--- a/solution.py
+++ b/solution.py
@@ -196,7 +196,7 @@
 
 
 def halo_kernel(
-    first_in, second_in, first_edges, second_edges, weights, acc, mix, out, ext, hidden,
+    second_in, first_in, second_edges, first_edges, weights, acc, mix, out, ext, hidden,
 ):
     rows, cols, chans = out.shape
     basis = mix.shape[0] // chans
@@ -232,12 +232,12 @@
     ahead, back = ring(lat_count, 1), ring(lat_count, -1)
     other = lax.ppermute(fields, "lon", SWAP)
     head, tail = fields[:HALO], fields[rows - HALO :]
+    second = lax.ppermute(jnp.where(core == 0, head, tail), axes, back)
     first = lax.ppermute(jnp.where(core == 0, tail, head), axes, ahead)
-    second = lax.ppermute(jnp.where(core == 0, head, tail), axes, back)
     edges = jnp.concatenate([other[:, :reach], other[:, cols - reach :]], axis=1)
     head, tail = edges[:HALO], edges[rows - HALO :]
+    second_edges = lax.ppermute(jnp.where(core == 0, head, tail), axes, back)
     first_edges = lax.ppermute(jnp.where(core == 0, tail, head), axes, ahead)
-    second_edges = lax.ppermute(jnp.where(core == 0, head, tail), axes, back)
 
     vmem = pl.BlockSpec(memory_space=pltpu.VMEM)
     hbm = pl.BlockSpec(memory_space=pltpu.HBM)
@@ -287,8 +287,8 @@
         other,
     )
 
-    first, second, first_edges, second_edges, acc = lax.optimization_barrier(
-        (first, second, first_edges, second_edges, acc)
+    second, first, second_edges, first_edges, acc = lax.optimization_barrier(
+        (second, first, second_edges, first_edges, acc)
     )
     return pl.pallas_call(
         halo_kernel,
@@ -301,7 +301,7 @@
         ],
         compiler_params=pltpu.CompilerParams(vmem_limit_bytes=32 * 1024 * 1024),
         name="halo_rows",
-    )(first, second, first_edges, second_edges, halo_weights, acc, mix)
+    )(second, first, second_edges, first_edges, halo_weights, acc, mix)
 
 
 def solution(mesh):

time: 13.6 us -> 13.2 us (0.971)
  the two profiles are of different devices: /device:TPU:0 before, /device:TPU:1 now
where the time goes in v5:
time: 13.2 us; the launch traced here: 13.1 us
  Pallas kernels  6.16 us (47%)
  starting transfers between devices  4.3 us (33%)
  waiting for transfers between devices  1.45 us (11%)
  other arithmetic  1.09 us (8%)
    pallas_call x1, Pallas kernels, shards(): pl.pallas_call(own_kernel, out_shape=(sds((rows, cols, chans), F32), sds(...  4.1 us
    ppermute x1, starting transfers between devices, shards(): second = lax.ppermute(jnp.where(core == 0, head, tail), axes, back)  2.76 us
    pallas_call x1, Pallas kernels, shards(): pl.pallas_call(halo_kernel, out_shape=sds((rows, cols, chans), BF16), in_...  2.06 us
    ppermute x1, starting transfers between devices, shards(): second_edges = lax.ppermute(jnp.where(core == 0, head, tail), axes, back)  1.48 us
    ppermute x1, waiting for transfers between devices, shards(): first = lax.ppermute(jnp.where(core == 0, tail, head), axes, ahead)  1.23 us
    select_n x1, other arithmetic, shards(): first = lax.ppermute(jnp.where(core == 0, tail, head), axes, ahead)  1.07 us
  transfers between devices with their start and end apart: 5, of which 3 were waited for; matrix products, arithmetic and copies ran while one was open for 8% of the time, Pallas kernels for 31%

profile of v5, /device:TPU:1, one launch (start us, length us, event | category | flops | bytes accessed | tf_op | source)
XLA Modules:
  0.0 13.1 jit_solution(9893465702865329584)
XLA Ops:
  0.0 0.1 collective-permute-start.2
  0.1 1.1 %broadcast_select_fusion = (bf16[4,128,256]{2,1,0:T(8,128)(2,1)S(1)}, bf16[4,128,256]{2,1,0:T(8,128)(2,1)S(1)}) fusion(pred[]{:T(512)S(6)} %eq.2, bf16[8,128,256]{2,1,0:T(8,128)(2,1)} %fields_in.1), kind=kLoop, calls=%fused_computation | loop fusion | flops 262144 | bytes 1048577 | tf_op jit(solution)/shard_map/jit(_where)/select_n | solution.py:236
  1.1 2.8 %collective-permute-start = (bf16[4,128,256]{2,1,0:T(8,128)(2,1)S(1)}, bf16[4,128,256]{2,1,0:T(8,128)(2,1)S(1)}, u32[]{:S(2)}, u32[]{:S(2)}) collective-permute-start(bf16[4,128,256]{2,1,0:T(8,128)(2,1)S(1)} %get-tuple-element.24), channel_id=1, source_target_pairs={{0,4},{4,12},{8,0},{12,20},{16,8},{20,28},{24,16},{28,24},{1,5},{5... | collective-permute-start | bytes 786440 | tf_op jit(solution)/shard_map/ppermute | solution.py:235
  3.9 0.0 collective-permute-start.1
  3.9 0.0 collective-permute-done.2.other
  3.9 1.5 %collective-permute-start.3 = (bf16[4,8,256]{2,1,0:T(8,128)(2,1)S(1)}, bf16[4,8,256]{2,1,0:T(8,128)(2,1)S(1)}, u32[]{:S(2)}, u32[]{:S(2)}) collective-permute-start(bf16[4,8,256]{2,1,0:T(8,128)(2,1)S(1)} %get-tuple-element.26), channel_id=1, source_target_pairs={{0,4},{4,12},{8,0},{12,20},{16,8},{20,28},{24,16},{28,24},{1,5},{5... | collective-permute-start | bytes 49160 | tf_op jit(solution)/shard_map/ppermute | solution.py:239
  5.4 0.0 collective-permute-start.4
  5.4 4.1 %own_rows.1 = (f32[8,128,256]{2,1,0:T(8,128)S(1)}, bf16[512,256]{1,0:T(8,128)(2,1)S(1)}, bf16[1024,256]{1,0:T(8,128)(2,1)S(1)}) custom-call(s32[8]{0:T(128)} %start_in.1, s32[8]{0:T(128)} %width_in.1, f32[9,4,32]{2,1,0:T(4,128)} %bitcast.4, bf16[6,4,8]{2,1,0:T(4,128)(2,1)} %bitcast.5, bf16[8,128,256]{2,1,0:T(8,128)(2,1)} %fields_in.1, ...), custom_call_target="tpu_custom_call" | custom-call | flops 2000000000 | bytes 6000000 | tf_op jit(solution)/shard_map/own_rows/pallas_call | solution.py:247
  9.5 0.1 collective-permute-done.second_in
  9.6 1.2 %collective-permute-done.1.first_in = bf16[4,128,256]{2,1,0:T(8,128)(2,1)S(1)} collective-permute-done((bf16[4,128,256]{2,1,0:T(8,128)(2,1)S(1)}, bf16[4,128,256]{2,1,0:T(8,128)(2,1)S(1)}, u32[]{:S(2)}, u32[]{:S(2)}) %collective-permute-start.1) | collective-permute-done | bytes 262176 | tf_op jit(solution)/shard_map/ppermute | solution.py:236
  10.8 0.0 collective-permute-done.3.second_edges
  10.8 0.2 %collective-permute-done.4.first_edges = bf16[4,8,256]{2,1,0:T(8,128)(2,1)S(1)} collective-permute-done((bf16[4,8,256]{2,1,0:T(8,128)(2,1)S(1)}, bf16[4,8,256]{2,1,0:T(8,128)(2,1)S(1)}, u32[]{:S(2)}, u32[]{:S(2)}) %collective-permute-start.4) | collective-permute-done | bytes 16416 | tf_op jit(solution)/shard_map/ppermute | solution.py:240
  11.0 2.1 %halo_rows.1 = bf16[8,128,256]{2,1,0:T(8,128)(2,1)} custom-call(bf16[4,128,256]{2,1,0:T(8,128)(2,1)S(1)} %collective-permute-done.second_in, bf16[4,128,256]{2,1,0:T(8,128)(2,1)S(1)} %collective-permute-done.1.first_in, bf16[4,8,256]{2,1,0:T(8,128)(2,1)S(1)} %collective-permute-done.3.second_edges, ...), custom_call_target="tpu_custom_call" | custom-call | tf_op jit(solution)/shard_map/halo_rows/pallas_call | solution.py:293
  (2 shorter events, 0.0 us)
Async XLA Ops:
  0.0 3.9 %collective-permute-start.2 = (bf16[8,128,256]{2,1,0:T(8,128)(2,1)}, bf16[8,128,256]{2,1,0:T(8,128)(2,1)S(1)}, u32[]{:S(2)}, u32[]{:S(2)}) collective-permute-start(bf16[8,128,256]{2,1,0:T(8,128)(2,1)} %fields_in.1), channel_id=1, source_target_pairs={{0,4},{4,0},{1,5},{5,1},{2,6},{6,2},{3,7},{7,3},{8,12},{12,8},{9,1... | collective-permute-start | bytes 1572872 | tf_op jit(solution)/shard_map/ppermute | solution.py:233
  1.1 8.5 %collective-permute-start = (bf16[4,128,256]{2,1,0:T(8,128)(2,1)S(1)}, bf16[4,128,256]{2,1,0:T(8,128)(2,1)S(1)}, u32[]{:S(2)}, u32[]{:S(2)}) collective-permute-start(bf16[4,128,256]{2,1,0:T(8,128)(2,1)S(1)} %get-tuple-element.24), channel_id=1, source_target_pairs={{0,4},{4,12},{8,0},{12,20},{16,8},{20,28},{24,16},{28,24},{1,5},{5... | collective-permute-start | bytes 786440 | tf_op jit(solution)/shard_map/ppermute | solution.py:235
  3.9 6.9 %collective-permute-start.1 = (bf16[4,128,256]{2,1,0:T(8,128)(2,1)S(1)}, bf16[4,128,256]{2,1,0:T(8,128)(2,1)S(1)}, u32[]{:S(2)}, u32[]{:S(2)}) collective-permute-start(bf16[4,128,256]{2,1,0:T(8,128)(2,1)S(1)} %get-tuple-element.23), channel_id=1, source_target_pairs={{0,8},{4,0},{8,16},{12,4},{16,24},{20,12},{24,28},{28,20},{1,9},{5... | collective-permute-start | bytes 786440 | tf_op jit(solution)/shard_map/ppermute | solution.py:236
  3.9 6.9 %collective-permute-start.3 = (bf16[4,8,256]{2,1,0:T(8,128)(2,1)S(1)}, bf16[4,8,256]{2,1,0:T(8,128)(2,1)S(1)}, u32[]{:S(2)}, u32[]{:S(2)}) collective-permute-start(bf16[4,8,256]{2,1,0:T(8,128)(2,1)S(1)} %get-tuple-element.26), channel_id=1, source_target_pairs={{0,4},{4,12},{8,0},{12,20},{16,8},{20,28},{24,16},{28,24},{1,5},{5... | collective-permute-start | bytes 49160 | tf_op jit(solution)/shard_map/ppermute | solution.py:239
  5.4 5.6 %collective-permute-start.4 = (bf16[4,8,256]{2,1,0:T(8,128)(2,1)S(1)}, bf16[4,8,256]{2,1,0:T(8,128)(2,1)S(1)}, u32[]{:S(2)}, u32[]{:S(2)}) collective-permute-start(bf16[4,8,256]{2,1,0:T(8,128)(2,1)S(1)} %get-tuple-element.25), channel_id=1, source_target_pairs={{0,8},{4,0},{8,16},{12,4},{16,24},{20,12},{24,28},{28,20},{1,9},{5... | collective-permute-start | bytes 49160 | tf_op jit(solution)/shard_map/ppermute | solution.py:240

commit v6 on v5

--- a/solution.py
+++ b/solution.py
@@ -41,17 +41,14 @@
     return total
 
 
-def window_products(weights, ext, hidden, blocks, rows, basis, cols, chans):
-    for b in blocks:
-        cells = ext[:, BLOCK * b : BLOCK * b + SPAN, :].reshape(-1, chans)
+def window_products(weights, ext, hidden, groups, cols, chans):
+    for at in range(0, cols, BLOCK):
+        cells = ext[:, at : at + SPAN, :].reshape(-1, chans)
         part = matmul(weights[...], cells).astype(BF16)
-        for k in range(basis):
-            for i in range(rows):
-                at = (k * rows + i) * BLOCK
-                hidden[
-                    i * cols + BLOCK * b : i * cols + BLOCK * (b + 1),
-                    k * chans : (k + 1) * chans,
-                ] = part[at : at + BLOCK]
+        for n, (i, k) in enumerate(groups):
+            hidden[i * cols + at : i * cols + at + BLOCK, k * chans : (k + 1) * chans] = part[
+                n * BLOCK : (n + 1) * BLOCK
+            ]
 
 
 def own_kernel(
@@ -134,6 +131,7 @@
         for i in range(rows):
             at = (k * rows + i) * BLOCK
             own_weights[at : at + BLOCK, :] = staircase(own_line[i : i + 1], BLOCK)
+            at = ((i // HALO * basis + k) * HALO + i % HALO) * BLOCK
             halo_weights[at : at + BLOCK, :] = staircase(halo_line[i : i + 1], BLOCK)
 
     copies[4].wait()
@@ -142,9 +140,8 @@
         ext[r] = jnp.concatenate(
             [other[r, cols - reach :], fields[r], other[r, :reach], pad], axis=0
         )
-    window_products(
-        own_weights, ext, hidden, range(cols // BLOCK), rows, basis, cols, chans
-    )
+    groups = [(i, k) for k in range(basis) for i in range(rows)]
+    window_products(own_weights, ext, hidden, groups, cols, chans)
     copies[5].wait()
     copies[6].wait()
     half = rows // 2
@@ -202,20 +199,51 @@
     basis = mix.shape[0] // chans
     reach = first_edges.shape[1] // 2
     is_first = lax.axis_index("lon") == 0
+    has_upper = lax.axis_index("lat") != 0
+    has_lower = lax.axis_index("lat") != lax.axis_size("lat") - 1
+    half = rows // 2
+    group = half * basis * BLOCK
     pad = jnp.zeros((ext.shape[1] - cols - 2 * reach, chans), BF16)
-    for s in range(2 * HALO):
-        p = s % HALO
-        by = (first_in, second_in) if s < HALO else (second_in, first_in)
-        body = jnp.where(is_first, by[0][p], by[1][p])
-        by = (first_edges, second_edges) if s < HALO else (second_edges, first_edges)
-        edge = jnp.where(is_first, by[0][p], by[1][p])
-        ext[s] = jnp.concatenate([edge[reach:], body, edge[:reach], pad], axis=0)
-    window_products(weights, ext, hidden, range(cols // BLOCK), rows, basis, cols, chans)
-    half = rows // 2
-    for n in range(2):
-        total = matmul(hidden[n * half * cols : (n + 1) * half * cols], mix[...])
-        at = slice(n * half, (n + 1) * half)
-        out[at] = (total.reshape(half, cols, chans) + acc[at]).astype(BF16)
+
+    def add(sides):
+        groups = []
+        for side in sides:
+            by = [(first_in, second_in), (second_in, first_in)][side]
+            by_edges = [(first_edges, second_edges), (second_edges, first_edges)][side]
+            for p in range(HALO):
+                body = jnp.where(is_first, by[0][p], by[1][p])
+                edge = jnp.where(is_first, by_edges[0][p], by_edges[1][p])
+                ext[side * HALO + p] = jnp.concatenate(
+                    [edge[reach:], body, edge[:reach], pad], axis=0
+                )
+            groups += [(side * half + i, k) for k in range(basis) for i in range(half)]
+        at, end = sides[0], sides[-1] + 1
+        window_products(
+            weights.at[at * group : end * group, at * HALO * SPAN : end * HALO * SPAN],
+            ext.at[at * HALO : end * HALO], hidden, groups, cols, chans,
+        )
+        for side in sides:
+            at = slice(side * half, (side + 1) * half)
+            total = matmul(hidden[side * half * cols : (side + 1) * half * cols], mix[...])
+            out[at] = (total.reshape(half, cols, chans) + acc[at]).astype(BF16)
+
+    def keep(side):
+        at = slice(side * half, (side + 1) * half)
+        out[at] = acc[at].astype(BF16)
+
+    @pl.when(has_upper & has_lower)
+    def both_sides():
+        add((0, 1))
+
+    @pl.when(jnp.logical_not(has_upper))
+    def lower_side():
+        keep(0)
+        add((1,))
+
+    @pl.when(jnp.logical_not(has_lower))
+    def upper_side():
+        add((0,))
+        keep(1)
 
 
 def shards(fields, lon_taps, lat_taps, cycle_taps, band_start, band_width, mixing):

time: 13.2 us -> 12.8 us (0.970)
  the two profiles are of different devices: /device:TPU:1 before, /device:TPU:15 now
where the time goes in v6:
time: 12.8 us; the launch traced here: 12.7 us
  Pallas kernels  4.98 us (39%)
  starting transfers between devices  3.64 us (28%)
  waiting for transfers between devices  2.94 us (23%)
  other arithmetic  1.09 us (9%)
    pallas_call x1, Pallas kernels, shards(): pl.pallas_call(own_kernel, out_shape=(sds((rows, cols, chans), F32), sds(...  2.9 us
    pallas_call x1, Pallas kernels, shards(): pl.pallas_call(halo_kernel, out_shape=sds((rows, cols, chans), BF16), in_...  2.09 us
    ppermute x1, waiting for transfers between devices, shards(): second = lax.ppermute(jnp.where(core == 0, head, tail), axes, back)  1.52 us
    ppermute x1, starting transfers between devices, shards(): second = lax.ppermute(jnp.where(core == 0, head, tail), axes, back)  1.31 us
    ppermute x1, starting transfers between devices, shards(): second_edges = lax.ppermute(jnp.where(core == 0, head, tail), axes, back)  1.31 us
    ppermute x1, waiting for transfers between devices, shards(): first = lax.ppermute(jnp.where(core == 0, tail, head), axes, ahead)  1.25 us
    select_n x1, other arithmetic, shards(): first = lax.ppermute(jnp.where(core == 0, tail, head), axes, ahead)  1.07 us
    ppermute x1, starting transfers between devices, shards(): other = lax.ppermute(fields, 'lon', SWAP)  0.68 us
  transfers between devices with their start and end apart: 5, of which 3 were waited for; matrix products, arithmetic and copies ran while one was open for 9% of the time, Pallas kernels for 23%

profile of v6, /device:TPU:15, one launch (start us, length us, event | category | flops | bytes accessed | tf_op | source)
XLA Modules:
  0.0 12.7 jit_solution(15904907680999707687)
XLA Ops:
  0.0 0.7 %collective-permute-start.2 = (bf16[8,128,256]{2,1,0:T(8,128)(2,1)}, bf16[8,128,256]{2,1,0:T(8,128)(2,1)S(1)}, u32[]{:S(2)}, u32[]{:S(2)}) collective-permute-start(bf16[8,128,256]{2,1,0:T(8,128)(2,1)} %fields_in.1), channel_id=1, source_target_pairs={{0,4},{4,0},{1,5},{5,1},{2,6},{6,2},{3,7},{7,3},{8,12},{12,8},{9,1... | collective-permute-start | bytes 1572872 | tf_op jit(solution)/shard_map/ppermute | solution.py:261
  0.7 1.1 %broadcast_select_fusion = (bf16[4,128,256]{2,1,0:T(8,128)(2,1)S(1)}, bf16[4,128,256]{2,1,0:T(8,128)(2,1)S(1)}) fusion(pred[]{:T(512)S(6)} %eq.2, bf16[8,128,256]{2,1,0:T(8,128)(2,1)} %fields_in.1), kind=kLoop, calls=%fused_computation | loop fusion | flops 262144 | bytes 1048577 | tf_op jit(solution)/shard_map/jit(_where)/select_n | solution.py:264
  1.7 1.3 %collective-permute-start = (bf16[4,128,256]{2,1,0:T(8,128)(2,1)S(1)}, bf16[4,128,256]{2,1,0:T(8,128)(2,1)S(1)}, u32[]{:S(2)}, u32[]{:S(2)}) collective-permute-start(bf16[4,128,256]{2,1,0:T(8,128)(2,1)S(1)} %get-tuple-element.24), channel_id=1, source_target_pairs={{0,4},{4,12},{8,0},{12,20},{16,8},{20,28},{24,16},{28,24},{1,5},{5... | collective-permute-start | bytes 786440 | tf_op jit(solution)/shard_map/ppermute | solution.py:263
  3.1 0.2 %collective-permute-start.1 = (bf16[4,128,256]{2,1,0:T(8,128)(2,1)S(1)}, bf16[4,128,256]{2,1,0:T(8,128)(2,1)S(1)}, u32[]{:S(2)}, u32[]{:S(2)}) collective-permute-start(bf16[4,128,256]{2,1,0:T(8,128)(2,1)S(1)} %get-tuple-element.23), channel_id=1, source_target_pairs={{0,8},{4,0},{8,16},{12,4},{16,24},{20,12},{24,28},{28,20},{1,9},{5... | collective-permute-start | bytes 786440 | tf_op jit(solution)/shard_map/ppermute | solution.py:264
  3.2 0.0 collective-permute-done.2.other
  3.3 1.3 %collective-permute-start.3 = (bf16[4,8,256]{2,1,0:T(8,128)(2,1)S(1)}, bf16[4,8,256]{2,1,0:T(8,128)(2,1)S(1)}, u32[]{:S(2)}, u32[]{:S(2)}) collective-permute-start(bf16[4,8,256]{2,1,0:T(8,128)(2,1)S(1)} %get-tuple-element.26), channel_id=1, source_target_pairs={{0,4},{4,12},{8,0},{12,20},{16,8},{20,28},{24,16},{28,24},{1,5},{5... | collective-permute-start | bytes 49160 | tf_op jit(solution)/shard_map/ppermute | solution.py:267
  4.6 0.2 %collective-permute-start.4 = (bf16[4,8,256]{2,1,0:T(8,128)(2,1)S(1)}, bf16[4,8,256]{2,1,0:T(8,128)(2,1)S(1)}, u32[]{:S(2)}, u32[]{:S(2)}) collective-permute-start(bf16[4,8,256]{2,1,0:T(8,128)(2,1)S(1)} %get-tuple-element.25), channel_id=1, source_target_pairs={{0,8},{4,0},{8,16},{12,4},{16,24},{20,12},{24,28},{28,20},{1,9},{5... | collective-permute-start | bytes 49160 | tf_op jit(solution)/shard_map/ppermute | solution.py:268
  4.8 2.9 %own_rows.1 = (f32[8,128,256]{2,1,0:T(8,128)S(1)}, bf16[512,256]{1,0:T(8,128)(2,1)S(1)}, bf16[1024,256]{1,0:T(8,128)(2,1)S(1)}) custom-call(s32[8]{0:T(128)} %start_in.1, s32[8]{0:T(128)} %width_in.1, f32[9,4,32]{2,1,0:T(4,128)} %bitcast.4, bf16[6,4,8]{2,1,0:T(4,128)(2,1)} %bitcast.5, bf16[8,128,256]{2,1,0:T(8,128)(2,1)} %fields_in.1, ...), custom_call_target="tpu_custom_call" | custom-call | flops 2000000000 | bytes 6000000 | tf_op jit(solution)/shard_map/own_rows/pallas_call | solution.py:275
  7.7 1.5 %collective-permute-done.second_in = bf16[4,128,256]{2,1,0:T(8,128)(2,1)S(1)} collective-permute-done((bf16[4,128,256]{2,1,0:T(8,128)(2,1)S(1)}, bf16[4,128,256]{2,1,0:T(8,128)(2,1)S(1)}, u32[]{:S(2)}, u32[]{:S(2)}) %collective-permute-start) | collective-permute-done | bytes 262176 | tf_op jit(solution)/shard_map/ppermute | solution.py:263
  9.2 1.3 %collective-permute-done.1.first_in = bf16[4,128,256]{2,1,0:T(8,128)(2,1)S(1)} collective-permute-done((bf16[4,128,256]{2,1,0:T(8,128)(2,1)S(1)}, bf16[4,128,256]{2,1,0:T(8,128)(2,1)S(1)}, u32[]{:S(2)}, u32[]{:S(2)}) %collective-permute-start.1) | collective-permute-done | bytes 262176 | tf_op jit(solution)/shard_map/ppermute | solution.py:264
  10.4 0.0 collective-permute-done.3.second_edges
  10.4 0.2 %collective-permute-done.4.first_edges = bf16[4,8,256]{2,1,0:T(8,128)(2,1)S(1)} collective-permute-done((bf16[4,8,256]{2,1,0:T(8,128)(2,1)S(1)}, bf16[4,8,256]{2,1,0:T(8,128)(2,1)S(1)}, u32[]{:S(2)}, u32[]{:S(2)}) %collective-permute-start.4) | collective-permute-done | bytes 16416 | tf_op jit(solution)/shard_map/ppermute | solution.py:268
  10.6 2.1 %halo_rows.1 = bf16[8,128,256]{2,1,0:T(8,128)(2,1)} custom-call(bf16[4,128,256]{2,1,0:T(8,128)(2,1)S(1)} %collective-permute-done.second_in, bf16[4,128,256]{2,1,0:T(8,128)(2,1)S(1)} %collective-permute-done.1.first_in, bf16[4,8,256]{2,1,0:T(8,128)(2,1)S(1)} %collective-permute-done.3.second_edges, ...), custom_call_target="tpu_custom_call" | custom-call | tf_op jit(solution)/shard_map/halo_rows/pallas_call | solution.py:321
  (2 shorter events, 0.0 us)
Async XLA Ops:
  0.0 3.2 %collective-permute-start.2 = (bf16[8,128,256]{2,1,0:T(8,128)(2,1)}, bf16[8,128,256]{2,1,0:T(8,128)(2,1)S(1)}, u32[]{:S(2)}, u32[]{:S(2)}) collective-permute-start(bf16[8,128,256]{2,1,0:T(8,128)(2,1)} %fields_in.1), channel_id=1, source_target_pairs={{0,4},{4,0},{1,5},{5,1},{2,6},{6,2},{3,7},{7,3},{8,12},{12,8},{9,1... | collective-permute-start | bytes 1572872 | tf_op jit(solution)/shard_map/ppermute | solution.py:261
  1.7 7.4 %collective-permute-start = (bf16[4,128,256]{2,1,0:T(8,128)(2,1)S(1)}, bf16[4,128,256]{2,1,0:T(8,128)(2,1)S(1)}, u32[]{:S(2)}, u32[]{:S(2)}) collective-permute-start(bf16[4,128,256]{2,1,0:T(8,128)(2,1)S(1)} %get-tuple-element.24), channel_id=1, source_target_pairs={{0,4},{4,12},{8,0},{12,20},{16,8},{20,28},{24,16},{28,24},{1,5},{5... | collective-permute-start | bytes 786440 | tf_op jit(solution)/shard_map/ppermute | solution.py:263
  3.1 7.4 %collective-permute-start.1 = (bf16[4,128,256]{2,1,0:T(8,128)(2,1)S(1)}, bf16[4,128,256]{2,1,0:T(8,128)(2,1)S(1)}, u32[]{:S(2)}, u32[]{:S(2)}) collective-permute-start(bf16[4,128,256]{2,1,0:T(8,128)(2,1)S(1)} %get-tuple-element.23), channel_id=1, source_target_pairs={{0,8},{4,0},{8,16},{12,4},{16,24},{20,12},{24,28},{28,20},{1,9},{5... | collective-permute-start | bytes 786440 | tf_op jit(solution)/shard_map/ppermute | solution.py:264
  3.3 7.2 %collective-permute-start.3 = (bf16[4,8,256]{2,1,0:T(8,128)(2,1)S(1)}, bf16[4,8,256]{2,1,0:T(8,128)(2,1)S(1)}, u32[]{:S(2)}, u32[]{:S(2)}) collective-permute-start(bf16[4,8,256]{2,1,0:T(8,128)(2,1)S(1)} %get-tuple-element.26), channel_id=1, source_target_pairs={{0,4},{4,12},{8,0},{12,20},{16,8},{20,28},{24,16},{28,24},{1,5},{5... | collective-permute-start | bytes 49160 | tf_op jit(solution)/shard_map/ppermute | solution.py:267
  4.6 6.0 %collective-permute-start.4 = (bf16[4,8,256]{2,1,0:T(8,128)(2,1)S(1)}, bf16[4,8,256]{2,1,0:T(8,128)(2,1)S(1)}, u32[]{:S(2)}, u32[]{:S(2)}) collective-permute-start(bf16[4,8,256]{2,1,0:T(8,128)(2,1)S(1)} %get-tuple-element.25), channel_id=1, source_target_pairs={{0,8},{4,0},{8,16},{12,4},{16,24},{20,12},{24,28},{28,20},{1,9},{5... | collective-permute-start | bytes 49160 | tf_op jit(solution)/shard_map/ppermute | solution.py:268

commit v7 on v5

--- a/solution.py
+++ b/solution.py
@@ -41,17 +41,14 @@
     return total
 
 
-def window_products(weights, ext, hidden, blocks, rows, basis, cols, chans):
-    for b in blocks:
-        cells = ext[:, BLOCK * b : BLOCK * b + SPAN, :].reshape(-1, chans)
+def window_products(weights, ext, hidden, groups, cols, chans):
+    for at in range(0, cols, BLOCK):
+        cells = ext[:, at : at + SPAN, :].reshape(-1, chans)
         part = matmul(weights[...], cells).astype(BF16)
-        for k in range(basis):
-            for i in range(rows):
-                at = (k * rows + i) * BLOCK
-                hidden[
-                    i * cols + BLOCK * b : i * cols + BLOCK * (b + 1),
-                    k * chans : (k + 1) * chans,
-                ] = part[at : at + BLOCK]
+        for n, (i, k) in enumerate(groups):
+            hidden[i * cols + at : i * cols + at + BLOCK, k * chans : (k + 1) * chans] = part[
+                n * BLOCK : (n + 1) * BLOCK
+            ]
 
 
 def own_kernel(
@@ -134,7 +131,9 @@
         for i in range(rows):
             at = (k * rows + i) * BLOCK
             own_weights[at : at + BLOCK, :] = staircase(own_line[i : i + 1], BLOCK)
-            halo_weights[at : at + BLOCK, :] = staircase(halo_line[i : i + 1], BLOCK)
+            side, at = i // HALO, (k * HALO + i % HALO) * BLOCK
+            reached = halo_line[i : i + 1, side * HALO * SPAN : (side + 1) * HALO * SPAN]
+            halo_weights[side, at : at + BLOCK, :] = staircase(reached, BLOCK)
 
     copies[4].wait()
     pad = jnp.zeros((ext.shape[1] - cols - 2 * reach, chans), BF16)
@@ -142,9 +141,8 @@
         ext[r] = jnp.concatenate(
             [other[r, cols - reach :], fields[r], other[r, :reach], pad], axis=0
         )
-    window_products(
-        own_weights, ext, hidden, range(cols // BLOCK), rows, basis, cols, chans
-    )
+    groups = [(i, k) for k in range(basis) for i in range(rows)]
+    window_products(own_weights, ext, hidden, groups, cols, chans)
     copies[5].wait()
     copies[6].wait()
     half = rows // 2
@@ -195,27 +193,52 @@
             acc[:, at, :] = acc[:, at, :] + matmul(weights, cells).reshape(rows, BLOCK, chans)
 
 
-def halo_kernel(
-    second_in, first_in, second_edges, first_edges, weights, acc, mix, out, ext, hidden,
-):
-    rows, cols, chans = out.shape
+def side_rows(side, halo, edges, weights, acc, mix, ext, hidden, present, result):
+    half, cols, chans = result.shape
     basis = mix.shape[0] // chans
-    reach = first_edges.shape[1] // 2
-    is_first = lax.axis_index("lon") == 0
-    pad = jnp.zeros((ext.shape[1] - cols - 2 * reach, chans), BF16)
-    for s in range(2 * HALO):
-        p = s % HALO
-        by = (first_in, second_in) if s < HALO else (second_in, first_in)
-        body = jnp.where(is_first, by[0][p], by[1][p])
-        by = (first_edges, second_edges) if s < HALO else (second_edges, first_edges)
-        edge = jnp.where(is_first, by[0][p], by[1][p])
-        ext[s] = jnp.concatenate([edge[reach:], body, edge[:reach], pad], axis=0)
-    window_products(weights, ext, hidden, range(cols // BLOCK), rows, basis, cols, chans)
-    half = rows // 2
-    for n in range(2):
-        total = matmul(hidden[n * half * cols : (n + 1) * half * cols], mix[...])
-        at = slice(n * half, (n + 1) * half)
-        out[at] = (total.reshape(half, cols, chans) + acc[at]).astype(BF16)
+    reach = edges.shape[1] // 2
+    rows = pl.ds(side * half, half)
+
+    @pl.when(present)
+    def arrived():
+        pad = jnp.zeros((ext.shape[1] - cols - 2 * reach, chans), BF16)
+        for p in range(HALO):
+            edge = edges[p]
+            ext[p] = jnp.concatenate([edge[reach:], halo[p], edge[:reach], pad], axis=0)
+        groups = [(i, k) for k in range(basis) for i in range(half)]
+        window_products(weights.at[side], ext, hidden, groups, cols, chans)
+        total = matmul(hidden[...], mix[...]).reshape(half, cols, chans)
+        result[...] = (total + acc[rows]).astype(BF16)
+
+    @pl.when(jnp.logical_not(present))
+    def absent():
+        result[...] = acc[rows].astype(BF16)
+
+
+def from_side(which):
+    core = lax.axis_index("lon")
+    side = 1 - core if which == 0 else core
+    lat_pos = lax.axis_index("lat")
+    last = lax.axis_size("lat") - 1
+    present = jnp.where(side == 0, lat_pos != 0, lat_pos != last)
+    return side, present
+
+
+def early_kernel(halo, edges, weights, acc, mix, result, ext, hidden):
+    side, present = from_side(0)
+    side_rows(side, halo, edges, weights, acc, mix, ext, hidden, present, result)
+
+
+def late_kernel(early, halo, edges, weights, acc, mix, out, ext, hidden, result, sems):
+    half = result.shape[0]
+    side, present = from_side(1)
+    first = pltpu.make_async_copy(early, out.at[pl.ds((1 - side) * half, half)], sems.at[0])
+    first.start()
+    side_rows(side, halo, edges, weights, acc, mix, ext, hidden, present, result)
+    second = pltpu.make_async_copy(result, out.at[pl.ds(side * half, half)], sems.at[1])
+    second.start()
+    first.wait()
+    second.wait()
 
 
 def shards(fields, lon_taps, lat_taps, cycle_taps, band_start, band_width, mixing):
@@ -248,7 +271,7 @@
         own_kernel,
         out_shape=(
             sds((rows, cols, chans), F32),
-            sds((group, rows * SPAN), BF16),
+            sds((2, group // 2, HALO * SPAN), BF16),
             sds((basis * chans, chans), BF16),
         ),
         in_specs=[hbm] * 7 + [vmem],
@@ -287,21 +310,39 @@
         other,
     )
 
-    second, first, second_edges, first_edges, acc = lax.optimization_barrier(
-        (second, first, second_edges, first_edges, acc)
-    )
+    half = rows // 2
+    scratch = [
+        pltpu.VMEM((HALO, ext_cols, chans), BF16),
+        pltpu.VMEM((half * cols, basis * chans), BF16),
+    ]
+    limit = pltpu.CompilerParams(vmem_limit_bytes=32 * 1024 * 1024)
+    second, second_edges, acc = lax.optimization_barrier((second, second_edges, acc))
+    early = pl.pallas_call(
+        early_kernel,
+        out_shape=sds((half, cols, chans), BF16),
+        in_specs=[vmem] * 5,
+        out_specs=vmem,
+        scratch_shapes=scratch,
+        compiler_params=limit,
+        cost_estimate=pl.CostEstimate(
+            flops=300_000_000, bytes_accessed=1_000_000, transcendentals=0
+        ),
+        name="early_side",
+    )(second, second_edges, halo_weights, acc, mix)
+    first, first_edges, early = lax.optimization_barrier((first, first_edges, early))
     return pl.pallas_call(
-        halo_kernel,
+        late_kernel,
         out_shape=sds((rows, cols, chans), BF16),
-        in_specs=[vmem] * 7,
-        out_specs=vmem,
+        in_specs=[vmem] * 6,
+        out_specs=hbm,
         scratch_shapes=[
-            pltpu.VMEM((rows, ext_cols, chans), BF16),
-            pltpu.VMEM((rows * cols, basis * chans), BF16),
+            *scratch,
+            pltpu.VMEM((half, cols, chans), BF16),
+            pltpu.SemaphoreType.DMA((2,)),
         ],
-        compiler_params=pltpu.CompilerParams(vmem_limit_bytes=32 * 1024 * 1024),
-        name="halo_rows",
-    )(second, first, second_edges, first_edges, halo_weights, acc, mix)
+        compiler_params=limit,
+        name="late_side",
+    )(early, first, first_edges, halo_weights, acc, mix)
 
 
 def solution(mesh):

time: 13.2 us -> 12.6 us (0.955)
  Pallas kernels: 6.16 us -> 5.6 us
    pallas_call x1 -> x2, Pallas kernels: 2.06 us -> 1.51 us  [the longest x1 1.49 us: shards(): pl.pallas_call(late_kernel, out_shape=sds((rows, cols, chans), BF16), in_...]
    ppermute x1, waiting for transfers between devices: 1.23 us -> 0.84 us  [shards(): first = lax.ppermute(jnp.where(core == 0, tail, head), axes, ahead)]
    ppermute x1, waiting for transfers between devices: 0.01 us -> 0.35 us  [shards(): second_edges = lax.ppermute(jnp.where(core == 0, head, tail), axes, back)]
  transfers between devices with their start and end apart: 5 -> 5, of which waited for: 3 -> 4; matrix products, arithmetic and copies ran while one was open for 8% -> 9% of each run, Pallas kernels for 31% -> 33%
where the time goes in v7:
time: 12.6 us; the launch traced here: 12.5 us
  Pallas kernels  5.6 us (44%)
  starting transfers between devices  4.3 us (34%)
  waiting for transfers between devices  1.44 us (11%)
  other arithmetic  1.09 us (9%)
    pallas_call x1, Pallas kernels, shards(): pl.pallas_call(own_kernel, out_shape=(sds((rows, cols, chans), F32), sds(...  4.08 us
    ppermute x1, starting transfers between devices, shards(): second = lax.ppermute(jnp.where(core == 0, head, tail), axes, back)  2.76 us
    pallas_call x1, Pallas kernels, shards(): pl.pallas_call(late_kernel, out_shape=sds((rows, cols, chans), BF16), in_...  1.49 us
    ppermute x1, starting transfers between devices, shards(): second_edges = lax.ppermute(jnp.where(core == 0, head, tail), axes, back)  1.48 us
    select_n x1, other arithmetic, shards(): second = lax.ppermute(jnp.where(core == 0, head, tail), axes, back)  1.07 us
    ppermute x1, waiting for transfers between devices, shards(): first = lax.ppermute(jnp.where(core == 0, tail, head), axes, ahead)  0.84 us
    ppermute x1, waiting for transfers between devices, shards(): second_edges = lax.ppermute(jnp.where(core == 0, head, tail), axes, back)  0.35 us
  transfers between devices with their start and end apart: 5, of which 4 were waited for; matrix products, arithmetic and copies ran while one was open for 9% of the time, Pallas kernels for 33%

profile of v7, /device:TPU:1, one launch (start us, length us, event | category | flops | bytes accessed | tf_op | source)
XLA Modules:
  0.0 12.5 jit_solution(10798617195929211982)
XLA Ops:
  0.0 0.1 collective-permute-start.1
  0.1 1.1 %broadcast_select_fusion = (bf16[4,128,256]{2,1,0:T(8,128)(2,1)S(1)}, bf16[4,128,256]{2,1,0:T(8,128)(2,1)S(1)}) fusion(pred[]{:T(512)S(6)} %eq.2, bf16[8,128,256]{2,1,0:T(8,128)(2,1)} %fields_in.1), kind=kLoop, calls=%fused_computation | loop fusion | flops 262144 | bytes 1048577 | tf_op jit(solution)/shard_map/jit(_where)/select_n | solution.py:258
  1.1 2.8 %collective-permute-start.3 = (bf16[4,128,256]{2,1,0:T(8,128)(2,1)S(1)}, bf16[4,128,256]{2,1,0:T(8,128)(2,1)S(1)}, u32[]{:S(2)}, u32[]{:S(2)}) collective-permute-start(bf16[4,128,256]{2,1,0:T(8,128)(2,1)S(1)} %get-tuple-element.23), channel_id=1, source_target_pairs={{0,4},{4,12},{8,0},{12,20},{16,8},{20,28},{24,16},{28,24},{1,5},{5... | collective-permute-start | bytes 786440 | tf_op jit(solution)/shard_map/ppermute | solution.py:258
  3.9 0.0 collective-permute-start
  3.9 0.0 collective-permute-done.1.other
  3.9 1.5 %collective-permute-start.4 = (bf16[4,8,256]{2,1,0:T(8,128)(2,1)S(1)}, bf16[4,8,256]{2,1,0:T(8,128)(2,1)S(1)}, u32[]{:S(2)}, u32[]{:S(2)}) collective-permute-start(bf16[4,8,256]{2,1,0:T(8,128)(2,1)S(1)} %get-tuple-element.27), channel_id=1, source_target_pairs={{0,4},{4,12},{8,0},{12,20},{16,8},{20,28},{24,16},{28,24},{1,5},{5... | collective-permute-start | bytes 49160 | tf_op jit(solution)/shard_map/ppermute | solution.py:262
  5.4 0.0 collective-permute-start.2
  5.4 4.1 %own_rows.1 = (f32[8,128,256]{2,1,0:T(8,128)S(1)}, bf16[2,256,128]{2,1,0:T(8,128)(2,1)S(1)}, bf16[1024,256]{1,0:T(8,128)(2,1)S(1)}) custom-call(s32[8]{0:T(128)} %start_in.1, s32[8]{0:T(128)} %width_in.1, f32[9,4,32]{2,1,0:T(4,128)} %bitcast.4, bf16[6,4,8]{2,1,0:T(4,128)(2,1)} %bitcast.5, bf16[8,128,256]{2,1,0:T(8,128)(2,1)} %fields_in.1, ...), custom_call_target="tpu_custom_call" | custom-call | flops 2000000000 | bytes 6000000 | tf_op jit(solution)/shard_map/own_rows/pallas_call | solution.py:270
  9.5 0.1 collective-permute-done.3.halo
  9.6 0.4 %collective-permute-done.4.edges = bf16[4,8,256]{2,1,0:T(8,128)(2,1)S(1)} collective-permute-done((bf16[4,8,256]{2,1,0:T(8,128)(2,1)S(1)}, bf16[4,8,256]{2,1,0:T(8,128)(2,1)S(1)}, u32[]{:S(2)}, u32[]{:S(2)}) %collective-permute-start.4) | collective-permute-done | bytes 16416 | tf_op jit(solution)/shard_map/ppermute | solution.py:262
  10.0 0.8 %collective-permute-done.halo = bf16[4,128,256]{2,1,0:T(8,128)(2,1)S(1)} collective-permute-done((bf16[4,128,256]{2,1,0:T(8,128)(2,1)S(1)}, bf16[4,128,256]{2,1,0:T(8,128)(2,1)S(1)}, u32[]{:S(2)}, u32[]{:S(2)}) %collective-permute-start) | collective-permute-done | bytes 262176 | tf_op jit(solution)/shard_map/ppermute | solution.py:259
  10.8 0.2 %collective-permute-done.2.edges = bf16[4,8,256]{2,1,0:T(8,128)(2,1)S(1)} collective-permute-done((bf16[4,8,256]{2,1,0:T(8,128)(2,1)S(1)}, bf16[4,8,256]{2,1,0:T(8,128)(2,1)S(1)}, u32[]{:S(2)}, u32[]{:S(2)}) %collective-permute-start.2) | collective-permute-done | bytes 16416 | tf_op jit(solution)/shard_map/ppermute | solution.py:263
  11.0 1.5 %late_side.1 = bf16[8,128,256]{2,1,0:T(8,128)(2,1)} custom-call(bf16[4,128,256]{2,1,0:T(8,128)(2,1)S(1)} %early_side.1.early, bf16[4,128,256]{2,1,0:T(8,128)(2,1)S(1)} %collective-permute-done.halo, bf16[4,8,256]{2,1,0:T(8,128)(2,1)S(1)} %collective-permute-done.2.edges, bf16[2,256,128]{2,1,0:T(8,128)(2,1)S(1)} %get-tuple-element.17.weights, ...), custom_call_target="tpu_custom_call" | custom-call | tf_op jit(solution)/shard_map/late_side/pallas_call | solution.py:333
  (3 shorter events, 0.1 us)
Async XLA Ops:
  0.0 3.9 %collective-permute-start.1 = (bf16[8,128,256]{2,1,0:T(8,128)(2,1)}, bf16[8,128,256]{2,1,0:T(8,128)(2,1)S(1)}, u32[]{:S(2)}, u32[]{:S(2)}) collective-permute-start(bf16[8,128,256]{2,1,0:T(8,128)(2,1)} %fields_in.1), channel_id=1, source_target_pairs={{0,4},{4,0},{1,5},{5,1},{2,6},{6,2},{3,7},{7,3},{8,12},{12,8},{9,1... | collective-permute-start | bytes 1572872 | tf_op jit(solution)/shard_map/ppermute | solution.py:256
  1.1 8.5 %collective-permute-start.3 = (bf16[4,128,256]{2,1,0:T(8,128)(2,1)S(1)}, bf16[4,128,256]{2,1,0:T(8,128)(2,1)S(1)}, u32[]{:S(2)}, u32[]{:S(2)}) collective-permute-start(bf16[4,128,256]{2,1,0:T(8,128)(2,1)S(1)} %get-tuple-element.23), channel_id=1, source_target_pairs={{0,4},{4,12},{8,0},{12,20},{16,8},{20,28},{24,16},{28,24},{1,5},{5... | collective-permute-start | bytes 786440 | tf_op jit(solution)/shard_map/ppermute | solution.py:258
  3.9 6.9 %collective-permute-start = (bf16[4,128,256]{2,1,0:T(8,128)(2,1)S(1)}, bf16[4,128,256]{2,1,0:T(8,128)(2,1)S(1)}, u32[]{:S(2)}, u32[]{:S(2)}) collective-permute-start(bf16[4,128,256]{2,1,0:T(8,128)(2,1)S(1)} %get-tuple-element.24), channel_id=1, source_target_pairs={{0,8},{4,0},{8,16},{12,4},{16,24},{20,12},{24,28},{28,20},{1,9},{5... | collective-permute-start | bytes 786440 | tf_op jit(solution)/shard_map/ppermute | solution.py:259
  3.9 6.0 %collective-permute-start.4 = (bf16[4,8,256]{2,1,0:T(8,128)(2,1)S(1)}, bf16[4,8,256]{2,1,0:T(8,128)(2,1)S(1)}, u32[]{:S(2)}, u32[]{:S(2)}) collective-permute-start(bf16[4,8,256]{2,1,0:T(8,128)(2,1)S(1)} %get-tuple-element.27), channel_id=1, source_target_pairs={{0,4},{4,12},{8,0},{12,20},{16,8},{20,28},{24,16},{28,24},{1,5},{5... | collective-permute-start | bytes 49160 | tf_op jit(solution)/shard_map/ppermute | solution.py:262
  5.4 5.6 %collective-permute-start.2 = (bf16[4,8,256]{2,1,0:T(8,128)(2,1)S(1)}, bf16[4,8,256]{2,1,0:T(8,128)(2,1)S(1)}, u32[]{:S(2)}, u32[]{:S(2)}) collective-permute-start(bf16[4,8,256]{2,1,0:T(8,128)(2,1)S(1)} %get-tuple-element.28), channel_id=1, source_target_pairs={{0,8},{4,0},{8,16},{12,4},{16,24},{20,12},{24,28},{28,20},{1,9},{5... | collective-permute-start | bytes 49160 | tf_op jit(solution)/shard_map/ppermute | solution.py:263

commit v8 on v7

--- a/solution.py
+++ b/solution.py
@@ -41,32 +41,25 @@
     return total
 
 
-def window_products(weights, ext, hidden, groups, cols, chans):
-    for at in range(0, cols, BLOCK):
-        cells = ext[:, at : at + SPAN, :].reshape(-1, chans)
-        part = matmul(weights[...], cells).astype(BF16)
-        for n, (i, k) in enumerate(groups):
-            hidden[i * cols + at : i * cols + at + BLOCK, k * chans : (k + 1) * chans] = part[
-                n * BLOCK : (n + 1) * BLOCK
-            ]
-
-
-def own_kernel(
-    start_in, width_in, lon_in, lat_in, fields_in, cycle_in, mixing_in, other,
-    acc, halo_weights, mix,
-    start, width, lon, lat, fields, cycle_taps, lon_wide, lat_wide, own_weights, ext, hidden,
-    turned, cycle_rows, mixed_rows, sems,
+def window_products(weights, cells, hidden, groups, width, offset, chans):
+    part = matmul(weights[...], cells.reshape(-1, chans)).astype(BF16)
+    for n, (i, k) in enumerate(groups):
+        at = i * width + offset
+        hidden[at : at + BLOCK, k * chans : (k + 1) * chans] = part[n * BLOCK : (n + 1) * BLOCK]
+
+
+def weight_kernel(
+    start_in, width_in, lon_in, lat_in, fields_in, cycle_in, mixing_in,
+    halo_weights, own_weights, polar_weights, cycle_taps, fields, mix,
+    start, width, lon, lat, lon_wide, lat_wide, sems,
 ):
     rows, cols, chans = fields.shape
     taps, basis, row_total = lon.shape
     band = lat.shape[0]
-    reach = taps // 2
     polar = cycle_taps.shape[1] // 2
-    cycle = cycle_taps.shape[2]
     lat_pos = lax.axis_index("lat")
     base = lat_pos * rows
     at_top = base == 0
-    at_bottom = base == row_total - rows
 
     copies = []
     for n, (source, target) in enumerate(
@@ -135,27 +128,35 @@
             reached = halo_line[i : i + 1, side * HALO * SPAN : (side + 1) * HALO * SPAN]
             halo_weights[side, at : at + BLOCK, :] = staircase(reached, BLOCK)
 
-    copies[4].wait()
-    pad = jnp.zeros((ext.shape[1] - cols - 2 * reach, chans), BF16)
-    for r in range(rows):
-        ext[r] = jnp.concatenate(
-            [other[r, cols - reach :], fields[r], other[r, :reach], pad], axis=0
-        )
-    groups = [(i, k) for k in range(basis) for i in range(rows)]
-    window_products(own_weights, ext, hidden, groups, cols, chans)
-    copies[5].wait()
-    copies[6].wait()
-    half = rows // 2
-    for n in range(2):
-        total = matmul(hidden[n * half * cols : (n + 1) * half * cols], mix[...])
-        acc[n * half : (n + 1) * half] = (
-            total.reshape(half, cols, chans)
-            + fields[n * half : (n + 1) * half].astype(F32)
-        )
+    offset = jnp.where(at_top, 0, rows - polar)
+    of_basis = lane // (polar * BLOCK)
+    step = base + offset + lax.rem(lane // BLOCK, polar) - first
+    at_start = lax.rem(lane, BLOCK) == 0
+    terms = []
+    for t in range(band):
+        value = spread[t][0]
+        for k in range(1, basis):
+            value = jnp.where(of_basis == k, spread[t][k], value)
+        terms.append(((step == t) & (count > t) & at_start, value))
+    line = chosen(terms)
+    for i in range(rows):
+        polar_weights[i * BLOCK : (i + 1) * BLOCK, :] = staircase(line[i : i + 1], BLOCK)
+    for n in range(4, 7):
+        copies[n].wait()
+
+
+def own_kernel(own_weights, cycle_taps, fields, mix, acc, turned, ext, hidden):
+    rows, cols, chans = fields.shape
+    basis = mix.shape[0] // chans
+    polar = cycle_taps.shape[1] // 2
+    cycle = cycle_taps.shape[2]
+    near = (SPAN - BLOCK) // 4
+    lat_pos = lax.axis_index("lat")
+    at_top = lat_pos == 0
+    at_bottom = lat_pos == lax.axis_size("lat") - 1
 
     @pl.when(at_top | at_bottom)
-    def polar_part():
-        offset = jnp.where(at_top, 0, rows - polar)
+    def polar_matrices():
         total = lax.broadcasted_iota(jnp.int32, (cycle, cycle), 0) + lax.broadcasted_iota(
             jnp.int32, (cycle, cycle), 1
         )
@@ -166,6 +167,62 @@
                 n = k * 2 * polar + p
                 line = jnp.where(at_top, negated[n : n + 1], negated[n + polar : n + polar + 1])
                 turned[p, k * cols : (k + 1) * cols, :] = staircase(line, cols)
+
+    blank = jnp.zeros((near, chans), BF16)
+    pad = jnp.zeros((ext.shape[1] - cols - near, chans), BF16)
+    for r in range(rows):
+        ext[r] = jnp.concatenate([blank, fields[r], pad], axis=0)
+    groups = [(i, k) for k in range(basis) for i in range(rows)]
+    inner = cols - 2 * BLOCK
+    for at in range(BLOCK, cols - BLOCK, BLOCK):
+        window_products(
+            own_weights, ext[:, at : at + SPAN, :], hidden, groups, inner, at - BLOCK, chans
+        )
+    half = rows // 2
+    for n in range(2):
+        at = slice(n * half, (n + 1) * half)
+        total = matmul(hidden[n * half * inner : (n + 1) * half * inner], mix[...])
+        acc[at, BLOCK : cols - BLOCK, :] = total.reshape(half, inner, chans) + fields[
+            at, BLOCK : cols - BLOCK, :
+        ].astype(F32)
+
+
+def partner_kernel(
+    acc_in, own_weights, polar_weights, turned, fields, mix, other,
+    acc, hidden, cycle_rows, mixed_rows,
+):
+    del acc_in
+    rows, cols, chans = fields.shape
+    polar = turned.shape[0]
+    basis = mix.shape[0] // chans
+    reach = (SPAN - BLOCK) // 4
+    lat_pos = lax.axis_index("lat")
+    at_top = lat_pos == 0
+    at_bottom = lat_pos == lax.axis_size("lat") - 1
+    groups = [(i, k) for k in range(basis) for i in range(rows)]
+    left, right = [], []
+    pad = jnp.zeros((SPAN - BLOCK - 2 * reach, chans), BF16)
+    for r in range(rows):
+        left.append(
+            jnp.concatenate([other[r, cols - reach :], fields[r, : SPAN - reach]], axis=0)
+        )
+        right.append(
+            jnp.concatenate(
+                [fields[r, cols - BLOCK - reach :], other[r, :reach], pad], axis=0
+            )
+        )
+    for n, cells in enumerate((left, right)):
+        window_products(
+            own_weights, jnp.concatenate(cells, axis=0), hidden, groups, 2 * BLOCK, n * BLOCK,
+            chans,
+        )
+    total = matmul(hidden[...], mix[...]).reshape(rows, 2 * BLOCK, chans)
+    for n, at in enumerate((slice(0, BLOCK), slice(cols - BLOCK, cols))):
+        acc[:, at, :] = total[:, n * BLOCK : (n + 1) * BLOCK] + fields[:, at, :].astype(F32)
+
+    @pl.when(at_top | at_bottom)
+    def polar_part():
+        offset = jnp.where(at_top, 0, rows - polar)
         for p in range(polar):
             whole = jnp.concatenate([fields[offset + p], other[offset + p]], axis=0)
             part = matmul(turned[p], whole).astype(BF16)
@@ -174,23 +231,12 @@
         for k in range(basis):
             part = matmul(cycle_rows[k], mix[k * chans : (k + 1) * chans, :]).astype(BF16)
             mixed_rows[k * polar : (k + 1) * polar] = part.reshape(polar, cols, chans)
-        of_basis = lane // (polar * BLOCK)
-        step = base + offset + lax.rem(lane // BLOCK, polar) - first
-        at_start = lax.rem(lane, BLOCK) == 0
-        terms = []
-        for t in range(band):
-            value = spread[t][0]
-            for k in range(1, basis):
-                value = jnp.where(of_basis == k, spread[t][k], value)
-            terms.append(((step == t) & (count > t) & at_start, value))
-        line = chosen(terms)
-        weights = jnp.concatenate(
-            [staircase(line[i : i + 1], BLOCK) for i in range(rows)], axis=0
-        )
         for b in range(cols // BLOCK):
             at = slice(BLOCK * b, BLOCK * (b + 1))
             cells = mixed_rows[:, at, :].reshape(-1, chans)
-            acc[:, at, :] = acc[:, at, :] + matmul(weights, cells).reshape(rows, BLOCK, chans)
+            acc[:, at, :] = acc[:, at, :] + matmul(polar_weights[...], cells).reshape(
+                rows, BLOCK, chans
+            )
 
 
 def side_rows(side, halo, edges, weights, acc, mix, ext, hidden, present, result):
@@ -206,7 +252,10 @@
             edge = edges[p]
             ext[p] = jnp.concatenate([edge[reach:], halo[p], edge[:reach], pad], axis=0)
         groups = [(i, k) for k in range(basis) for i in range(half)]
-        window_products(weights.at[side], ext, hidden, groups, cols, chans)
+        for at in range(0, cols, BLOCK):
+            window_products(
+                weights.at[side], ext[:, at : at + SPAN, :], hidden, groups, cols, at, chans
+            )
         total = matmul(hidden[...], mix[...]).reshape(half, cols, chans)
         result[...] = (total + acc[rows]).astype(BF16)
 
@@ -252,52 +301,47 @@
     core = lax.axis_index("lon")
     axes = ("lat", "lon")
     assert cycle == 2 * cols and rows == 2 * HALO and basis * polar * BLOCK == rows * SPAN
+    assert reach == (SPAN - BLOCK) // 4
     ahead, back = ring(lat_count, 1), ring(lat_count, -1)
+    head, tail = fields[:HALO], fields[rows - HALO :]
+    down = jnp.where(core == 0, head, tail)
+    up = jnp.where(core == 0, tail, head)
     other = lax.ppermute(fields, "lon", SWAP)
-    head, tail = fields[:HALO], fields[rows - HALO :]
-    second = lax.ppermute(jnp.where(core == 0, head, tail), axes, back)
-    first = lax.ppermute(jnp.where(core == 0, tail, head), axes, ahead)
-    edges = jnp.concatenate([other[:, :reach], other[:, cols - reach :]], axis=1)
-    head, tail = edges[:HALO], edges[rows - HALO :]
-    second_edges = lax.ppermute(jnp.where(core == 0, head, tail), axes, back)
-    first_edges = lax.ppermute(jnp.where(core == 0, tail, head), axes, ahead)
+    second = lax.ppermute(down, axes, back)
+    down, band_start = lax.optimization_barrier((down, band_start))
 
     vmem = pl.BlockSpec(memory_space=pltpu.VMEM)
     hbm = pl.BlockSpec(memory_space=pltpu.HBM)
     sds = jax.ShapeDtypeStruct
     group = basis * rows * BLOCK
     ext_cols = cols + SPAN - BLOCK
-    acc, halo_weights, mix = pl.pallas_call(
-        own_kernel,
+    limit = pltpu.CompilerParams(vmem_limit_bytes=32 * 1024 * 1024)
+    halo_weights, own_weights, polar_weights, turns, whole, mix = pl.pallas_call(
+        weight_kernel,
         out_shape=(
-            sds((rows, cols, chans), F32),
             sds((2, group // 2, HALO * SPAN), BF16),
+            sds((group, rows * SPAN), BF16),
+            sds((rows * BLOCK, rows * SPAN), BF16),
+            sds((basis, 2 * polar, cycle), BF16),
+            sds((rows, cols, chans), BF16),
             sds((basis * chans, chans), BF16),
         ),
-        in_specs=[hbm] * 7 + [vmem],
-        out_specs=(vmem, vmem, vmem),
+        in_specs=[hbm] * 7,
+        out_specs=[vmem] * 6,
         scratch_shapes=[
             pltpu.SMEM((rows,), jnp.int32),
             pltpu.SMEM((rows,), jnp.int32),
             pltpu.VMEM((taps, basis, row_total), F32),
             pltpu.VMEM((band, basis, rows), BF16),
-            pltpu.VMEM((rows, cols, chans), BF16),
-            pltpu.VMEM((basis, 2 * polar, cycle), BF16),
             pltpu.VMEM((128, -(-row_total // 128) * 128), F32),
             pltpu.VMEM((128, 128), F32),
-            pltpu.VMEM((group, rows * SPAN), BF16),
-            pltpu.VMEM((rows, ext_cols, chans), BF16),
-            pltpu.VMEM((rows * cols, basis * chans), BF16),
-            pltpu.VMEM((polar, basis * cols, cycle), BF16),
-            pltpu.VMEM((basis, polar * cols, chans), BF16),
-            pltpu.VMEM((basis * polar, cols, chans), BF16),
             pltpu.SemaphoreType.DMA((7,)),
         ],
-        compiler_params=pltpu.CompilerParams(vmem_limit_bytes=32 * 1024 * 1024),
+        compiler_params=limit,
         cost_estimate=pl.CostEstimate(
-            flops=2_000_000_000, bytes_accessed=6_000_000, transcendentals=0
-        ),
-        name="own_rows",
+            flops=100_000, bytes_accessed=1_000, transcendentals=0
+        ),
+        name="filter_weights",
     )(
         *(
             pltpu.with_memory_space_constraint(x, pltpu.HBM)
@@ -307,8 +351,49 @@
                 mixing.reshape(basis * chans, chans),
             )
         ),
-        other,
     )
+    edges = jnp.concatenate([other[:, :reach], other[:, cols - reach :]], axis=1)
+    head, tail = edges[:HALO], edges[rows - HALO :]
+    second_edges = lax.ppermute(jnp.where(core == 0, head, tail), axes, back)
+    up, own_weights = lax.optimization_barrier((up, own_weights))
+    first = lax.ppermute(up, axes, ahead)
+    first_edges = lax.ppermute(jnp.where(core == 0, tail, head), axes, ahead)
+    acc, turned = pl.pallas_call(
+        own_kernel,
+        out_shape=(
+            sds((rows, cols, chans), F32),
+            sds((polar, basis * cols, cycle), BF16),
+        ),
+        in_specs=[vmem] * 4,
+        out_specs=(vmem, vmem),
+        scratch_shapes=[
+            pltpu.VMEM((rows, ext_cols, chans), BF16),
+            pltpu.VMEM((rows * (cols - 2 * BLOCK), basis * chans), BF16),
+        ],
+        compiler_params=limit,
+        cost_estimate=pl.CostEstimate(
+            flops=100_000, bytes_accessed=1_000, transcendentals=0
+        ),
+        name="own_rows",
+    )(own_weights, turns, whole, mix)
+
+    acc = pl.pallas_call(
+        partner_kernel,
+        out_shape=sds((rows, cols, chans), F32),
+        in_specs=[vmem] * 7,
+        out_specs=vmem,
+        input_output_aliases={0: 0},
+        scratch_shapes=[
+            pltpu.VMEM((rows * 2 * BLOCK, basis * chans), BF16),
+            pltpu.VMEM((basis, polar * cols, chans), BF16),
+            pltpu.VMEM((basis * polar, cols, chans), BF16),
+        ],
+        compiler_params=limit,
+        cost_estimate=pl.CostEstimate(
+            flops=100_000, bytes_accessed=1_000, transcendentals=0
+        ),
+        name="partner_columns",
+    )(acc, own_weights, polar_weights, turned, whole, mix, other)
 
     half = rows // 2
     scratch = [

time: 12.6 us -> 12.6 us (level)
  waiting for transfers between devices: 1.44 us -> 0.84 us
  Pallas kernels: 5.6 us -> 6.14 us
    pallas_call x0 -> x2, Pallas kernels: none -> 3.13 us  [the longest x1 1.66 us: shards(): pl.pallas_call(partner_kernel, out_shape=sds((rows, cols, chans), F32), i...]
    pallas_call x1, Pallas kernels: 4.08 us -> 1.47 us  [shards(): pl.pallas_call(own_kernel, out_shape=(sds((rows, cols, chans), F32), sds(...]
    ppermute x1, waiting for transfers between devices: 0.35 us -> 0.01 us  [shards(): second_edges = lax.ppermute(jnp.where(core == 0, head, tail), axes, back)]
    ppermute x2, waiting for transfers between devices: 0.91 us -> 0.64 us  [the longest x1 0.64 us: shards(): first = lax.ppermute(up, axes, ahead)]
  transfers between devices with their start and end apart: 5 -> 5, of which waited for: 4 -> 2; matrix products, arithmetic and copies ran while one was open for 9% -> 9% of each run, Pallas kernels for 33% -> 37%
where the time goes in v8:
time: 12.6 us; the launch traced here: 12.5 us
  Pallas kernels  6.14 us (49%)
  starting transfers between devices  4.32 us (34%)
  other arithmetic  1.09 us (9%)
  waiting for transfers between devices  0.84 us (7%)
    ppermute x1, starting transfers between devices, shards(): second = lax.ppermute(down, axes, back)  2.76 us
    pallas_call x1, Pallas kernels, shards(): pl.pallas_call(partner_kernel, out_shape=sds((rows, cols, chans), F32), i...  1.66 us
    pallas_call x1, Pallas kernels, shards(): pl.pallas_call(late_kernel, out_shape=sds((rows, cols, chans), BF16), in_...  1.49 us
    pallas_call x1, Pallas kernels, shards(): pl.pallas_call(own_kernel, out_shape=(sds((rows, cols, chans), F32), sds(...  1.47 us
    pallas_call x1, Pallas kernels, shards(): pl.pallas_call(weight_kernel, out_shape=(sds((2, group // 2, HALO * SPAN)...  1.47 us
    ppermute x1, starting transfers between devices, shards(): second_edges = lax.ppermute(jnp.where(core == 0, head, tail), axes, back)  1.46 us
    select_n x1, other arithmetic, shards(): down = jnp.where(core == 0, head, tail)  1.07 us
    ppermute x1, waiting for transfers between devices, shards(): first = lax.ppermute(up, axes, ahead)  0.64 us
  transfers between devices with their start and end apart: 5, of which 2 were waited for; matrix products, arithmetic and copies ran while one was open for 9% of the time, Pallas kernels for 37%

profile of v8, /device:TPU:1, one launch (start us, length us, event | category | flops | bytes accessed | tf_op | source)
XLA Modules:
  0.0 12.5 jit_solution(15615558619845904724)
XLA Ops:
  0.0 0.1 collective-permute-start.1
  0.1 1.1 %broadcast_select_fusion = (bf16[4,128,256]{2,1,0:T(8,128)(2,1)S(1)}, bf16[4,128,256]{2,1,0:T(8,128)(2,1)S(1)}) fusion(pred[]{:T(512)S(6)} %eq.2, bf16[8,128,256]{2,1,0:T(8,128)(2,1)} %fields_in.1), kind=kLoop, calls=%fused_computation | loop fusion | flops 262144 | bytes 1048577 | tf_op jit(solution)/shard_map/jit(_where)/select_n | solution.py:307
  1.1 2.8 %collective-permute-start.3 = (bf16[4,128,256]{2,1,0:T(8,128)(2,1)S(1)}, bf16[4,128,256]{2,1,0:T(8,128)(2,1)S(1)}, u32[]{:S(2)}, u32[]{:S(2)}) collective-permute-start(bf16[4,128,256]{2,1,0:T(8,128)(2,1)S(1)} %get-tuple-element.41), channel_id=1, source_target_pairs={{0,4},{4,12},{8,0},{12,20},{16,8},{20,28},{24,16},{28,24},{1,5},{5... | collective-permute-start | bytes 786440 | tf_op jit(solution)/shard_map/ppermute | solution.py:310
  3.9 1.5 %filter_weights.1 = (bf16[2,256,128]{2,1,0:T(8,128)(2,1)S(1)}, bf16[512,256]{1,0:T(8,128)(2,1)S(1)}, bf16[128,256]{1,0:T(8,128)(2,1)S(1)}, bf16[4,8,256]{2,1,0:T...) custom-call(s32[8]{0:T(128)} %start_in, s32[8]{0:T(128)} %width_in.1, ...), custom_call_target="tpu_custom_call" | custom-call | flops 100000 | bytes 1000 | tf_op jit(solution)/shard_map/filter_weights/pallas_call | solution.py:319
  5.4 0.0 collective-permute-start
  5.4 0.0 collective-permute-done.1.other
  5.5 1.5 %collective-permute-start.4 = (bf16[4,8,256]{2,1,0:T(8,128)(2,1)S(1)}, bf16[4,8,256]{2,1,0:T(8,128)(2,1)S(1)}, u32[]{:S(2)}, u32[]{:S(2)}) collective-permute-start(bf16[4,8,256]{2,1,0:T(8,128)(2,1)S(1)} %get-tuple-element.43), channel_id=1, source_target_pairs={{0,4},{4,12},{8,0},{12,20},{16,8},{20,28},{24,16},{28,24},{1,5},{5... | collective-permute-start | bytes 49160 | tf_op jit(solution)/shard_map/ppermute | solution.py:357
  6.9 1.5 %own_rows.1 = (f32[8,128,256]{2,1,0:T(8,128)S(1)}, bf16[4,512,256]{2,1,0:T(8,128)(2,1)S(1)}) custom-call(bf16[512,256]{1,0:T(8,128)(2,1)S(1)} %get-tuple-element.25.own_weights, bf16[4,8,256]{2,1,0:T(8,128)(2,1)S(1)} %get-tuple-element.26.cycle_taps, bf16[8,128,256]{2,1,0:T(8,128)(2,1)S(1)} %get-tuple-element.27.fields, ...), custom_call_target="tpu_custom_call" | custom-call | flops 100000 | bytes 1000 | tf_op jit(solution)/shard_map/own_rows/pallas_call | solution.py:361
  8.4 0.0 collective-permute-start.2
  8.4 1.7 %partner_columns.1.acc = f32[8,128,256]{2,1,0:T(8,128)S(1)} custom-call(f32[8,128,256]{2,1,0:T(8,128)S(1)} %get-tuple-element.29.acc_in, bf16[512,256]{1,0:T(8,128)(2,1)S(1)} %get-tuple-element.25.own_weights, bf16[128,256]{1,0:T(8,128)(2,1)S(1)} %get-tuple-element.30.polar_weights, ...), custom_call_target="tpu_custom_call", output_to_operand_aliasing={{}: (0, {})} | custom-call | flops 100000 | bytes 1000 | tf_op jit(solution)/shard_map/partner_columns/pallas_call | solution.py:380
  10.1 0.0 collective-permute-done.3.halo
  10.1 0.0 collective-permute-done.4.edges
  10.2 0.6 %collective-permute-done.halo = bf16[4,128,256]{2,1,0:T(8,128)(2,1)S(1)} collective-permute-done((bf16[4,128,256]{2,1,0:T(8,128)(2,1)S(1)}, bf16[4,128,256]{2,1,0:T(8,128)(2,1)S(1)}, u32[]{:S(2)}, u32[]{:S(2)}) %collective-permute-start) | collective-permute-done | bytes 262176 | tf_op jit(solution)/shard_map/ppermute | solution.py:359
  10.8 0.2 %collective-permute-done.2.edges = bf16[4,8,256]{2,1,0:T(8,128)(2,1)S(1)} collective-permute-done((bf16[4,8,256]{2,1,0:T(8,128)(2,1)S(1)}, bf16[4,8,256]{2,1,0:T(8,128)(2,1)S(1)}, u32[]{:S(2)}, u32[]{:S(2)}) %collective-permute-start.2) | collective-permute-done | bytes 16416 | tf_op jit(solution)/shard_map/ppermute | solution.py:360
  11.0 1.5 %late_side.1 = bf16[8,128,256]{2,1,0:T(8,128)(2,1)} custom-call(bf16[4,128,256]{2,1,0:T(8,128)(2,1)S(1)} %early_side.1.early, bf16[4,128,256]{2,1,0:T(8,128)(2,1)S(1)} %collective-permute-done.halo, bf16[4,8,256]{2,1,0:T(8,128)(2,1)S(1)} %collective-permute-done.2.edges, bf16[2,256,128]{2,1,0:T(8,128)(2,1)S(1)} %get-tuple-element.34.weights, ...), custom_call_target="tpu_custom_call" | custom-call | tf_op jit(solution)/shard_map/late_side/pallas_call | solution.py:418
  (3 shorter events, 0.1 us)
Async XLA Ops:
  0.0 5.4 %collective-permute-start.1 = (bf16[8,128,256]{2,1,0:T(8,128)(2,1)}, bf16[8,128,256]{2,1,0:T(8,128)(2,1)S(1)}, u32[]{:S(2)}, u32[]{:S(2)}) collective-permute-start(bf16[8,128,256]{2,1,0:T(8,128)(2,1)} %fields_in.1), channel_id=1, source_target_pairs={{0,4},{4,0},{1,5},{5,1},{2,6},{6,2},{3,7},{7,3},{8,12},{12,8},{9,1... | collective-permute-start | bytes 1572872 | tf_op jit(solution)/shard_map/ppermute | solution.py:309
  1.1 9.0 %collective-permute-start.3 = (bf16[4,128,256]{2,1,0:T(8,128)(2,1)S(1)}, bf16[4,128,256]{2,1,0:T(8,128)(2,1)S(1)}, u32[]{:S(2)}, u32[]{:S(2)}) collective-permute-start(bf16[4,128,256]{2,1,0:T(8,128)(2,1)S(1)} %get-tuple-element.41), channel_id=1, source_target_pairs={{0,4},{4,12},{8,0},{12,20},{16,8},{20,28},{24,16},{28,24},{1,5},{5... | collective-permute-start | bytes 786440 | tf_op jit(solution)/shard_map/ppermute | solution.py:310
  5.4 5.5 %collective-permute-start = (bf16[4,128,256]{2,1,0:T(8,128)(2,1)S(1)}, bf16[4,128,256]{2,1,0:T(8,128)(2,1)S(1)}, u32[]{:S(2)}, u32[]{:S(2)}) collective-permute-start(bf16[4,128,256]{2,1,0:T(8,128)(2,1)S(1)} %get-tuple-element.24), channel_id=1, source_target_pairs={{0,8},{4,0},{8,16},{12,4},{16,24},{20,12},{24,28},{28,20},{1,9},{5... | collective-permute-start | bytes 786440 | tf_op jit(solution)/shard_map/ppermute | solution.py:359
  5.5 4.7 %collective-permute-start.4 = (bf16[4,8,256]{2,1,0:T(8,128)(2,1)S(1)}, bf16[4,8,256]{2,1,0:T(8,128)(2,1)S(1)}, u32[]{:S(2)}, u32[]{:S(2)}) collective-permute-start(bf16[4,8,256]{2,1,0:T(8,128)(2,1)S(1)} %get-tuple-element.43), channel_id=1, source_target_pairs={{0,4},{4,12},{8,0},{12,20},{16,8},{20,28},{24,16},{28,24},{1,5},{5... | collective-permute-start | bytes 49160 | tf_op jit(solution)/shard_map/ppermute | solution.py:357
  8.4 2.6 %collective-permute-start.2 = (bf16[4,8,256]{2,1,0:T(8,128)(2,1)S(1)}, bf16[4,8,256]{2,1,0:T(8,128)(2,1)S(1)}, u32[]{:S(2)}, u32[]{:S(2)}) collective-permute-start(bf16[4,8,256]{2,1,0:T(8,128)(2,1)S(1)} %get-tuple-element.44), channel_id=1, source_target_pairs={{0,8},{4,0},{8,16},{12,4},{16,24},{20,12},{24,28},{28,20},{1,9},{5... | collective-permute-start | bytes 49160 | tf_op jit(solution)/shard_map/ppermute | solution.py:360

commit v9 on v8

--- a/solution.py
+++ b/solution.py
@@ -48,32 +48,56 @@
         hidden[at : at + BLOCK, k * chans : (k + 1) * chans] = part[n * BLOCK : (n + 1) * BLOCK]
 
 
-def weight_kernel(
-    start_in, width_in, lon_in, lat_in, fields_in, cycle_in, mixing_in,
-    halo_weights, own_weights, polar_weights, cycle_taps, fields, mix,
-    start, width, lon, lat, lon_wide, lat_wide, sems,
+def polar_matrices(cycle_taps, turned, at_top):
+    basis, twice, cycle = cycle_taps.shape
+    polar = twice // 2
+    cols = turned.shape[1] // basis
+    total = lax.broadcasted_iota(jnp.int32, (cycle, cycle), 0) + lax.broadcasted_iota(
+        jnp.int32, (cycle, cycle), 1
+    )
+    turn = jnp.where((total == 0) | (total == cycle), 1.0, 0.0).astype(BF16)
+    negated = matmul(cycle_taps[...].reshape(-1, cycle), turn)
+    for p in range(polar):
+        for k in range(basis):
+            n = k * twice + (p if at_top else p + polar)
+            turned[p, k * cols : (k + 1) * cols, :] = staircase(negated[n : n + 1], cols)
+
+
+def fetch_kernel(
+    start_in, width_in, lon_in, lat_in, cycle_in, fields_in, mixing_in,
+    start, width, lon, lat, cycle_taps, fields, mix, turned, sems,
 ):
-    rows, cols, chans = fields.shape
-    taps, basis, row_total = lon.shape
-    band = lat.shape[0]
-    polar = cycle_taps.shape[1] // 2
-    lat_pos = lax.axis_index("lat")
-    base = lat_pos * rows
-    at_top = base == 0
-
     copies = []
     for n, (source, target) in enumerate(
         [
-            (lon_in, lon), (lat_in, lat), (start_in, start), (width_in, width),
-            (fields_in, fields), (cycle_in, cycle_taps), (mixing_in, mix),
+            (cycle_in, cycle_taps), (lon_in, lon), (lat_in, lat), (start_in, start),
+            (width_in, width), (fields_in, fields), (mixing_in, mix),
         ]
     ):
         copies.append(pltpu.make_async_copy(source, target, sems.at[n]))
         copies[-1].start()
+    copies[0].wait()
+
+    @pl.when(lax.axis_index("lat") == 0)
+    def top():
+        polar_matrices(cycle_taps, turned, True)
+
+    for copy in copies[1:]:
+        copy.wait()
+
+
+def weight_kernel(
+    start, width, lon, lat, cycle_taps, halo_weights, own_weights, polar_weights,
+    lon_wide, lat_wide,
+):
+    rows = halo_weights.shape[0] * HALO
+    taps, basis, row_total = lon.shape
+    band = lat.shape[0]
+    polar = cycle_taps.shape[1] // 2
+    base = lax.axis_index("lat") * rows
+    at_top = base == 0
     lon_wide[...] = jnp.zeros_like(lon_wide)
     lat_wide[...] = jnp.zeros_like(lat_wide)
-    for n in range(4):
-        copies[n].wait()
 
     for d in range(taps):
         for k in range(basis):
@@ -94,15 +118,14 @@
 
     for t in range(band):
         lat_wide[t * basis : (t + 1) * basis, 0:rows] = lat[t].astype(F32)
+    at = band * basis
+    lat_wide[at : at + 1, 0:rows] = start[...].reshape(1, rows).astype(F32)
+    lat_wide[at + 1 : at + 2, 0:rows] = width[...].reshape(1, rows).astype(F32)
     lat_cols = jnp.transpose(lat_wide[...])[:rows]
     shape = (rows, rows * SPAN)
     lane = lax.broadcasted_iota(jnp.int32, shape, 1)
-    out_row = lax.broadcasted_iota(jnp.int32, shape, 0)
-    first = jnp.zeros(shape, jnp.int32)
-    count = jnp.zeros(shape, jnp.int32)
-    for i in range(rows):
-        first = jnp.where(out_row == i, start[i], first)
-        count = jnp.where(out_row == i, width[i], count)
+    first = jnp.broadcast_to(lat_cols[:, at : at + 1], shape).astype(jnp.int32)
+    count = jnp.broadcast_to(lat_cols[:, at + 1 : at + 2], shape).astype(jnp.int32)
     spread = [
         [
             jnp.broadcast_to(lat_cols[:, t * basis + k : t * basis + k + 1], shape)
@@ -141,33 +164,12 @@
     line = chosen(terms)
     for i in range(rows):
         polar_weights[i * BLOCK : (i + 1) * BLOCK, :] = staircase(line[i : i + 1], BLOCK)
-    for n in range(4, 7):
-        copies[n].wait()
-
-
-def own_kernel(own_weights, cycle_taps, fields, mix, acc, turned, ext, hidden):
+
+
+def own_kernel(own_weights, fields, mix, acc, ext, hidden):
     rows, cols, chans = fields.shape
     basis = mix.shape[0] // chans
-    polar = cycle_taps.shape[1] // 2
-    cycle = cycle_taps.shape[2]
     near = (SPAN - BLOCK) // 4
-    lat_pos = lax.axis_index("lat")
-    at_top = lat_pos == 0
-    at_bottom = lat_pos == lax.axis_size("lat") - 1
-
-    @pl.when(at_top | at_bottom)
-    def polar_matrices():
-        total = lax.broadcasted_iota(jnp.int32, (cycle, cycle), 0) + lax.broadcasted_iota(
-            jnp.int32, (cycle, cycle), 1
-        )
-        turn = jnp.where((total == 0) | (total == cycle), 1.0, 0.0).astype(BF16)
-        negated = matmul(cycle_taps[...].reshape(-1, cycle), turn)
-        for p in range(polar):
-            for k in range(basis):
-                n = k * 2 * polar + p
-                line = jnp.where(at_top, negated[n : n + 1], negated[n + polar : n + polar + 1])
-                turned[p, k * cols : (k + 1) * cols, :] = staircase(line, cols)
-
     blank = jnp.zeros((near, chans), BF16)
     pad = jnp.zeros((ext.shape[1] - cols - near, chans), BF16)
     for r in range(rows):
@@ -188,10 +190,10 @@
 
 
 def partner_kernel(
-    acc_in, own_weights, polar_weights, turned, fields, mix, other,
-    acc, hidden, cycle_rows, mixed_rows,
+    acc_in, turned_in, own_weights, polar_weights, cycle_taps, fields, mix, other,
+    acc, turned, hidden, cycle_rows, mixed_rows,
 ):
-    del acc_in
+    del acc_in, turned_in
     rows, cols, chans = fields.shape
     polar = turned.shape[0]
     basis = mix.shape[0] // chans
@@ -220,6 +222,10 @@
     for n, at in enumerate((slice(0, BLOCK), slice(cols - BLOCK, cols))):
         acc[:, at, :] = total[:, n * BLOCK : (n + 1) * BLOCK] + fields[:, at, :].astype(F32)
 
+    @pl.when(at_bottom)
+    def bottom():
+        polar_matrices(cycle_taps, turned, False)
+
     @pl.when(at_top | at_bottom)
     def polar_part():
         offset = jnp.where(at_top, 0, rows - polar)
@@ -252,12 +258,17 @@
             edge = edges[p]
             ext[p] = jnp.concatenate([edge[reach:], halo[p], edge[:reach], pad], axis=0)
         groups = [(i, k) for k in range(basis) for i in range(half)]
-        for at in range(0, cols, BLOCK):
-            window_products(
-                weights.at[side], ext[:, at : at + SPAN, :], hidden, groups, cols, at, chans
-            )
-        total = matmul(hidden[...], mix[...]).reshape(half, cols, chans)
-        result[...] = (total + acc[rows]).astype(BF16)
+        wide = cols // 2
+        for n in range(2):
+            for at in range(0, wide, BLOCK):
+                cells = ext[:, n * wide + at : n * wide + at + SPAN, :]
+                window_products(
+                    weights.at[side], cells, hidden.at[n], groups, wide, at, chans
+                )
+        for n in range(2):
+            total = matmul(hidden[n], mix[...]).reshape(half, wide, chans)
+            at = slice(n * wide, (n + 1) * wide)
+            result[:, at, :] = (total + acc[rows, at, :]).astype(BF16)
 
     @pl.when(jnp.logical_not(present))
     def absent():
@@ -316,91 +327,97 @@
     group = basis * rows * BLOCK
     ext_cols = cols + SPAN - BLOCK
     limit = pltpu.CompilerParams(vmem_limit_bytes=32 * 1024 * 1024)
-    halo_weights, own_weights, polar_weights, turns, whole, mix = pl.pallas_call(
+    small = pl.CostEstimate(flops=100_000, bytes_accessed=1_000, transcendentals=0)
+    start, width, lon, lat, turns, whole, mix, turned = pl.pallas_call(
+        fetch_kernel,
+        out_shape=(
+            sds((rows,), jnp.int32),
+            sds((rows,), jnp.int32),
+            sds((taps, basis, row_total), F32),
+            sds((band, basis, rows), BF16),
+            sds((basis, 2 * polar, cycle), BF16),
+            sds((rows, cols, chans), BF16),
+            sds((basis * chans, chans), BF16),
+            sds((polar, basis * cols, cycle), BF16),
+        ),
+        in_specs=[hbm] * 7,
+        out_specs=[vmem] * 8,
+        scratch_shapes=[pltpu.SemaphoreType.DMA((7,))],
+        compiler_params=limit,
+        cost_estimate=small,
+        name="fetch_operands",
+    )(
+        *(
+            pltpu.with_memory_space_constraint(x, pltpu.HBM)
+            for x in (
+                band_start, band_width, jnp.transpose(lon_taps, (2, 1, 0)),
+                jnp.transpose(lat_taps, (2, 1, 0)), cycle_taps, fields,
+                mixing.reshape(basis * chans, chans),
+            )
+        ),
+    )
+    up, start = lax.optimization_barrier((up, start))
+    first = lax.ppermute(up, axes, ahead)
+    halo_weights, own_weights, polar_weights = pl.pallas_call(
         weight_kernel,
         out_shape=(
             sds((2, group // 2, HALO * SPAN), BF16),
             sds((group, rows * SPAN), BF16),
             sds((rows * BLOCK, rows * SPAN), BF16),
-            sds((basis, 2 * polar, cycle), BF16),
-            sds((rows, cols, chans), BF16),
-            sds((basis * chans, chans), BF16),
         ),
-        in_specs=[hbm] * 7,
-        out_specs=[vmem] * 6,
+        in_specs=[vmem] * 5,
+        out_specs=[vmem] * 3,
         scratch_shapes=[
-            pltpu.SMEM((rows,), jnp.int32),
-            pltpu.SMEM((rows,), jnp.int32),
-            pltpu.VMEM((taps, basis, row_total), F32),
-            pltpu.VMEM((band, basis, rows), BF16),
             pltpu.VMEM((128, -(-row_total // 128) * 128), F32),
             pltpu.VMEM((128, 128), F32),
-            pltpu.SemaphoreType.DMA((7,)),
         ],
         compiler_params=limit,
-        cost_estimate=pl.CostEstimate(
-            flops=100_000, bytes_accessed=1_000, transcendentals=0
-        ),
+        cost_estimate=small,
         name="filter_weights",
-    )(
-        *(
-            pltpu.with_memory_space_constraint(x, pltpu.HBM)
-            for x in (
-                band_start, band_width, jnp.transpose(lon_taps, (2, 1, 0)),
-                jnp.transpose(lat_taps, (2, 1, 0)), fields, cycle_taps,
-                mixing.reshape(basis * chans, chans),
-            )
-        ),
-    )
+    )(start, width, lon, lat, turns)
+
     edges = jnp.concatenate([other[:, :reach], other[:, cols - reach :]], axis=1)
     head, tail = edges[:HALO], edges[rows - HALO :]
     second_edges = lax.ppermute(jnp.where(core == 0, head, tail), axes, back)
-    up, own_weights = lax.optimization_barrier((up, own_weights))
-    first = lax.ppermute(up, axes, ahead)
     first_edges = lax.ppermute(jnp.where(core == 0, tail, head), axes, ahead)
-    acc, turned = pl.pallas_call(
+    acc = pl.pallas_call(
         own_kernel,
+        out_shape=sds((rows, cols, chans), F32),
+        in_specs=[vmem] * 3,
+        out_specs=vmem,
+        scratch_shapes=[
+            pltpu.VMEM((rows, ext_cols, chans), BF16),
+            pltpu.VMEM((rows * (cols - 2 * BLOCK), basis * chans), BF16),
+        ],
+        compiler_params=limit,
+        cost_estimate=small,
+        name="own_rows",
+    )(own_weights, whole, mix)
+
+    acc, _ = pl.pallas_call(
+        partner_kernel,
         out_shape=(
             sds((rows, cols, chans), F32),
             sds((polar, basis * cols, cycle), BF16),
         ),
-        in_specs=[vmem] * 4,
+        in_specs=[vmem] * 8,
         out_specs=(vmem, vmem),
-        scratch_shapes=[
-            pltpu.VMEM((rows, ext_cols, chans), BF16),
-            pltpu.VMEM((rows * (cols - 2 * BLOCK), basis * chans), BF16),
-        ],
-        compiler_params=limit,
-        cost_estimate=pl.CostEstimate(
-            flops=100_000, bytes_accessed=1_000, transcendentals=0
-        ),
-        name="own_rows",
-    )(own_weights, turns, whole, mix)
-
-    acc = pl.pallas_call(
-        partner_kernel,
-        out_shape=sds((rows, cols, chans), F32),
-        in_specs=[vmem] * 7,
-        out_specs=vmem,
-        input_output_aliases={0: 0},
+        input_output_aliases={0: 0, 1: 1},
         scratch_shapes=[
             pltpu.VMEM((rows * 2 * BLOCK, basis * chans), BF16),
             pltpu.VMEM((basis, polar * cols, chans), BF16),
             pltpu.VMEM((basis * polar, cols, chans), BF16),
         ],
         compiler_params=limit,
-        cost_estimate=pl.CostEstimate(
-            flops=100_000, bytes_accessed=1_000, transcendentals=0
-        ),
+        cost_estimate=small,
         name="partner_columns",
-    )(acc, own_weights, polar_weights, turned, whole, mix, other)
+    )(acc, turned, own_weights, polar_weights, turns, whole, mix, other)
 
     half = rows // 2
     scratch = [
         pltpu.VMEM((HALO, ext_cols, chans), BF16),
-        pltpu.VMEM((half * cols, basis * chans), BF16),
+        pltpu.VMEM((2, half * cols // 2, basis * chans), BF16),
     ]
-    limit = pltpu.CompilerParams(vmem_limit_bytes=32 * 1024 * 1024)
     second, second_edges, acc = lax.optimization_barrier((second, second_edges, acc))
     early = pl.pallas_call(
         early_kernel,
@@ -409,9 +426,7 @@
         out_specs=vmem,
         scratch_shapes=scratch,
         compiler_params=limit,
-        cost_estimate=pl.CostEstimate(
-            flops=300_000_000, bytes_accessed=1_000_000, transcendentals=0
-        ),
+        cost_estimate=small,
         name="early_side",
     )(second, second_edges, halo_weights, acc, mix)
     first, first_edges, early = lax.optimization_barrier((first, first_edges, early))

time: 12.6 us -> 12.8 us (1.016)
  the two profiles are of different devices: /device:TPU:1 before, /device:TPU:0 now
where the time goes in v9:
time: 12.8 us; the launch traced here: 12.5 us
  Pallas kernels  6.2 us (48%)
  starting transfers between devices  5.13 us (40%)
  other arithmetic  1.09 us (9%)
    ppermute x1, starting transfers between devices, shards(): first = lax.ppermute(up, axes, ahead)  2.55 us
    ppermute x1, starting transfers between devices, shards(): first_edges = lax.ppermute(jnp.where(core == 0, tail, head), axes, ahead)  1.8 us
    pallas_call x1, Pallas kernels, shards(): pl.pallas_call(partner_kernel, out_shape=(sds((rows, cols, chans), F32),...  1.66 us
    pallas_call x1, Pallas kernels, shards(): pl.pallas_call(fetch_kernel, out_shape=(sds((rows,), jnp.int32), sds((row...  1.34 us
    select_n x1, other arithmetic, shards(): down = jnp.where(core == 0, head, tail)  1.07 us
    pallas_call x1, Pallas kernels, shards(): pl.pallas_call(own_kernel, out_shape=sds((rows, cols, chans), F32), in_sp...  0.98 us
    pallas_call x1, Pallas kernels, shards(): pl.pallas_call(late_kernel, out_shape=sds((rows, cols, chans), BF16), in_...  0.82 us
    pallas_call x1, Pallas kernels, shards(): pl.pallas_call(early_kernel, out_shape=sds((half, cols, chans), BF16), in...  0.75 us
  transfers between devices with their start and end apart: 5, of which 0 were waited for; matrix products, arithmetic and copies ran while one was open for 9% of the time, Pallas kernels for 43%

profile of v9, /device:TPU:0, one launch (start us, length us, event | category | flops | bytes accessed | tf_op | source)
XLA Modules:
  0.0 12.5 jit_solution(7071293866112000595)
XLA Ops:
  0.0 0.5 %collective-permute-start.1 = (bf16[8,128,256]{2,1,0:T(8,128)(2,1)}, bf16[8,128,256]{2,1,0:T(8,128)(2,1)S(1)}, u32[]{:S(2)}, u32[]{:S(2)}) collective-permute-start(bf16[8,128,256]{2,1,0:T(8,128)(2,1)} %fields_in.1), channel_id=1, source_target_pairs={{0,4},{4,0},{1,5},{5,1},{2,6},{6,2},{3,7},{7,3},{8,12},{12,8},{9,1... | collective-permute-start | bytes 1572872 | tf_op jit(solution)/shard_map/ppermute | solution.py:320
  0.5 1.1 %broadcast_select_fusion = (bf16[4,128,256]{2,1,0:T(8,128)(2,1)S(1)}, bf16[4,128,256]{2,1,0:T(8,128)(2,1)S(1)}) fusion(pred[]{:T(512)S(6)} %eq.2, bf16[8,128,256]{2,1,0:T(8,128)(2,1)} %fields_in.1), kind=kLoop, calls=%fused_computation | loop fusion | flops 262144 | bytes 1048577 | tf_op jit(solution)/shard_map/jit(_where)/select_n | solution.py:318
  1.5 0.1 collective-permute-start.3
  1.6 1.3 %fetch_operands.1 = (s32[8]{0:T(128)S(1)}, s32[8]{0:T(128)S(1)}, f32[9,4,32]{2,1,0:T(4,128)S(1)}, bf16[6,4,8]{2,1,0:T(4,128)(2,1)S(1)}, bf16[4,8,256]{2,1,0:T(8,...) custom-call(s32[8]{0:T(128)} %start_in, ...), custom_call_target="tpu_custom_call" | custom-call | flops 100000 | bytes 1000 | tf_op jit(solution)/shard_map/fetch_operands/pallas_call | solution.py:331
  2.9 2.6 %collective-permute-start = (bf16[4,128,256]{2,1,0:T(8,128)(2,1)S(1)}, bf16[4,128,256]{2,1,0:T(8,128)(2,1)S(1)}, u32[]{:S(2)}, u32[]{:S(2)}) collective-permute-start(bf16[4,128,256]{2,1,0:T(8,128)(2,1)S(1)} %get-tuple-element.28), channel_id=1, source_target_pairs={{0,8},{4,0},{8,16},{12,4},{16,24},{20,12},{24,28},{28,20},{1,9},{5... | collective-permute-start | bytes 786440 | tf_op jit(solution)/shard_map/ppermute | solution.py:360
  5.5 0.0 collective-permute-done.1.other
  5.6 0.2 %collective-permute-start.4 = (bf16[4,8,256]{2,1,0:T(8,128)(2,1)S(1)}, bf16[4,8,256]{2,1,0:T(8,128)(2,1)S(1)}, u32[]{:S(2)}, u32[]{:S(2)}) collective-permute-start(bf16[4,8,256]{2,1,0:T(8,128)(2,1)S(1)} %get-tuple-element.51), channel_id=1, source_target_pairs={{0,4},{4,12},{8,0},{12,20},{16,8},{20,28},{24,16},{28,24},{1,5},{5... | collective-permute-start | bytes 49160 | tf_op jit(solution)/shard_map/ppermute | solution.py:381
  5.8 1.8 %collective-permute-start.2 = (bf16[4,8,256]{2,1,0:T(8,128)(2,1)S(1)}, bf16[4,8,256]{2,1,0:T(8,128)(2,1)S(1)}, u32[]{:S(2)}, u32[]{:S(2)}) collective-permute-start(bf16[4,8,256]{2,1,0:T(8,128)(2,1)S(1)} %get-tuple-element.52), channel_id=1, source_target_pairs={{0,8},{4,0},{8,16},{12,4},{16,24},{20,12},{24,28},{28,20},{1,9},{5... | collective-permute-start | bytes 49160 | tf_op jit(solution)/shard_map/ppermute | solution.py:382
  7.6 0.6 %filter_weights.1 = (bf16[2,256,128]{2,1,0:T(8,128)(2,1)S(1)}, bf16[512,256]{1,0:T(8,128)(2,1)S(1)}, bf16[128,256]{1,0:T(8,128)(2,1)S(1)}) custom-call(s32[8]{0:T(128)S(1)} %get-tuple-element.29.start, s32[8]{0:T(128)S(1)} %get-tuple-element.30.width, f32[9,4,32]{2,1,0:T(4,128)S(1)} %get-tuple-element.31.lon, bf16[6,4,8]{2,1,0:T(4,128)(2,1)S(1)} %get-tuple-element.32.lat, ...), custom_call_target="tpu_custom_call" | custom-call | flops 100000 | bytes 1000 | tf_op jit(solution)/shard_map/filter_weights/pallas_call | solution.py:361
  8.3 1.0 %own_rows.1.acc_in = f32[8,128,256]{2,1,0:T(8,128)S(1)} custom-call(bf16[512,256]{1,0:T(8,128)(2,1)S(1)} %get-tuple-element.34.own_weights, bf16[8,128,256]{2,1,0:T(8,128)(2,1)S(1)} %get-tuple-element.35.fields, bf16[1024,256]{1,0:T(8,128)(2,1)S(1)} %get-tuple-element.36.mix), custom_call_target="tpu_custom_call" | custom-call | flops 100000 | bytes 1000 | tf_op jit(solution)/shard_map/own_rows/pallas_call | solution.py:383
  9.2 1.7 %partner_columns.1 = (f32[8,128,256]{2,1,0:T(8,128)S(1)}, bf16[4,512,256]{2,1,0:T(8,128)(2,1)S(1)}) custom-call(f32[8,128,256]{2,1,0:T(8,128)S(1)} %own_rows.1.acc_in, bf16[4,512,256]{2,1,0:T(8,128)(2,1)S(1)} %get-tuple-element.37.turned_in, bf16[512,256]{1,0:T(8,128)(2,1)S(1)} %get-tuple-element.34.own_weights, ...), custom_call_target="tpu_custom_call", output_to_operand_aliasing={{0}: (0, {}), {1}: (1, {})} | custom-call | flops 100000 | bytes 1000 | tf_op jit(solution)/shard_map/partner_columns/pallas_call | solution.py:397
  10.9 0.0 collective-permute-done.3.halo
  10.9 0.0 collective-permute-done.4.edges
  10.9 0.8 %early_side.1.early = bf16[4,128,256]{2,1,0:T(8,128)(2,1)S(1)} custom-call(bf16[4,128,256]{2,1,0:T(8,128)(2,1)S(1)} %collective-permute-done.3.halo, bf16[4,8,256]{2,1,0:T(8,128)(2,1)S(1)} %collective-permute-done.4.edges, bf16[2,256,128]{2,1,0:T(8,128)(2,1)S(1)} %get-tuple-element.42.weights, f32[8,128,256]{2,1,0:T(8,128)S(1)} %get-tuple-element.43.acc, ...), custom_call_target="tpu_custom_call" | custom-call | flops 100000 | bytes 1000 | tf_op jit(solution)/shard_map/early_side/pallas_call | solution.py:422
  11.7 0.0 collective-permute-done.halo
  11.7 0.0 collective-permute-done.2.edges
  11.7 0.8 %late_side.1 = bf16[8,128,256]{2,1,0:T(8,128)(2,1)} custom-call(bf16[4,128,256]{2,1,0:T(8,128)(2,1)S(1)} %early_side.1.early, bf16[4,128,256]{2,1,0:T(8,128)(2,1)S(1)} %collective-permute-done.halo, bf16[4,8,256]{2,1,0:T(8,128)(2,1)S(1)} %collective-permute-done.2.edges, bf16[2,256,128]{2,1,0:T(8,128)(2,1)S(1)} %get-tuple-element.42.weights, ...), custom_call_target="tpu_custom_call" | custom-call | tf_op jit(solution)/shard_map/late_side/pallas_call | solution.py:433
  (2 shorter events, 0.0 us)
Async XLA Ops:
  0.0 5.5 %collective-permute-start.1 = (bf16[8,128,256]{2,1,0:T(8,128)(2,1)}, bf16[8,128,256]{2,1,0:T(8,128)(2,1)S(1)}, u32[]{:S(2)}, u32[]{:S(2)}) collective-permute-start(bf16[8,128,256]{2,1,0:T(8,128)(2,1)} %fields_in.1), channel_id=1, source_target_pairs={{0,4},{4,0},{1,5},{5,1},{2,6},{6,2},{3,7},{7,3},{8,12},{12,8},{9,1... | collective-permute-start | bytes 1572872 | tf_op jit(solution)/shard_map/ppermute | solution.py:320
  1.5 9.4 %collective-permute-start.3 = (bf16[4,128,256]{2,1,0:T(8,128)(2,1)S(1)}, bf16[4,128,256]{2,1,0:T(8,128)(2,1)S(1)}, u32[]{:S(2)}, u32[]{:S(2)}) collective-permute-start(bf16[4,128,256]{2,1,0:T(8,128)(2,1)S(1)} %get-tuple-element.49), channel_id=1, source_target_pairs={{0,4},{4,12},{8,0},{12,20},{16,8},{20,28},{24,16},{28,24},{1,5},{5... | collective-permute-start | bytes 786440 | tf_op jit(solution)/shard_map/ppermute | solution.py:321
  2.9 8.8 %collective-permute-start = (bf16[4,128,256]{2,1,0:T(8,128)(2,1)S(1)}, bf16[4,128,256]{2,1,0:T(8,128)(2,1)S(1)}, u32[]{:S(2)}, u32[]{:S(2)}) collective-permute-start(bf16[4,128,256]{2,1,0:T(8,128)(2,1)S(1)} %get-tuple-element.28), channel_id=1, source_target_pairs={{0,8},{4,0},{8,16},{12,4},{16,24},{20,12},{24,28},{28,20},{1,9},{5... | collective-permute-start | bytes 786440 | tf_op jit(solution)/shard_map/ppermute | solution.py:360
  5.6 5.4 %collective-permute-start.4 = (bf16[4,8,256]{2,1,0:T(8,128)(2,1)S(1)}, bf16[4,8,256]{2,1,0:T(8,128)(2,1)S(1)}, u32[]{:S(2)}, u32[]{:S(2)}) collective-permute-start(bf16[4,8,256]{2,1,0:T(8,128)(2,1)S(1)} %get-tuple-element.51), channel_id=1, source_target_pairs={{0,4},{4,12},{8,0},{12,20},{16,8},{20,28},{24,16},{28,24},{1,5},{5... | collective-permute-start | bytes 49160 | tf_op jit(solution)/shard_map/ppermute | solution.py:381
  5.8 5.9 %collective-permute-start.2 = (bf16[4,8,256]{2,1,0:T(8,128)(2,1)S(1)}, bf16[4,8,256]{2,1,0:T(8,128)(2,1)S(1)}, u32[]{:S(2)}, u32[]{:S(2)}) collective-permute-start(bf16[4,8,256]{2,1,0:T(8,128)(2,1)S(1)} %get-tuple-element.52), channel_id=1, source_target_pairs={{0,8},{4,0},{8,16},{12,4},{16,24},{20,12},{24,28},{28,20},{1,9},{5... | collective-permute-start | bytes 49160 | tf_op jit(solution)/shard_map/ppermute | solution.py:382

commit v10 on v8

--- a/solution.py
+++ b/solution.py
@@ -48,9 +48,24 @@
         hidden[at : at + BLOCK, k * chans : (k + 1) * chans] = part[n * BLOCK : (n + 1) * BLOCK]
 
 
+def polar_matrices(cycle_taps, turned, at_top):
+    basis, twice, cycle = cycle_taps.shape
+    polar = twice // 2
+    cols = turned.shape[1] // basis
+    total = lax.broadcasted_iota(jnp.int32, (cycle, cycle), 0) + lax.broadcasted_iota(
+        jnp.int32, (cycle, cycle), 1
+    )
+    turn = jnp.where((total == 0) | (total == cycle), 1.0, 0.0).astype(BF16)
+    negated = matmul(cycle_taps[...].reshape(-1, cycle), turn)
+    for p in range(polar):
+        for k in range(basis):
+            n = k * twice + (p if at_top else p + polar)
+            turned[p, k * cols : (k + 1) * cols, :] = staircase(negated[n : n + 1], cols)
+
+
 def weight_kernel(
     start_in, width_in, lon_in, lat_in, fields_in, cycle_in, mixing_in,
-    halo_weights, own_weights, polar_weights, cycle_taps, fields, mix,
+    halo_weights, own_weights, polar_weights, cycle_taps, fields, mix, turned,
     start, width, lon, lat, lon_wide, lat_wide, sems,
 ):
     rows, cols, chans = fields.shape
@@ -141,32 +156,25 @@
     line = chosen(terms)
     for i in range(rows):
         polar_weights[i * BLOCK : (i + 1) * BLOCK, :] = staircase(line[i : i + 1], BLOCK)
-    for n in range(4, 7):
-        copies[n].wait()
-
-
-def own_kernel(own_weights, cycle_taps, fields, mix, acc, turned, ext, hidden):
+    copies[5].wait()
+
+    @pl.when(at_top)
+    def top():
+        polar_matrices(cycle_taps, turned, True)
+
+    copies[4].wait()
+    copies[6].wait()
+
+
+def own_kernel(turned_in, own_weights, cycle_taps, fields, mix, acc, turned, ext, hidden):
+    del turned_in
     rows, cols, chans = fields.shape
     basis = mix.shape[0] // chans
-    polar = cycle_taps.shape[1] // 2
-    cycle = cycle_taps.shape[2]
     near = (SPAN - BLOCK) // 4
-    lat_pos = lax.axis_index("lat")
-    at_top = lat_pos == 0
-    at_bottom = lat_pos == lax.axis_size("lat") - 1
-
-    @pl.when(at_top | at_bottom)
-    def polar_matrices():
-        total = lax.broadcasted_iota(jnp.int32, (cycle, cycle), 0) + lax.broadcasted_iota(
-            jnp.int32, (cycle, cycle), 1
-        )
-        turn = jnp.where((total == 0) | (total == cycle), 1.0, 0.0).astype(BF16)
-        negated = matmul(cycle_taps[...].reshape(-1, cycle), turn)
-        for p in range(polar):
-            for k in range(basis):
-                n = k * 2 * polar + p
-                line = jnp.where(at_top, negated[n : n + 1], negated[n + polar : n + polar + 1])
-                turned[p, k * cols : (k + 1) * cols, :] = staircase(line, cols)
+
+    @pl.when(lax.axis_index("lat") == lax.axis_size("lat") - 1)
+    def bottom():
+        polar_matrices(cycle_taps, turned, False)
 
     blank = jnp.zeros((near, chans), BF16)
     pad = jnp.zeros((ext.shape[1] - cols - near, chans), BF16)
@@ -239,11 +247,15 @@
             )
 
 
-def side_rows(side, halo, edges, weights, acc, mix, ext, hidden, present, result):
+def side_rows(
+    side, halo, edges, weights, acc, mix, ext, hidden, present, result, ready=lambda at: None
+):
     half, cols, chans = result.shape
     basis = mix.shape[0] // chans
     reach = edges.shape[1] // 2
     rows = pl.ds(side * half, half)
+    wide = cols // 2
+    parts = [slice(n * wide, (n + 1) * wide) for n in range(2)]
 
     @pl.when(present)
     def arrived():
@@ -252,16 +264,22 @@
             edge = edges[p]
             ext[p] = jnp.concatenate([edge[reach:], halo[p], edge[:reach], pad], axis=0)
         groups = [(i, k) for k in range(basis) for i in range(half)]
-        for at in range(0, cols, BLOCK):
-            window_products(
-                weights.at[side], ext[:, at : at + SPAN, :], hidden, groups, cols, at, chans
-            )
-        total = matmul(hidden[...], mix[...]).reshape(half, cols, chans)
-        result[...] = (total + acc[rows]).astype(BF16)
+        for n, part in enumerate(parts):
+            for at in range(0, wide, BLOCK):
+                cells = ext[:, part.start + at : part.start + at + SPAN, :]
+                window_products(
+                    weights.at[side], cells, hidden.at[n], groups, wide, at, chans
+                )
+        for n, part in enumerate(parts):
+            total = matmul(hidden[n], mix[...]).reshape(half, wide, chans)
+            result[:, part, :] = (total + acc[rows, part, :]).astype(BF16)
+            ready(part)
 
     @pl.when(jnp.logical_not(present))
     def absent():
-        result[...] = acc[rows].astype(BF16)
+        for part in parts:
+            result[:, part, :] = acc[rows, part, :].astype(BF16)
+            ready(part)
 
 
 def from_side(which):
@@ -279,15 +297,26 @@
 
 
 def late_kernel(early, halo, edges, weights, acc, mix, out, ext, hidden, result, sems):
-    half = result.shape[0]
+    half, cols, _ = result.shape
     side, present = from_side(1)
-    first = pltpu.make_async_copy(early, out.at[pl.ds((1 - side) * half, half)], sems.at[0])
+    rows = pl.ds(side * half, half)
+    other_rows = pl.ds((1 - side) * half, half)
+
+    def copy_of(part):
+        n = 0 if part.start == 0 else 1
+        return pltpu.make_async_copy(
+            result.at[:, part, :], out.at[rows, part, :], sems.at[n]
+        )
+
+    first = pltpu.make_async_copy(early, out.at[other_rows], sems.at[2])
     first.start()
-    side_rows(side, halo, edges, weights, acc, mix, ext, hidden, present, result)
-    second = pltpu.make_async_copy(result, out.at[pl.ds(side * half, half)], sems.at[1])
-    second.start()
+    side_rows(
+        side, halo, edges, weights, acc, mix, ext, hidden, present, result,
+        lambda part: copy_of(part).start(),
+    )
     first.wait()
-    second.wait()
+    for n in range(2):
+        copy_of(slice(n * cols // 2, (n + 1) * cols // 2)).wait()
 
 
 def shards(fields, lon_taps, lat_taps, cycle_taps, band_start, band_width, mixing):
@@ -303,12 +332,10 @@
     assert cycle == 2 * cols and rows == 2 * HALO and basis * polar * BLOCK == rows * SPAN
     assert reach == (SPAN - BLOCK) // 4
     ahead, back = ring(lat_count, 1), ring(lat_count, -1)
-    head, tail = fields[:HALO], fields[rows - HALO :]
-    down = jnp.where(core == 0, head, tail)
-    up = jnp.where(core == 0, tail, head)
     other = lax.ppermute(fields, "lon", SWAP)
-    second = lax.ppermute(down, axes, back)
-    down, band_start = lax.optimization_barrier((down, band_start))
+    going = lax.dynamic_slice_in_dim(fields, core * HALO, HALO, 0)
+    second = lax.ppermute(going, axes, back)
+    going, band_start = lax.optimization_barrier((going, band_start))
 
     vmem = pl.BlockSpec(memory_space=pltpu.VMEM)
     hbm = pl.BlockSpec(memory_space=pltpu.HBM)
@@ -316,7 +343,7 @@
     group = basis * rows * BLOCK
     ext_cols = cols + SPAN - BLOCK
     limit = pltpu.CompilerParams(vmem_limit_bytes=32 * 1024 * 1024)
-    halo_weights, own_weights, polar_weights, turns, whole, mix = pl.pallas_call(
+    halo_weights, own_weights, polar_weights, turns, whole, mix, turned = pl.pallas_call(
         weight_kernel,
         out_shape=(
             sds((2, group // 2, HALO * SPAN), BF16),
@@ -325,9 +352,10 @@
             sds((basis, 2 * polar, cycle), BF16),
             sds((rows, cols, chans), BF16),
             sds((basis * chans, chans), BF16),
+            sds((polar, basis * cols, cycle), BF16),
         ),
         in_specs=[hbm] * 7,
-        out_specs=[vmem] * 6,
+        out_specs=[vmem] * 7,
         scratch_shapes=[
             pltpu.SMEM((rows,), jnp.int32),
             pltpu.SMEM((rows,), jnp.int32),
@@ -353,19 +381,20 @@
         ),
     )
     edges = jnp.concatenate([other[:, :reach], other[:, cols - reach :]], axis=1)
-    head, tail = edges[:HALO], edges[rows - HALO :]
-    second_edges = lax.ppermute(jnp.where(core == 0, head, tail), axes, back)
-    up, own_weights = lax.optimization_barrier((up, own_weights))
-    first = lax.ppermute(up, axes, ahead)
-    first_edges = lax.ppermute(jnp.where(core == 0, tail, head), axes, ahead)
+    upper, lower = edges[:HALO], edges[rows - HALO :]
+    second_edges = lax.ppermute(jnp.where(core == 0, upper, lower), axes, back)
+    head, tail = whole[:HALO], whole[rows - HALO :]
+    first = lax.ppermute(jnp.where(core == 0, tail, head), axes, ahead)
+    first_edges = lax.ppermute(jnp.where(core == 0, lower, upper), axes, ahead)
     acc, turned = pl.pallas_call(
         own_kernel,
         out_shape=(
             sds((rows, cols, chans), F32),
             sds((polar, basis * cols, cycle), BF16),
         ),
-        in_specs=[vmem] * 4,
+        in_specs=[vmem] * 5,
         out_specs=(vmem, vmem),
+        input_output_aliases={0: 1},
         scratch_shapes=[
             pltpu.VMEM((rows, ext_cols, chans), BF16),
             pltpu.VMEM((rows * (cols - 2 * BLOCK), basis * chans), BF16),
@@ -375,7 +404,7 @@
             flops=100_000, bytes_accessed=1_000, transcendentals=0
         ),
         name="own_rows",
-    )(own_weights, turns, whole, mix)
+    )(turned, own_weights, turns, whole, mix)
 
     acc = pl.pallas_call(
         partner_kernel,
@@ -398,7 +427,7 @@
     half = rows // 2
     scratch = [
         pltpu.VMEM((HALO, ext_cols, chans), BF16),
-        pltpu.VMEM((half * cols, basis * chans), BF16),
+        pltpu.VMEM((2, half * cols // 2, basis * chans), BF16),
     ]
     limit = pltpu.CompilerParams(vmem_limit_bytes=32 * 1024 * 1024)
     second, second_edges, acc = lax.optimization_barrier((second, second_edges, acc))
@@ -423,7 +452,7 @@
         scratch_shapes=[
             *scratch,
             pltpu.VMEM((half, cols, chans), BF16),
-            pltpu.SemaphoreType.DMA((2,)),
+            pltpu.SemaphoreType.DMA((3,)),
         ],
         compiler_params=limit,
         name="late_side",

time: 12.6 us -> 13.7 us (1.087)
  local copies, waits for them, and re-layouts: 0.02 us -> 1.69 us
  other arithmetic: 1.09 us -> 0.06 us
  waiting for transfers between devices: 0.84 us -> 1.28 us
    dynamic_slice x0 -> x1, local copies, waits for them, and re-layouts: none -> 1.67 us  [shards(): going = lax.dynamic_slice_in_dim(fields, core * HALO, HALO, 0)]
    select_n x2, other arithmetic: 1.09 us -> 0.06 us  [the longest x1 0.03 us: shards(): first = lax.ppermute(jnp.where(core == 0, tail, head), axes, ahead)]
    pallas_call x1, Pallas kernels: 1.47 us -> 0.98 us  [shards(): pl.pallas_call(own_kernel, out_shape=(sds((rows, cols, chans), F32), sds(...]
    pallas_call x1, Pallas kernels: 1.47 us -> 1.96 us  [shards(): pl.pallas_call(weight_kernel, out_shape=(sds((2, group // 2, HALO * SPAN)...]
    ppermute x4, waiting for transfers between devices: 0.83 us -> 1.27 us  [the longest x1 1.09 us: shards(): first = lax.ppermute(jnp.where(core == 0, tail, head), axes, ahead)]
  transfers between devices with their start and end apart: 5 -> 5, of which waited for: 2 -> 2; matrix products, arithmetic and copies ran while one was open for 9% -> 13% of each run, Pallas kernels for 37% -> 34%
where the time goes in v10:
time: 13.7 us; the launch traced here: 13.5 us
  Pallas kernels  6.07 us (44%)
  starting transfers between devices  4.3 us (31%)
  local copies, waits for them, and re-layouts  1.69 us (12%)
  waiting for transfers between devices  1.28 us (9%)
    ppermute x1, starting transfers between devices, shards(): second = lax.ppermute(going, axes, back)  2.74 us
    pallas_call x1, Pallas kernels, shards(): pl.pallas_call(weight_kernel, out_shape=(sds((2, group // 2, HALO * SPAN)...  1.96 us
    dynamic_slice x1, local copies, waits for them, and re-layouts, shards(): going = lax.dynamic_slice_in_dim(fields, core * HALO, HALO, 0)  1.67 us
    pallas_call x1, Pallas kernels, shards(): pl.pallas_call(partner_kernel, out_shape=sds((rows, cols, chans), F32), i...  1.66 us
    ppermute x1, starting transfers between devices, shards(): second_edges = lax.ppermute(jnp.where(core == 0, upper, lower), axes, back)  1.46 us
    pallas_call x1, Pallas kernels, shards(): pl.pallas_call(late_kernel, out_shape=sds((rows, cols, chans), BF16), in_...  1.42 us
    ppermute x1, waiting for transfers between devices, shards(): first = lax.ppermute(jnp.where(core == 0, tail, head), axes, ahead)  1.09 us
    pallas_call x1, Pallas kernels, shards(): pl.pallas_call(own_kernel, out_shape=(sds((rows, cols, chans), F32), sds(...  0.98 us
  transfers between devices with their start and end apart: 5, of which 2 were waited for; matrix products, arithmetic and copies ran while one was open for 13% of the time, Pallas kernels for 34%

profile of v10, /device:TPU:1, one launch (start us, length us, event | category | flops | bytes accessed | tf_op | source)
XLA Modules:
  0.0 13.5 jit_solution(6870472293951268557)
XLA Ops:
  0.0 0.1 collective-permute-start.1
  0.1 1.7 %constant_dynamic-slice_fusion = bf16[4,128,256]{2,1,0:T(8,128)(2,1)} fusion(bf16[8,128,256]{2,1,0:T(8,128)(2,1)} %fields_in.1, s32[]{:T(128)S(6)} %select_n.24), kind=kLoop, calls=%fused_computation.7 | loop fusion | bytes 524292 | tf_op jit(solution)/shard_map/dynamic_slice | solution.py:336
  1.7 2.7 %collective-permute-start.3 = (bf16[4,128,256]{2,1,0:T(8,128)(2,1)}, bf16[4,128,256]{2,1,0:T(8,128)(2,1)S(1)}, u32[]{:S(2)}, u32[]{:S(2)}) collective-permute-start(bf16[4,128,256]{2,1,0:T(8,128)(2,1)} %constant_dynamic-slice_fusion), channel_id=1, source_target_pairs={{0,4},{4,12},{8,0},{12,20},{16,8},{20,28},{24,16},{28,24},{1,5},{5... | collective-permute-start | bytes 786440 | tf_op jit(solution)/shard_map/ppermute | solution.py:337
  4.5 2.0 %filter_weights.1 = (bf16[2,256,128]{2,1,0:T(8,128)(2,1)S(1)}, bf16[512,256]{1,0:T(8,128)(2,1)S(1)}, bf16[128,256]{1,0:T(8,128)(2,1)S(1)}, bf16[4,8,256]{2,1,0:T...) custom-call(s32[8]{0:T(128)} %start_in, ...), custom_call_target="tpu_custom_call" | custom-call | flops 100000 | bytes 1000 | tf_op jit(solution)/shard_map/filter_weights/pallas_call | solution.py:346
  6.5 0.0 collective-permute-start
  6.5 0.0 collective-permute-done.1.other
  6.6 1.5 %collective-permute-start.4 = (bf16[4,8,256]{2,1,0:T(8,128)(2,1)S(1)}, bf16[4,8,256]{2,1,0:T(8,128)(2,1)S(1)}, u32[]{:S(2)}, u32[]{:S(2)}) collective-permute-start(bf16[4,8,256]{2,1,0:T(8,128)(2,1)S(1)} %get-tuple-element.39), channel_id=1, source_target_pairs={{0,4},{4,12},{8,0},{12,20},{16,8},{20,28},{24,16},{28,24},{1,5},{5... | collective-permute-start | bytes 49160 | tf_op jit(solution)/shard_map/ppermute | solution.py:385
  8.0 1.0 %own_rows.1 = (f32[8,128,256]{2,1,0:T(8,128)S(1)}, bf16[4,512,256]{2,1,0:T(8,128)(2,1)S(1)}) custom-call(bf16[4,512,256]{2,1,0:T(8,128)(2,1)S(1)} %get-tuple-element.23.turned_in, bf16[512,256]{1,0:T(8,128)(2,1)S(1)} %get-tuple-element.24.own_weights, bf16[4,8,256]{2,1,0:T(8,128)(2,1)S(1)} %get-tuple-element.25.cycle_taps, ...), custom_call_target="tpu_custom_call", output_to_operand_aliasing={{1}: (0, {})} | custom-call | flops 100000 | bytes 1000 | tf_op jit(solution)/shard_map/own_rows/pallas_call | solution.py:389
  9.0 0.0 collective-permute-start.2
  9.1 1.7 %partner_columns.1.acc = f32[8,128,256]{2,1,0:T(8,128)S(1)} custom-call(f32[8,128,256]{2,1,0:T(8,128)S(1)} %get-tuple-element.27.acc_in, bf16[512,256]{1,0:T(8,128)(2,1)S(1)} %get-tuple-element.24.own_weights, bf16[128,256]{1,0:T(8,128)(2,1)S(1)} %get-tuple-element.28.polar_weights, ...), custom_call_target="tpu_custom_call", output_to_operand_aliasing={{}: (0, {})} | custom-call | flops 100000 | bytes 1000 | tf_op jit(solution)/shard_map/partner_columns/pallas_call | solution.py:409
  10.7 0.0 collective-permute-done.3.halo
  10.7 0.0 collective-permute-done.4.edges
  10.8 1.1 %collective-permute-done.halo = bf16[4,128,256]{2,1,0:T(8,128)(2,1)S(1)} collective-permute-done((bf16[4,128,256]{2,1,0:T(8,128)(2,1)S(1)}, bf16[4,128,256]{2,1,0:T(8,128)(2,1)S(1)}, u32[]{:S(2)}, u32[]{:S(2)}) %collective-permute-start) | collective-permute-done | bytes 262176 | tf_op jit(solution)/shard_map/ppermute | solution.py:387
  11.9 0.2 %collective-permute-done.2.edges = bf16[4,8,256]{2,1,0:T(8,128)(2,1)S(1)} collective-permute-done((bf16[4,8,256]{2,1,0:T(8,128)(2,1)S(1)}, bf16[4,8,256]{2,1,0:T(8,128)(2,1)S(1)}, u32[]{:S(2)}, u32[]{:S(2)}) %collective-permute-start.2) | collective-permute-done | bytes 16416 | tf_op jit(solution)/shard_map/ppermute | solution.py:388
  12.1 1.4 %late_side.1 = bf16[8,128,256]{2,1,0:T(8,128)(2,1)} custom-call(bf16[4,128,256]{2,1,0:T(8,128)(2,1)S(1)} %early_side.1.early, bf16[4,128,256]{2,1,0:T(8,128)(2,1)S(1)} %collective-permute-done.halo, bf16[4,8,256]{2,1,0:T(8,128)(2,1)S(1)} %collective-permute-done.2.edges, bf16[2,256,128]{2,1,0:T(8,128)(2,1)S(1)} %get-tuple-element.32.weights, ...), custom_call_target="tpu_custom_call" | custom-call | tf_op jit(solution)/shard_map/late_side/pallas_call | solution.py:447
  (4 shorter events, 0.1 us)
Async XLA Ops:
  0.0 6.5 %collective-permute-start.1 = (bf16[8,128,256]{2,1,0:T(8,128)(2,1)}, bf16[8,128,256]{2,1,0:T(8,128)(2,1)S(1)}, u32[]{:S(2)}, u32[]{:S(2)}) collective-permute-start(bf16[8,128,256]{2,1,0:T(8,128)(2,1)} %fields_in.1), channel_id=1, source_target_pairs={{0,4},{4,0},{1,5},{5,1},{2,6},{6,2},{3,7},{7,3},{8,12},{12,8},{9,1... | collective-permute-start | bytes 1572872 | tf_op jit(solution)/shard_map/ppermute | solution.py:335
  1.7 9.0 %collective-permute-start.3 = (bf16[4,128,256]{2,1,0:T(8,128)(2,1)}, bf16[4,128,256]{2,1,0:T(8,128)(2,1)S(1)}, u32[]{:S(2)}, u32[]{:S(2)}) collective-permute-start(bf16[4,128,256]{2,1,0:T(8,128)(2,1)} %constant_dynamic-slice_fusion), channel_id=1, source_target_pairs={{0,4},{4,12},{8,0},{12,20},{16,8},{20,28},{24,16},{28,24},{1,5},{5... | collective-permute-start | bytes 786440 | tf_op jit(solution)/shard_map/ppermute | solution.py:337
  6.5 5.4 %collective-permute-start = (bf16[4,128,256]{2,1,0:T(8,128)(2,1)S(1)}, bf16[4,128,256]{2,1,0:T(8,128)(2,1)S(1)}, u32[]{:S(2)}, u32[]{:S(2)}) collective-permute-start(bf16[4,128,256]{2,1,0:T(8,128)(2,1)S(1)} %slice_select_fusion), channel_id=1, source_target_pairs={{0,8},{4,0},{8,16},{12,4},{16,24},{20,12},{24,28},{28,20},{1,9},{5... | collective-permute-start | bytes 786440 | tf_op jit(solution)/shard_map/ppermute | solution.py:387
  6.6 4.2 %collective-permute-start.4 = (bf16[4,8,256]{2,1,0:T(8,128)(2,1)S(1)}, bf16[4,8,256]{2,1,0:T(8,128)(2,1)S(1)}, u32[]{:S(2)}, u32[]{:S(2)}) collective-permute-start(bf16[4,8,256]{2,1,0:T(8,128)(2,1)S(1)} %get-tuple-element.39), channel_id=1, source_target_pairs={{0,4},{4,12},{8,0},{12,20},{16,8},{20,28},{24,16},{28,24},{1,5},{5... | collective-permute-start | bytes 49160 | tf_op jit(solution)/shard_map/ppermute | solution.py:385
  9.0 3.0 %collective-permute-start.2 = (bf16[4,8,256]{2,1,0:T(8,128)(2,1)S(1)}, bf16[4,8,256]{2,1,0:T(8,128)(2,1)S(1)}, u32[]{:S(2)}, u32[]{:S(2)}) collective-permute-start(bf16[4,8,256]{2,1,0:T(8,128)(2,1)S(1)} %get-tuple-element.40), channel_id=1, source_target_pairs={{0,8},{4,0},{8,16},{12,4},{16,24},{20,12},{24,28},{28,20},{1,9},{5... | collective-permute-start | bytes 49160 | tf_op jit(solution)/shard_map/ppermute | solution.py:388

commit v11 on v10

--- a/solution.py
+++ b/solution.py
@@ -158,7 +158,7 @@
         polar_weights[i * BLOCK : (i + 1) * BLOCK, :] = staircase(line[i : i + 1], BLOCK)
     copies[5].wait()
 
-    @pl.when(at_top)
+    @pl.when(at_top & (lax.axis_index("lon") == 0))
     def top():
         polar_matrices(cycle_taps, turned, True)
 
@@ -172,7 +172,13 @@
     basis = mix.shape[0] // chans
     near = (SPAN - BLOCK) // 4
 
-    @pl.when(lax.axis_index("lat") == lax.axis_size("lat") - 1)
+    lat_pos = lax.axis_index("lat")
+
+    @pl.when((lat_pos == 0) & (lax.axis_index("lon") != 0))
+    def top():
+        polar_matrices(cycle_taps, turned, True)
+
+    @pl.when(lat_pos == lax.axis_size("lat") - 1)
     def bottom():
         polar_matrices(cycle_taps, turned, False)
 
@@ -333,7 +339,7 @@
     assert reach == (SPAN - BLOCK) // 4
     ahead, back = ring(lat_count, 1), ring(lat_count, -1)
     other = lax.ppermute(fields, "lon", SWAP)
-    going = lax.dynamic_slice_in_dim(fields, core * HALO, HALO, 0)
+    going = jnp.where(core == 0, fields[:HALO], fields[rows - HALO :])
     second = lax.ppermute(going, axes, back)
     going, band_start = lax.optimization_barrier((going, band_start))
 

time: 13.7 us -> 12.6 us (0.920)
  local copies, waits for them, and re-layouts: 1.69 us -> 0.02 us
  other arithmetic: 0.06 us -> 1.11 us
  waiting for transfers between devices: 1.28 us -> 0.84 us
    dynamic_slice x1 -> x0, local copies, waits for them, and re-layouts: 1.67 us -> none  [shards(): going = lax.dynamic_slice_in_dim(fields, core * HALO, HALO, 0)]
    select_n x0 -> x1, other arithmetic: none -> 1.06 us  [shards(): going = jnp.where(core == 0, fields[:HALO], fields[rows - HALO:])]
    pallas_call x1, Pallas kernels: 0.98 us -> 1.47 us  [shards(): pl.pallas_call(own_kernel, out_shape=(sds((rows, cols, chans), F32), sds(...]
    ppermute x1, waiting for transfers between devices: 1.09 us -> 0.6 us  [shards(): first = lax.ppermute(jnp.where(core == 0, tail, head), axes, ahead)]
    pallas_call x1, Pallas kernels: 1.96 us -> 1.47 us  [shards(): pl.pallas_call(weight_kernel, out_shape=(sds((2, group // 2, HALO * SPAN)...]
  transfers between devices with their start and end apart: 5 -> 5, of which waited for: 2 -> 2; matrix products, arithmetic and copies ran while one was open for 13% -> 9% of each run, Pallas kernels for 34% -> 37%
where the time goes in v11:
time: 12.6 us; the launch traced here: 12.5 us
  Pallas kernels  6.08 us (48%)
  starting transfers between devices  4.32 us (34%)
  other arithmetic  1.11 us (9%)
  waiting for transfers between devices  0.84 us (7%)
    ppermute x1, starting transfers between devices, shards(): second = lax.ppermute(going, axes, back)  2.76 us
    pallas_call x1, Pallas kernels, shards(): pl.pallas_call(partner_kernel, out_shape=sds((rows, cols, chans), F32), i...  1.66 us
    pallas_call x1, Pallas kernels, shards(): pl.pallas_call(weight_kernel, out_shape=(sds((2, group // 2, HALO * SPAN)...  1.47 us
    pallas_call x1, Pallas kernels, shards(): pl.pallas_call(own_kernel, out_shape=(sds((rows, cols, chans), F32), sds(...  1.47 us
    ppermute x1, starting transfers between devices, shards(): second_edges = lax.ppermute(jnp.where(core == 0, upper, lower), axes, back)  1.46 us
    pallas_call x1, Pallas kernels, shards(): pl.pallas_call(late_kernel, out_shape=sds((rows, cols, chans), BF16), in_...  1.43 us
    select_n x1, other arithmetic, shards(): going = jnp.where(core == 0, fields[:HALO], fields[rows - HALO:])  1.06 us
    ppermute x1, waiting for transfers between devices, shards(): first = lax.ppermute(jnp.where(core == 0, tail, head), axes, ahead)  0.6 us
  transfers between devices with their start and end apart: 5, of which 2 were waited for; matrix products, arithmetic and copies ran while one was open for 9% of the time, Pallas kernels for 37%

profile of v11, /device:TPU:1, one launch (start us, length us, event | category | flops | bytes accessed | tf_op | source)
XLA Modules:
  0.0 12.5 jit_solution(9455692273587989638)
XLA Ops:
  0.0 0.1 collective-permute-start.1
  0.1 1.1 %slice_select_fusion.1 = bf16[4,128,256]{2,1,0:T(8,128)(2,1)S(1)} fusion(bf16[8,128,256]{2,1,0:T(8,128)(2,1)} %fields_in.1, pred[]{:T(512)S(6)} %eq.2), kind=kLoop, calls=%fused_computation.1 | loop fusion | flops 131072 | bytes 786433 | tf_op jit(solution)/shard_map/jit(_where)/select_n | solution.py:342
  1.1 2.8 %collective-permute-start.3 = (bf16[4,128,256]{2,1,0:T(8,128)(2,1)S(1)}, bf16[4,128,256]{2,1,0:T(8,128)(2,1)S(1)}, u32[]{:S(2)}, u32[]{:S(2)}) collective-permute-start(bf16[4,128,256]{2,1,0:T(8,128)(2,1)S(1)} %slice_select_fusion.1), channel_id=1, source_target_pairs={{0,4},{4,12},{8,0},{12,20},{16,8},{20,28},{24,16},{28,24},{1,5},{5... | collective-permute-start | bytes 786440 | tf_op jit(solution)/shard_map/ppermute | solution.py:343
  3.9 1.5 %filter_weights.1 = (bf16[2,256,128]{2,1,0:T(8,128)(2,1)S(1)}, bf16[512,256]{1,0:T(8,128)(2,1)S(1)}, bf16[128,256]{1,0:T(8,128)(2,1)S(1)}, bf16[4,8,256]{2,1,0:T...) custom-call(s32[8]{0:T(128)} %start_in, ...), custom_call_target="tpu_custom_call" | custom-call | flops 100000 | bytes 1000 | tf_op jit(solution)/shard_map/filter_weights/pallas_call | solution.py:352
  5.4 0.0 collective-permute-start
  5.4 0.0 collective-permute-done.1.other
  5.5 1.5 %collective-permute-start.4 = (bf16[4,8,256]{2,1,0:T(8,128)(2,1)S(1)}, bf16[4,8,256]{2,1,0:T(8,128)(2,1)S(1)}, u32[]{:S(2)}, u32[]{:S(2)}) collective-permute-start(bf16[4,8,256]{2,1,0:T(8,128)(2,1)S(1)} %get-tuple-element.39), channel_id=1, source_target_pairs={{0,4},{4,12},{8,0},{12,20},{16,8},{20,28},{24,16},{28,24},{1,5},{5... | collective-permute-start | bytes 49160 | tf_op jit(solution)/shard_map/ppermute | solution.py:391
  7.0 1.5 %own_rows.1 = (f32[8,128,256]{2,1,0:T(8,128)S(1)}, bf16[4,512,256]{2,1,0:T(8,128)(2,1)S(1)}) custom-call(bf16[4,512,256]{2,1,0:T(8,128)(2,1)S(1)} %get-tuple-element.23.turned_in, bf16[512,256]{1,0:T(8,128)(2,1)S(1)} %get-tuple-element.24.own_weights, bf16[4,8,256]{2,1,0:T(8,128)(2,1)S(1)} %get-tuple-element.25.cycle_taps, ...), custom_call_target="tpu_custom_call", output_to_operand_aliasing={{1}: (0, {})} | custom-call | flops 100000 | bytes 1000 | tf_op jit(solution)/shard_map/own_rows/pallas_call | solution.py:395
  8.4 0.0 collective-permute-start.2
  8.5 1.7 %partner_columns.1.acc = f32[8,128,256]{2,1,0:T(8,128)S(1)} custom-call(f32[8,128,256]{2,1,0:T(8,128)S(1)} %get-tuple-element.27.acc_in, bf16[512,256]{1,0:T(8,128)(2,1)S(1)} %get-tuple-element.24.own_weights, bf16[128,256]{1,0:T(8,128)(2,1)S(1)} %get-tuple-element.28.polar_weights, ...), custom_call_target="tpu_custom_call", output_to_operand_aliasing={{}: (0, {})} | custom-call | flops 100000 | bytes 1000 | tf_op jit(solution)/shard_map/partner_columns/pallas_call | solution.py:415
  10.1 0.0 collective-permute-done.3.halo
  10.1 0.0 collective-permute-done.4.edges
  10.2 0.6 %collective-permute-done.halo = bf16[4,128,256]{2,1,0:T(8,128)(2,1)S(1)} collective-permute-done((bf16[4,128,256]{2,1,0:T(8,128)(2,1)S(1)}, bf16[4,128,256]{2,1,0:T(8,128)(2,1)S(1)}, u32[]{:S(2)}, u32[]{:S(2)}) %collective-permute-start) | collective-permute-done | bytes 262176 | tf_op jit(solution)/shard_map/ppermute | solution.py:393
  10.8 0.2 %collective-permute-done.2.edges = bf16[4,8,256]{2,1,0:T(8,128)(2,1)S(1)} collective-permute-done((bf16[4,8,256]{2,1,0:T(8,128)(2,1)S(1)}, bf16[4,8,256]{2,1,0:T(8,128)(2,1)S(1)}, u32[]{:S(2)}, u32[]{:S(2)}) %collective-permute-start.2) | collective-permute-done | bytes 16416 | tf_op jit(solution)/shard_map/ppermute | solution.py:394
  11.0 1.4 %late_side.1 = bf16[8,128,256]{2,1,0:T(8,128)(2,1)} custom-call(bf16[4,128,256]{2,1,0:T(8,128)(2,1)S(1)} %early_side.1.early, bf16[4,128,256]{2,1,0:T(8,128)(2,1)S(1)} %collective-permute-done.halo, bf16[4,8,256]{2,1,0:T(8,128)(2,1)S(1)} %collective-permute-done.2.edges, bf16[2,256,128]{2,1,0:T(8,128)(2,1)S(1)} %get-tuple-element.32.weights, ...), custom_call_target="tpu_custom_call" | custom-call | tf_op jit(solution)/shard_map/late_side/pallas_call | solution.py:453
  (4 shorter events, 0.1 us)
Async XLA Ops:
  0.0 5.4 %collective-permute-start.1 = (bf16[8,128,256]{2,1,0:T(8,128)(2,1)}, bf16[8,128,256]{2,1,0:T(8,128)(2,1)S(1)}, u32[]{:S(2)}, u32[]{:S(2)}) collective-permute-start(bf16[8,128,256]{2,1,0:T(8,128)(2,1)} %fields_in.1), channel_id=1, source_target_pairs={{0,4},{4,0},{1,5},{5,1},{2,6},{6,2},{3,7},{7,3},{8,12},{12,8},{9,1... | collective-permute-start | bytes 1572872 | tf_op jit(solution)/shard_map/ppermute | solution.py:341
  1.1 9.0 %collective-permute-start.3 = (bf16[4,128,256]{2,1,0:T(8,128)(2,1)S(1)}, bf16[4,128,256]{2,1,0:T(8,128)(2,1)S(1)}, u32[]{:S(2)}, u32[]{:S(2)}) collective-permute-start(bf16[4,128,256]{2,1,0:T(8,128)(2,1)S(1)} %slice_select_fusion.1), channel_id=1, source_target_pairs={{0,4},{4,12},{8,0},{12,20},{16,8},{20,28},{24,16},{28,24},{1,5},{5... | collective-permute-start | bytes 786440 | tf_op jit(solution)/shard_map/ppermute | solution.py:343
  5.4 5.4 %collective-permute-start = (bf16[4,128,256]{2,1,0:T(8,128)(2,1)S(1)}, bf16[4,128,256]{2,1,0:T(8,128)(2,1)S(1)}, u32[]{:S(2)}, u32[]{:S(2)}) collective-permute-start(bf16[4,128,256]{2,1,0:T(8,128)(2,1)S(1)} %slice_select_fusion), channel_id=1, source_target_pairs={{0,8},{4,0},{8,16},{12,4},{16,24},{20,12},{24,28},{28,20},{1,9},{5... | collective-permute-start | bytes 786440 | tf_op jit(solution)/shard_map/ppermute | solution.py:393
  5.5 4.6 %collective-permute-start.4 = (bf16[4,8,256]{2,1,0:T(8,128)(2,1)S(1)}, bf16[4,8,256]{2,1,0:T(8,128)(2,1)S(1)}, u32[]{:S(2)}, u32[]{:S(2)}) collective-permute-start(bf16[4,8,256]{2,1,0:T(8,128)(2,1)S(1)} %get-tuple-element.39), channel_id=1, source_target_pairs={{0,4},{4,12},{8,0},{12,20},{16,8},{20,28},{24,16},{28,24},{1,5},{5... | collective-permute-start | bytes 49160 | tf_op jit(solution)/shard_map/ppermute | solution.py:391
  8.4 2.6 %collective-permute-start.2 = (bf16[4,8,256]{2,1,0:T(8,128)(2,1)S(1)}, bf16[4,8,256]{2,1,0:T(8,128)(2,1)S(1)}, u32[]{:S(2)}, u32[]{:S(2)}) collective-permute-start(bf16[4,8,256]{2,1,0:T(8,128)(2,1)S(1)} %get-tuple-element.40), channel_id=1, source_target_pairs={{0,8},{4,0},{8,16},{12,4},{16,24},{20,12},{24,28},{28,20},{1,9},{5... | collective-permute-start | bytes 49160 | tf_op jit(solution)/shard_map/ppermute | solution.py:394

commit v12 on v11

--- a/solution.py
+++ b/solution.py
@@ -158,7 +158,7 @@
         polar_weights[i * BLOCK : (i + 1) * BLOCK, :] = staircase(line[i : i + 1], BLOCK)
     copies[5].wait()
 
-    @pl.when(at_top & (lax.axis_index("lon") == 0))
+    @pl.when(at_top & (lax.axis_index("lon") != 0))
     def top():
         polar_matrices(cycle_taps, turned, True)
 
@@ -174,7 +174,7 @@
 
     lat_pos = lax.axis_index("lat")
 
-    @pl.when((lat_pos == 0) & (lax.axis_index("lon") != 0))
+    @pl.when((lat_pos == 0) & (lax.axis_index("lon") == 0))
     def top():
         polar_matrices(cycle_taps, turned, True)
 
@@ -290,7 +290,7 @@
 
 def from_side(which):
     core = lax.axis_index("lon")
-    side = 1 - core if which == 0 else core
+    side = core if which == 0 else 1 - core
     lat_pos = lax.axis_index("lat")
     last = lax.axis_size("lat") - 1
     present = jnp.where(side == 0, lat_pos != 0, lat_pos != last)
@@ -339,8 +339,8 @@
     assert reach == (SPAN - BLOCK) // 4
     ahead, back = ring(lat_count, 1), ring(lat_count, -1)
     other = lax.ppermute(fields, "lon", SWAP)
-    going = jnp.where(core == 0, fields[:HALO], fields[rows - HALO :])
-    second = lax.ppermute(going, axes, back)
+    going = jnp.where(core == 0, fields[rows - HALO :], fields[:HALO])
+    early_halo = lax.ppermute(going, axes, ahead)
     going, band_start = lax.optimization_barrier((going, band_start))
 
     vmem = pl.BlockSpec(memory_space=pltpu.VMEM)
@@ -388,10 +388,10 @@
     )
     edges = jnp.concatenate([other[:, :reach], other[:, cols - reach :]], axis=1)
     upper, lower = edges[:HALO], edges[rows - HALO :]
-    second_edges = lax.ppermute(jnp.where(core == 0, upper, lower), axes, back)
+    early_edges = lax.ppermute(jnp.where(core == 0, lower, upper), axes, ahead)
     head, tail = whole[:HALO], whole[rows - HALO :]
-    first = lax.ppermute(jnp.where(core == 0, tail, head), axes, ahead)
-    first_edges = lax.ppermute(jnp.where(core == 0, lower, upper), axes, ahead)
+    late_halo = lax.ppermute(jnp.where(core == 0, head, tail), axes, back)
+    late_edges = lax.ppermute(jnp.where(core == 0, upper, lower), axes, back)
     acc, turned = pl.pallas_call(
         own_kernel,
         out_shape=(
@@ -436,7 +436,7 @@
         pltpu.VMEM((2, half * cols // 2, basis * chans), BF16),
     ]
     limit = pltpu.CompilerParams(vmem_limit_bytes=32 * 1024 * 1024)
-    second, second_edges, acc = lax.optimization_barrier((second, second_edges, acc))
+    early_halo, early_edges, acc = lax.optimization_barrier((early_halo, early_edges, acc))
     early = pl.pallas_call(
         early_kernel,
         out_shape=sds((half, cols, chans), BF16),
@@ -448,8 +448,8 @@
             flops=300_000_000, bytes_accessed=1_000_000, transcendentals=0
         ),
         name="early_side",
-    )(second, second_edges, halo_weights, acc, mix)
-    first, first_edges, early = lax.optimization_barrier((first, first_edges, early))
+    )(early_halo, early_edges, halo_weights, acc, mix)
+    late_halo, late_edges, early = lax.optimization_barrier((late_halo, late_edges, early))
     return pl.pallas_call(
         late_kernel,
         out_shape=sds((rows, cols, chans), BF16),
@@ -462,7 +462,7 @@
         ],
         compiler_params=limit,
         name="late_side",
-    )(early, first, first_edges, halo_weights, acc, mix)
+    )(early, late_halo, late_edges, halo_weights, acc, mix)
 
 
 def solution(mesh):

time: 12.6 us -> 14.5 us (1.15)
  the two profiles are of different devices: /device:TPU:1 before, /device:TPU:0 now
where the time goes in v12:
time: 14.5 us; the launch traced here: 14.4 us
  Pallas kernels  6.08 us (42%)
  starting transfers between devices  5.1 us (35%)
  waiting for transfers between devices  1.99 us (14%)
  other arithmetic  1.11 us (8%)
    ppermute x1, starting transfers between devices, shards(): early_halo = lax.ppermute(going, axes, ahead)  2.59 us
    ppermute x1, starting transfers between devices, shards(): early_edges = lax.ppermute(jnp.where(core == 0, lower, upper), axes, ahead)  2.02 us
    pallas_call x1, Pallas kernels, shards(): pl.pallas_call(partner_kernel, out_shape=sds((rows, cols, chans), F32), i...  1.66 us
    pallas_call x1, Pallas kernels, shards(): pl.pallas_call(weight_kernel, out_shape=(sds((2, group // 2, HALO * SPAN)...  1.47 us
    pallas_call x1, Pallas kernels, shards(): pl.pallas_call(own_kernel, out_shape=(sds((rows, cols, chans), F32), sds(...  1.47 us
    pallas_call x1, Pallas kernels, shards(): pl.pallas_call(late_kernel, out_shape=sds((rows, cols, chans), BF16), in_...  1.42 us
    select_n x1, other arithmetic, shards(): going = jnp.where(core == 0, fields[rows - HALO:], fields[:HALO])  1.06 us
    ppermute x1, waiting for transfers between devices, shards(): late_halo = lax.ppermute(jnp.where(core == 0, head, tail), axes, back)  1.02 us
  transfers between devices with their start and end apart: 5, of which 2 were waited for; matrix products, arithmetic and copies ran while one was open for 8% of the time, Pallas kernels for 32%

profile of v12, /device:TPU:0, one launch (start us, length us, event | category | flops | bytes accessed | tf_op | source)
XLA Modules:
  0.0 14.4 jit_solution(16387918683983053129)
XLA Ops:
  0.0 0.5 %collective-permute-start.1 = (bf16[8,128,256]{2,1,0:T(8,128)(2,1)}, bf16[8,128,256]{2,1,0:T(8,128)(2,1)S(1)}, u32[]{:S(2)}, u32[]{:S(2)}) collective-permute-start(bf16[8,128,256]{2,1,0:T(8,128)(2,1)} %fields_in.1), channel_id=1, source_target_pairs={{0,4},{4,0},{1,5},{5,1},{2,6},{6,2},{3,7},{7,3},{8,12},{12,8},{9,1... | collective-permute-start | bytes 1572872 | tf_op jit(solution)/shard_map/ppermute | solution.py:341
  0.5 1.1 %slice_select_fusion.1 = bf16[4,128,256]{2,1,0:T(8,128)(2,1)S(1)} fusion(bf16[8,128,256]{2,1,0:T(8,128)(2,1)} %fields_in.1, pred[]{:T(512)S(6)} %eq.2), kind=kLoop, calls=%fused_computation.1 | loop fusion | flops 131072 | bytes 786433 | tf_op jit(solution)/shard_map/jit(_where)/select_n | solution.py:342
  1.5 2.6 %collective-permute-start.3 = (bf16[4,128,256]{2,1,0:T(8,128)(2,1)S(1)}, bf16[4,128,256]{2,1,0:T(8,128)(2,1)S(1)}, u32[]{:S(2)}, u32[]{:S(2)}) collective-permute-start(bf16[4,128,256]{2,1,0:T(8,128)(2,1)S(1)} %slice_select_fusion.1), channel_id=1, source_target_pairs={{0,8},{4,0},{8,16},{12,4},{16,24},{20,12},{24,28},{28,20},{1,9},{5... | collective-permute-start | bytes 786440 | tf_op jit(solution)/shard_map/ppermute | solution.py:343
  4.1 1.5 %filter_weights.1 = (bf16[2,256,128]{2,1,0:T(8,128)(2,1)S(1)}, bf16[512,256]{1,0:T(8,128)(2,1)S(1)}, bf16[128,256]{1,0:T(8,128)(2,1)S(1)}, bf16[4,8,256]{2,1,0:T...) custom-call(s32[8]{0:T(128)} %start_in, ...), custom_call_target="tpu_custom_call" | custom-call | flops 100000 | bytes 1000 | tf_op jit(solution)/shard_map/filter_weights/pallas_call | solution.py:352
  5.6 0.0 collective-permute-start
  5.7 0.0 collective-permute-done.1.other
  5.7 2.0 %collective-permute-start.4 = (bf16[4,8,256]{2,1,0:T(8,128)(2,1)S(1)}, bf16[4,8,256]{2,1,0:T(8,128)(2,1)S(1)}, u32[]{:S(2)}, u32[]{:S(2)}) collective-permute-start(bf16[4,8,256]{2,1,0:T(8,128)(2,1)S(1)} %get-tuple-element.39), channel_id=1, source_target_pairs={{0,8},{4,0},{8,16},{12,4},{16,24},{20,12},{24,28},{28,20},{1,9},{5... | collective-permute-start | bytes 49160 | tf_op jit(solution)/shard_map/ppermute | solution.py:391
  7.7 1.5 %own_rows.1 = (f32[8,128,256]{2,1,0:T(8,128)S(1)}, bf16[4,512,256]{2,1,0:T(8,128)(2,1)S(1)}) custom-call(bf16[4,512,256]{2,1,0:T(8,128)(2,1)S(1)} %get-tuple-element.23.turned_in, bf16[512,256]{1,0:T(8,128)(2,1)S(1)} %get-tuple-element.24.own_weights, bf16[4,8,256]{2,1,0:T(8,128)(2,1)S(1)} %get-tuple-element.25.cycle_taps, ...), custom_call_target="tpu_custom_call", output_to_operand_aliasing={{1}: (0, {})} | custom-call | flops 100000 | bytes 1000 | tf_op jit(solution)/shard_map/own_rows/pallas_call | solution.py:395
  9.2 0.0 collective-permute-start.2
  9.3 1.7 %partner_columns.1.acc = f32[8,128,256]{2,1,0:T(8,128)S(1)} custom-call(f32[8,128,256]{2,1,0:T(8,128)S(1)} %get-tuple-element.27.acc_in, bf16[512,256]{1,0:T(8,128)(2,1)S(1)} %get-tuple-element.24.own_weights, bf16[128,256]{1,0:T(8,128)(2,1)S(1)} %get-tuple-element.28.polar_weights, ...), custom_call_target="tpu_custom_call", output_to_operand_aliasing={{}: (0, {})} | custom-call | flops 100000 | bytes 1000 | tf_op jit(solution)/shard_map/partner_columns/pallas_call | solution.py:415
  10.9 0.0 collective-permute-done.3.halo
  10.9 0.0 collective-permute-done.4.edges
  11.0 1.0 %collective-permute-done.halo = bf16[4,128,256]{2,1,0:T(8,128)(2,1)S(1)} collective-permute-done((bf16[4,128,256]{2,1,0:T(8,128)(2,1)S(1)}, bf16[4,128,256]{2,1,0:T(8,128)(2,1)S(1)}, u32[]{:S(2)}, u32[]{:S(2)}) %collective-permute-start) | collective-permute-done | bytes 262176 | tf_op jit(solution)/shard_map/ppermute | solution.py:393
  12.0 1.0 %collective-permute-done.2.edges = bf16[4,8,256]{2,1,0:T(8,128)(2,1)S(1)} collective-permute-done((bf16[4,8,256]{2,1,0:T(8,128)(2,1)S(1)}, bf16[4,8,256]{2,1,0:T(8,128)(2,1)S(1)}, u32[]{:S(2)}, u32[]{:S(2)}) %collective-permute-start.2) | collective-permute-done | bytes 16416 | tf_op jit(solution)/shard_map/ppermute | solution.py:394
  13.0 1.4 %late_side.1 = bf16[8,128,256]{2,1,0:T(8,128)(2,1)} custom-call(bf16[4,128,256]{2,1,0:T(8,128)(2,1)S(1)} %early_side.1.early, bf16[4,128,256]{2,1,0:T(8,128)(2,1)S(1)} %collective-permute-done.halo, bf16[4,8,256]{2,1,0:T(8,128)(2,1)S(1)} %collective-permute-done.2.edges, bf16[2,256,128]{2,1,0:T(8,128)(2,1)S(1)} %get-tuple-element.32.weights, ...), custom_call_target="tpu_custom_call" | custom-call | tf_op jit(solution)/shard_map/late_side/pallas_call | solution.py:453
  (4 shorter events, 0.1 us)
Async XLA Ops:
  0.0 5.7 %collective-permute-start.1 = (bf16[8,128,256]{2,1,0:T(8,128)(2,1)}, bf16[8,128,256]{2,1,0:T(8,128)(2,1)S(1)}, u32[]{:S(2)}, u32[]{:S(2)}) collective-permute-start(bf16[8,128,256]{2,1,0:T(8,128)(2,1)} %fields_in.1), channel_id=1, source_target_pairs={{0,4},{4,0},{1,5},{5,1},{2,6},{6,2},{3,7},{7,3},{8,12},{12,8},{9,1... | collective-permute-start | bytes 1572872 | tf_op jit(solution)/shard_map/ppermute | solution.py:341
  1.5 9.4 %collective-permute-start.3 = (bf16[4,128,256]{2,1,0:T(8,128)(2,1)S(1)}, bf16[4,128,256]{2,1,0:T(8,128)(2,1)S(1)}, u32[]{:S(2)}, u32[]{:S(2)}) collective-permute-start(bf16[4,128,256]{2,1,0:T(8,128)(2,1)S(1)} %slice_select_fusion.1), channel_id=1, source_target_pairs={{0,8},{4,0},{8,16},{12,4},{16,24},{20,12},{24,28},{28,20},{1,9},{5... | collective-permute-start | bytes 786440 | tf_op jit(solution)/shard_map/ppermute | solution.py:343
  5.6 6.4 %collective-permute-start = (bf16[4,128,256]{2,1,0:T(8,128)(2,1)S(1)}, bf16[4,128,256]{2,1,0:T(8,128)(2,1)S(1)}, u32[]{:S(2)}, u32[]{:S(2)}) collective-permute-start(bf16[4,128,256]{2,1,0:T(8,128)(2,1)S(1)} %slice_select_fusion), channel_id=1, source_target_pairs={{0,4},{4,12},{8,0},{12,20},{16,8},{20,28},{24,16},{28,24},{1,5},{5... | collective-permute-start | bytes 786440 | tf_op jit(solution)/shard_map/ppermute | solution.py:393
  5.7 5.2 %collective-permute-start.4 = (bf16[4,8,256]{2,1,0:T(8,128)(2,1)S(1)}, bf16[4,8,256]{2,1,0:T(8,128)(2,1)S(1)}, u32[]{:S(2)}, u32[]{:S(2)}) collective-permute-start(bf16[4,8,256]{2,1,0:T(8,128)(2,1)S(1)} %get-tuple-element.39), channel_id=1, source_target_pairs={{0,8},{4,0},{8,16},{12,4},{16,24},{20,12},{24,28},{28,20},{1,9},{5... | collective-permute-start | bytes 49160 | tf_op jit(solution)/shard_map/ppermute | solution.py:391
  9.2 3.8 %collective-permute-start.2 = (bf16[4,8,256]{2,1,0:T(8,128)(2,1)S(1)}, bf16[4,8,256]{2,1,0:T(8,128)(2,1)S(1)}, u32[]{:S(2)}, u32[]{:S(2)}) collective-permute-start(bf16[4,8,256]{2,1,0:T(8,128)(2,1)S(1)} %get-tuple-element.40), channel_id=1, source_target_pairs={{0,4},{4,12},{8,0},{12,20},{16,8},{20,28},{24,16},{28,24},{1,5},{5... | collective-permute-start | bytes 49160 | tf_op jit(solution)/shard_map/ppermute | solution.py:394

commit v13 on v11

--- a/solution.py
+++ b/solution.py
@@ -166,6 +166,17 @@
     copies[6].wait()
 
 
+def pack_kernel(fields, other, message):
+    rows, cols, _ = fields.shape
+    reach = (message.shape[1] - cols) // 2
+    start = jnp.where(lax.axis_index("lon") == 0, rows - HALO, 0)
+    for p in range(HALO):
+        near = other[start + p]
+        message[p] = jnp.concatenate(
+            [near[cols - reach :], fields[start + p], near[:reach]], axis=0
+        )
+
+
 def own_kernel(turned_in, own_weights, cycle_taps, fields, mix, acc, turned, ext, hidden):
     del turned_in
     rows, cols, chans = fields.shape
@@ -254,21 +265,20 @@
 
 
 def side_rows(
-    side, halo, edges, weights, acc, mix, ext, hidden, present, result, ready=lambda at: None
+    side, halo, weights, acc, mix, ext, hidden, present, result, ready=lambda at: None
 ):
     half, cols, chans = result.shape
     basis = mix.shape[0] // chans
-    reach = edges.shape[1] // 2
     rows = pl.ds(side * half, half)
     wide = cols // 2
     parts = [slice(n * wide, (n + 1) * wide) for n in range(2)]
 
     @pl.when(present)
     def arrived():
-        pad = jnp.zeros((ext.shape[1] - cols - 2 * reach, chans), BF16)
         for p in range(HALO):
-            edge = edges[p]
-            ext[p] = jnp.concatenate([edge[reach:], halo[p], edge[:reach], pad], axis=0)
+            cells = halo(p)
+            pad = jnp.zeros((ext.shape[1] - cells.shape[0], chans), BF16)
+            ext[p] = jnp.concatenate([cells, pad], axis=0)
         groups = [(i, k) for k in range(basis) for i in range(half)]
         for n, part in enumerate(parts):
             for at in range(0, wide, BLOCK):
@@ -299,10 +309,16 @@
 
 def early_kernel(halo, edges, weights, acc, mix, result, ext, hidden):
     side, present = from_side(0)
-    side_rows(side, halo, edges, weights, acc, mix, ext, hidden, present, result)
-
-
-def late_kernel(early, halo, edges, weights, acc, mix, out, ext, hidden, result, sems):
+    reach = edges.shape[1] // 2
+
+    def cells(p):
+        edge = edges[p]
+        return jnp.concatenate([edge[reach:], halo[p], edge[:reach]], axis=0)
+
+    side_rows(side, cells, weights, acc, mix, ext, hidden, present, result)
+
+
+def late_kernel(early, halo, weights, acc, mix, out, ext, hidden, result, sems):
     half, cols, _ = result.shape
     side, present = from_side(1)
     rows = pl.ds(side * half, half)
@@ -317,7 +333,7 @@
     first = pltpu.make_async_copy(early, out.at[other_rows], sems.at[2])
     first.start()
     side_rows(
-        side, halo, edges, weights, acc, mix, ext, hidden, present, result,
+        side, lambda p: halo[p], weights, acc, mix, ext, hidden, present, result,
         lambda part: copy_of(part).start(),
     )
     first.wait()
@@ -349,6 +365,7 @@
     group = basis * rows * BLOCK
     ext_cols = cols + SPAN - BLOCK
     limit = pltpu.CompilerParams(vmem_limit_bytes=32 * 1024 * 1024)
+    small = pl.CostEstimate(flops=100_000, bytes_accessed=1_000, transcendentals=0)
     halo_weights, own_weights, polar_weights, turns, whole, mix, turned = pl.pallas_call(
         weight_kernel,
         out_shape=(
@@ -386,12 +403,19 @@
             )
         ),
     )
+    message = pl.pallas_call(
+        pack_kernel,
+        out_shape=sds((HALO, cols + 2 * reach, chans), BF16),
+        in_specs=[vmem] * 2,
+        out_specs=vmem,
+        compiler_params=limit,
+        cost_estimate=small,
+        name="late_message",
+    )(whole, other)
+    first = lax.ppermute(message, axes, ahead)
     edges = jnp.concatenate([other[:, :reach], other[:, cols - reach :]], axis=1)
     upper, lower = edges[:HALO], edges[rows - HALO :]
     second_edges = lax.ppermute(jnp.where(core == 0, upper, lower), axes, back)
-    head, tail = whole[:HALO], whole[rows - HALO :]
-    first = lax.ppermute(jnp.where(core == 0, tail, head), axes, ahead)
-    first_edges = lax.ppermute(jnp.where(core == 0, lower, upper), axes, ahead)
     acc, turned = pl.pallas_call(
         own_kernel,
         out_shape=(
@@ -449,11 +473,11 @@
         ),
         name="early_side",
     )(second, second_edges, halo_weights, acc, mix)
-    first, first_edges, early = lax.optimization_barrier((first, first_edges, early))
+    first, early = lax.optimization_barrier((first, early))
     return pl.pallas_call(
         late_kernel,
         out_shape=sds((rows, cols, chans), BF16),
-        in_specs=[vmem] * 6,
+        in_specs=[vmem] * 5,
         out_specs=hbm,
         scratch_shapes=[
             *scratch,
@@ -462,7 +486,7 @@
         ],
         compiler_params=limit,
         name="late_side",
-    )(early, first, first_edges, halo_weights, acc, mix)
+    )(early, first, halo_weights, acc, mix)
 
 
 def solution(mesh):

time: 12.6 us -> 12.6 us (level)
    ppermute x2 -> x1, waiting for transfers between devices: 0.83 us -> 0.82 us  [shards(): first = lax.ppermute(message, axes, ahead)]
  transfers between devices with their start and end apart: 5 -> 4, of which waited for: 2 -> 1; matrix products, arithmetic and copies ran while one was open for 9% -> 9% of each run, Pallas kernels for 37% -> 38%
where the time goes in v13:
time: 12.6 us; the launch traced here: 12.4 us
  Pallas kernels  6.12 us (49%)
  starting transfers between devices  4.3 us (34%)
  other arithmetic  1.08 us (9%)
  waiting for transfers between devices  0.83 us (7%)
    ppermute x1, starting transfers between devices, shards(): second = lax.ppermute(going, axes, back)  2.76 us
    pallas_call x1, Pallas kernels, shards(): pl.pallas_call(partner_kernel, out_shape=sds((rows, cols, chans), F32), i...  1.66 us
    pallas_call x1, Pallas kernels, shards(): pl.pallas_call(weight_kernel, out_shape=(sds((2, group // 2, HALO * SPAN)...  1.47 us
    pallas_call x1, Pallas kernels, shards(): pl.pallas_call(own_kernel, out_shape=(sds((rows, cols, chans), F32), sds(...  1.47 us
    ppermute x1, starting transfers between devices, shards(): second_edges = lax.ppermute(jnp.where(core == 0, upper, lower), axes, back)  1.46 us
    pallas_call x1, Pallas kernels, shards(): pl.pallas_call(late_kernel, out_shape=sds((rows, cols, chans), BF16), in_...  1.42 us
    select_n x1, other arithmetic, shards(): going = jnp.where(core == 0, fields[:HALO], fields[rows - HALO:])  1.06 us
    ppermute x1, waiting for transfers between devices, shards(): first = lax.ppermute(message, axes, ahead)  0.82 us
  transfers between devices with their start and end apart: 4, of which 1 were waited for; matrix products, arithmetic and copies ran while one was open for 9% of the time, Pallas kernels for 38%

profile of v13, /device:TPU:1, one launch (start us, length us, event | category | flops | bytes accessed | tf_op | source)
XLA Modules:
  0.0 12.4 jit_solution(11988900676792854494)
XLA Ops:
  0.0 0.1 collective-permute-start
  0.1 1.1 %slice_select_fusion = bf16[4,128,256]{2,1,0:T(8,128)(2,1)S(1)} fusion(bf16[8,128,256]{2,1,0:T(8,128)(2,1)} %fields_in.1, pred[]{:T(512)S(6)} %eq.4), kind=kLoop, calls=%fused_computation | loop fusion | flops 131072 | bytes 786433 | tf_op jit(solution)/shard_map/jit(_where)/select_n | solution.py:358
  1.1 2.8 %collective-permute-start.2 = (bf16[4,128,256]{2,1,0:T(8,128)(2,1)S(1)}, bf16[4,128,256]{2,1,0:T(8,128)(2,1)S(1)}, u32[]{:S(2)}, u32[]{:S(2)}) collective-permute-start(bf16[4,128,256]{2,1,0:T(8,128)(2,1)S(1)} %slice_select_fusion), channel_id=1, source_target_pairs={{0,4},{4,12},{8,0},{12,20},{16,8},{20,28},{24,16},{28,24},{1,5},{5... | collective-permute-start | bytes 786440 | tf_op jit(solution)/shard_map/ppermute | solution.py:359
  3.9 1.5 %filter_weights.1 = (bf16[2,256,128]{2,1,0:T(8,128)(2,1)S(1)}, bf16[512,256]{1,0:T(8,128)(2,1)S(1)}, bf16[128,256]{1,0:T(8,128)(2,1)S(1)}, bf16[4,8,256]{2,1,0:T...) custom-call(s32[8]{0:T(128)} %start_in, ...), custom_call_target="tpu_custom_call" | custom-call | flops 100000 | bytes 1000 | tf_op jit(solution)/shard_map/filter_weights/pallas_call | solution.py:369
  5.4 0.0 collective-permute-done.other
  5.4 0.0 collective-permute-start.1
  5.5 1.5 %collective-permute-start.3 = (bf16[4,8,256]{2,1,0:T(8,128)(2,1)S(1)}, bf16[4,8,256]{2,1,0:T(8,128)(2,1)S(1)}, u32[]{:S(2)}, u32[]{:S(2)}) collective-permute-start(bf16[4,8,256]{2,1,0:T(8,128)(2,1)S(1)} %fusion.1), channel_id=1, source_target_pairs={{0,4},{4,12},{8,0},{12,20},{16,8},{20,28},{24,16},{28,24},{1,5},{5... | collective-permute-start | bytes 49160 | tf_op jit(solution)/shard_map/ppermute | solution.py:418
  7.0 1.5 %own_rows.1 = (f32[8,128,256]{2,1,0:T(8,128)S(1)}, bf16[4,512,256]{2,1,0:T(8,128)(2,1)S(1)}) custom-call(bf16[4,512,256]{2,1,0:T(8,128)(2,1)S(1)} %get-tuple-element.22.turned_in, bf16[512,256]{1,0:T(8,128)(2,1)S(1)} %get-tuple-element.23.own_weights, bf16[4,8,256]{2,1,0:T(8,128)(2,1)S(1)} %get-tuple-element.24.cycle_taps, ...), custom_call_target="tpu_custom_call", output_to_operand_aliasing={{1}: (0, {})} | custom-call | flops 100000 | bytes 1000 | tf_op jit(solution)/shard_map/own_rows/pallas_call | solution.py:419
  8.5 1.7 %partner_columns.1.acc = f32[8,128,256]{2,1,0:T(8,128)S(1)} custom-call(f32[8,128,256]{2,1,0:T(8,128)S(1)} %get-tuple-element.26.acc_in, bf16[512,256]{1,0:T(8,128)(2,1)S(1)} %get-tuple-element.23.own_weights, bf16[128,256]{1,0:T(8,128)(2,1)S(1)} %get-tuple-element.27.polar_weights, ...), custom_call_target="tpu_custom_call", output_to_operand_aliasing={{}: (0, {})} | custom-call | flops 100000 | bytes 1000 | tf_op jit(solution)/shard_map/partner_columns/pallas_call | solution.py:439
  10.1 0.0 collective-permute-done.2.halo
  10.1 0.0 collective-permute-done.3.edges
  10.2 0.8 %collective-permute-done.1.halo = bf16[4,136,256]{2,1,0:T(8,128)(2,1)S(1)} collective-permute-done((bf16[4,136,256]{2,1,0:T(8,128)(2,1)S(1)}, bf16[4,136,256]{2,1,0:T(8,128)(2,1)S(1)}, u32[]{:S(2)}, u32[]{:S(2)}) %collective-permute-start.1) | collective-permute-done | bytes 278560 | tf_op jit(solution)/shard_map/ppermute | solution.py:415
  11.0 1.4 %late_side.1 = bf16[8,128,256]{2,1,0:T(8,128)(2,1)} custom-call(bf16[4,128,256]{2,1,0:T(8,128)(2,1)S(1)} %early_side.1.early, bf16[4,136,256]{2,1,0:T(8,128)(2,1)S(1)} %collective-permute-done.1.halo, bf16[2,256,128]{2,1,0:T(8,128)(2,1)S(1)} %get-tuple-element.31.weights, f32[8,128,256]{2,1,0:T(8,128)S(1)} %partner_columns.1.acc, ...), custom_call_target="tpu_custom_call" | custom-call | tf_op jit(solution)/shard_map/late_side/pallas_call | solution.py:477
  (4 shorter events, 0.1 us)
Async XLA Ops:
  0.0 5.4 %collective-permute-start = (bf16[8,128,256]{2,1,0:T(8,128)(2,1)}, bf16[8,128,256]{2,1,0:T(8,128)(2,1)S(1)}, u32[]{:S(2)}, u32[]{:S(2)}) collective-permute-start(bf16[8,128,256]{2,1,0:T(8,128)(2,1)} %fields_in.1), channel_id=1, source_target_pairs={{0,4},{4,0},{1,5},{5,1},{2,6},{6,2},{3,7},{7,3},{8,12},{12,8},{9,1... | collective-permute-start | bytes 1572872 | tf_op jit(solution)/shard_map/ppermute | solution.py:357
  1.1 9.0 %collective-permute-start.2 = (bf16[4,128,256]{2,1,0:T(8,128)(2,1)S(1)}, bf16[4,128,256]{2,1,0:T(8,128)(2,1)S(1)}, u32[]{:S(2)}, u32[]{:S(2)}) collective-permute-start(bf16[4,128,256]{2,1,0:T(8,128)(2,1)S(1)} %slice_select_fusion), channel_id=1, source_target_pairs={{0,4},{4,12},{8,0},{12,20},{16,8},{20,28},{24,16},{28,24},{1,5},{5... | collective-permute-start | bytes 786440 | tf_op jit(solution)/shard_map/ppermute | solution.py:359
  5.4 5.6 %collective-permute-start.1 = (bf16[4,136,256]{2,1,0:T(8,128)(2,1)S(1)}, bf16[4,136,256]{2,1,0:T(8,128)(2,1)S(1)}, u32[]{:S(2)}, u32[]{:S(2)}) collective-permute-start(bf16[4,136,256]{2,1,0:T(8,128)(2,1)S(1)} %late_message.1), channel_id=1, source_target_pairs={{0,8},{4,0},{8,16},{12,4},{16,24},{20,12},{24,28},{28,20},{1,9},{5... | collective-permute-start | bytes 835592 | tf_op jit(solution)/shard_map/ppermute | solution.py:415
  5.5 4.6 %collective-permute-start.3 = (bf16[4,8,256]{2,1,0:T(8,128)(2,1)S(1)}, bf16[4,8,256]{2,1,0:T(8,128)(2,1)S(1)}, u32[]{:S(2)}, u32[]{:S(2)}) collective-permute-start(bf16[4,8,256]{2,1,0:T(8,128)(2,1)S(1)} %fusion.1), channel_id=1, source_target_pairs={{0,4},{4,12},{8,0},{12,20},{16,8},{20,28},{24,16},{28,24},{1,5},{5... | collective-permute-start | bytes 49160 | tf_op jit(solution)/shard_map/ppermute | solution.py:418

commit v14 on v13

--- a/solution.py
+++ b/solution.py
@@ -1,3 +1,5 @@
+import functools
+
 import jax
 import jax.numpy as jnp
 from jax import lax
@@ -64,11 +66,13 @@
 
 
 def weight_kernel(
-    start_in, width_in, lon_in, lat_in, fields_in, cycle_in, mixing_in,
-    halo_weights, own_weights, polar_weights, cycle_taps, fields, mix, turned,
-    start, width, lon, lat, lon_wide, lat_wide, sems,
+    late, start_in, width_in, lon_in, lat_in, cycle_in, mixing_in, *refs,
 ):
-    rows, cols, chans = fields.shape
+    if late:
+        refs = refs[6:]
+    halo_weights, own_weights, polar_weights, cycle_taps, mix, turned = refs[:6]
+    start, width, lon, lat, lon_wide, lat_wide, sems = refs[6:]
+    rows = halo_weights.shape[0] * HALO
     taps, basis, row_total = lon.shape
     band = lat.shape[0]
     polar = cycle_taps.shape[1] // 2
@@ -76,105 +80,123 @@
     base = lat_pos * rows
     at_top = base == 0
 
-    copies = []
-    for n, (source, target) in enumerate(
-        [
-            (lon_in, lon), (lat_in, lat), (start_in, start), (width_in, width),
-            (fields_in, fields), (cycle_in, cycle_taps), (mixing_in, mix),
+    is_early = at_top & (lax.axis_index("lon") == 0)
+
+    @pl.when(jnp.logical_not(is_early) if late else is_early)
+    def make():
+        copies = []
+        for n, (source, target) in enumerate(
+            [
+                (lon_in, lon), (lat_in, lat), (start_in, start), (width_in, width),
+                (cycle_in, cycle_taps), (mixing_in, mix),
+            ]
+        ):
+            copies.append(pltpu.make_async_copy(source, target, sems.at[n]))
+            copies[-1].start()
+        lon_wide[...] = jnp.zeros_like(lon_wide)
+        lat_wide[...] = jnp.zeros_like(lat_wide)
+        for n in range(4):
+            copies[n].wait()
+
+        for d in range(taps):
+            for k in range(basis):
+                lon_wide[k * 16 + d : k * 16 + d + 1, 0:row_total] = lon[d, k : k + 1, :]
+        lanes = lon_wide.shape[1]
+        slots = pltpu.roll(lon_wide[...], lax.rem(lanes + HALO - base, lanes), 1)[:, :128]
+        slots = jnp.transpose(slots)[: rows + 2 * HALO]
+        is_tap = lax.broadcasted_iota(jnp.int32, slots.shape, 1) < taps
+        own_taps, halo_taps = [], []
+        for k in range(basis):
+            moved = slots if k == 0 else pltpu.roll(slots, 128 - 16 * k, 1)
+            moved = jnp.where(is_tap, moved, 0.0)
+            for _ in range(2):
+                moved = pltpu.roll(moved, 0, 1, stride=SPAN // 2, stride_axis=0)
+            quads = [jnp.sum(moved[4 * q : 4 * q + 4], axis=0, keepdims=True) for q in range(4)]
+            own_taps.append(jnp.concatenate([quads[1], quads[2]], axis=1))
+            halo_taps.append(jnp.concatenate([quads[0], quads[3]], axis=1))
+
+        for t in range(band):
+            lat_wide[t * basis : (t + 1) * basis, 0:rows] = lat[t].astype(F32)
+        lat_cols = jnp.transpose(lat_wide[...])[:rows]
+        shape = (rows, rows * SPAN)
+        lane = lax.broadcasted_iota(jnp.int32, shape, 1)
+        out_row = lax.broadcasted_iota(jnp.int32, shape, 0)
+        first = jnp.zeros(shape, jnp.int32)
+        count = jnp.zeros(shape, jnp.int32)
+        for i in range(rows):
+            first = jnp.where(out_row == i, start[i], first)
+            count = jnp.where(out_row == i, width[i], count)
+        spread = [
+            [
+                jnp.broadcast_to(lat_cols[:, t * basis + k : t * basis + k + 1], shape)
+                for k in range(basis)
+            ]
+            for t in range(band)
         ]
-    ):
-        copies.append(pltpu.make_async_copy(source, target, sems.at[n]))
-        copies[-1].start()
-    lon_wide[...] = jnp.zeros_like(lon_wide)
-    lat_wide[...] = jnp.zeros_like(lat_wide)
-    for n in range(4):
-        copies[n].wait()
-
-    for d in range(taps):
+        slot = lane // SPAN
+        own_row = base + slot
+        halo_row = jnp.where(slot < HALO, own_row - HALO, own_row + rows - HALO)
+        is_polar = (own_row < polar) | (own_row >= row_total - polar)
+        in_grid = (halo_row >= 0) & (halo_row < row_total)
+        own_step, halo_step = own_row - first, halo_row - first
+        own_used = [(own_step == t) & (count > t) & ~is_polar for t in range(band)]
+        halo_used = [(halo_step == t) & (count > t) & in_grid for t in range(band)]
         for k in range(basis):
-            lon_wide[k * 16 + d : k * 16 + d + 1, 0:row_total] = lon[d, k : k + 1, :]
-    lanes = lon_wide.shape[1]
-    slots = pltpu.roll(lon_wide[...], lax.rem(lanes + HALO - base, lanes), 1)[:, :128]
-    slots = jnp.transpose(slots)[: rows + 2 * HALO]
-    is_tap = lax.broadcasted_iota(jnp.int32, slots.shape, 1) < taps
-    own_taps, halo_taps = [], []
-    for k in range(basis):
-        moved = slots if k == 0 else pltpu.roll(slots, 128 - 16 * k, 1)
-        moved = jnp.where(is_tap, moved, 0.0)
-        for _ in range(2):
-            moved = pltpu.roll(moved, 0, 1, stride=SPAN // 2, stride_axis=0)
-        quads = [jnp.sum(moved[4 * q : 4 * q + 4], axis=0, keepdims=True) for q in range(4)]
-        own_taps.append(jnp.concatenate([quads[1], quads[2]], axis=1))
-        halo_taps.append(jnp.concatenate([quads[0], quads[3]], axis=1))
-
-    for t in range(band):
-        lat_wide[t * basis : (t + 1) * basis, 0:rows] = lat[t].astype(F32)
-    lat_cols = jnp.transpose(lat_wide[...])[:rows]
-    shape = (rows, rows * SPAN)
-    lane = lax.broadcasted_iota(jnp.int32, shape, 1)
-    out_row = lax.broadcasted_iota(jnp.int32, shape, 0)
-    first = jnp.zeros(shape, jnp.int32)
-    count = jnp.zeros(shape, jnp.int32)
-    for i in range(rows):
-        first = jnp.where(out_row == i, start[i], first)
-        count = jnp.where(out_row == i, width[i], count)
-    spread = [
-        [
-            jnp.broadcast_to(lat_cols[:, t * basis + k : t * basis + k + 1], shape)
-            for k in range(basis)
-        ]
-        for t in range(band)
-    ]
-    slot = lane // SPAN
-    own_row = base + slot
-    halo_row = jnp.where(slot < HALO, own_row - HALO, own_row + rows - HALO)
-    is_polar = (own_row < polar) | (own_row >= row_total - polar)
-    in_grid = (halo_row >= 0) & (halo_row < row_total)
-    own_step, halo_step = own_row - first, halo_row - first
-    own_used = [(own_step == t) & (count > t) & ~is_polar for t in range(band)]
-    halo_used = [(halo_step == t) & (count > t) & in_grid for t in range(band)]
-    for k in range(basis):
-        own_line = own_taps[k] * chosen([(own_used[t], spread[t][k]) for t in range(band)])
-        halo_line = halo_taps[k] * chosen([(halo_used[t], spread[t][k]) for t in range(band)])
+            own_line = own_taps[k] * chosen([(own_used[t], spread[t][k]) for t in range(band)])
+            halo_line = halo_taps[k] * chosen([(halo_used[t], spread[t][k]) for t in range(band)])
+            for i in range(rows):
+                at = (k * rows + i) * BLOCK
+                own_weights[at : at + BLOCK, :] = staircase(own_line[i : i + 1], BLOCK)
+                side, at = i // HALO, (k * HALO + i % HALO) * BLOCK
+                reached = halo_line[i : i + 1, side * HALO * SPAN : (side + 1) * HALO * SPAN]
+                halo_weights[side, at : at + BLOCK, :] = staircase(reached, BLOCK)
+
+        offset = jnp.where(at_top, 0, rows - polar)
+        of_basis = lane // (polar * BLOCK)
+        step = base + offset + lax.rem(lane // BLOCK, polar) - first
+        at_start = lax.rem(lane, BLOCK) == 0
+        terms = []
+        for t in range(band):
+            value = spread[t][0]
+            for k in range(1, basis):
+                value = jnp.where(of_basis == k, spread[t][k], value)
+            terms.append(((step == t) & (count > t) & at_start, value))
+        line = chosen(terms)
         for i in range(rows):
-            at = (k * rows + i) * BLOCK
-            own_weights[at : at + BLOCK, :] = staircase(own_line[i : i + 1], BLOCK)
-            side, at = i // HALO, (k * HALO + i % HALO) * BLOCK
-            reached = halo_line[i : i + 1, side * HALO * SPAN : (side + 1) * HALO * SPAN]
-            halo_weights[side, at : at + BLOCK, :] = staircase(reached, BLOCK)
-
-    offset = jnp.where(at_top, 0, rows - polar)
-    of_basis = lane // (polar * BLOCK)
-    step = base + offset + lax.rem(lane // BLOCK, polar) - first
-    at_start = lax.rem(lane, BLOCK) == 0
-    terms = []
-    for t in range(band):
-        value = spread[t][0]
-        for k in range(1, basis):
-            value = jnp.where(of_basis == k, spread[t][k], value)
-        terms.append(((step == t) & (count > t) & at_start, value))
-    line = chosen(terms)
-    for i in range(rows):
-        polar_weights[i * BLOCK : (i + 1) * BLOCK, :] = staircase(line[i : i + 1], BLOCK)
-    copies[5].wait()
-
-    @pl.when(at_top & (lax.axis_index("lon") == 0))
-    def top():
-        polar_matrices(cycle_taps, turned, True)
-
-    copies[4].wait()
-    copies[6].wait()
-
-
-def pack_kernel(fields, other, message):
-    rows, cols, _ = fields.shape
-    reach = (message.shape[1] - cols) // 2
+            polar_weights[i * BLOCK : (i + 1) * BLOCK, :] = staircase(line[i : i + 1], BLOCK)
+        copies[4].wait()
+
+        @pl.when(at_top & (lax.axis_index("lon") == 0))
+        def top():
+            polar_matrices(cycle_taps, turned, True)
+
+        copies[5].wait()
+
+
+def stage_kernel(going, staying, whole, edges, polar_left, polar_right):
+    cols = whole.shape[1]
+    reach = edges.shape[1] // 2
+    is_first = lax.axis_index("lon") == 0
+    at_top = lax.axis_index("lat") == 0
+    for p in range(HALO):
+        upper = jnp.where(is_first, going[p], staying[p])
+        lower = jnp.where(is_first, staying[p], going[p])
+        polar = jnp.where(at_top, upper, lower)
+        polar_left[p], polar_right[p] = polar[: cols // 2], polar[cols // 2 :]
+        for r, row in ((p, upper), (HALO + p, lower)):
+            whole[r] = row
+            edges[r] = jnp.concatenate([row[:reach], row[cols - reach :]], axis=0)
+
+
+def pack_kernel(whole, edges, message, corners):
+    rows = whole.shape[0]
+    reach = edges.shape[1] // 2
     start = jnp.where(lax.axis_index("lon") == 0, rows - HALO, 0)
+    early = rows - HALO - start
     for p in range(HALO):
-        near = other[start + p]
-        message[p] = jnp.concatenate(
-            [near[cols - reach :], fields[start + p], near[:reach]], axis=0
-        )
+        near = edges[start + p]
+        message[p] = jnp.concatenate([near[reach:], whole[start + p], near[:reach]], axis=0)
+        corners[p] = edges[early + p]
 
 
 def own_kernel(turned_in, own_weights, cycle_taps, fields, mix, acc, turned, ext, hidden):
@@ -213,7 +235,7 @@
 
 
 def partner_kernel(
-    acc_in, own_weights, polar_weights, turned, fields, mix, other,
+    acc_in, own_weights, polar_weights, turned, fields, mix, edges, polar_left, polar_right,
     acc, hidden, cycle_rows, mixed_rows,
 ):
     del acc_in
@@ -229,11 +251,11 @@
     pad = jnp.zeros((SPAN - BLOCK - 2 * reach, chans), BF16)
     for r in range(rows):
         left.append(
-            jnp.concatenate([other[r, cols - reach :], fields[r, : SPAN - reach]], axis=0)
+            jnp.concatenate([edges[r, reach:], fields[r, : SPAN - reach]], axis=0)
         )
         right.append(
             jnp.concatenate(
-                [fields[r, cols - BLOCK - reach :], other[r, :reach], pad], axis=0
+                [fields[r, cols - BLOCK - reach :], edges[r, :reach], pad], axis=0
             )
         )
     for n, cells in enumerate((left, right)):
@@ -249,7 +271,9 @@
     def polar_part():
         offset = jnp.where(at_top, 0, rows - polar)
         for p in range(polar):
-            whole = jnp.concatenate([fields[offset + p], other[offset + p]], axis=0)
+            whole = jnp.concatenate(
+                [fields[offset + p], polar_left[p], polar_right[p]], axis=0
+            )
             part = matmul(turned[p], whole).astype(BF16)
             for k in range(basis):
                 cycle_rows[k, p * cols : (p + 1) * cols, :] = part[k * cols : (k + 1) * cols]
@@ -352,12 +376,13 @@
     core = lax.axis_index("lon")
     axes = ("lat", "lon")
     assert cycle == 2 * cols and rows == 2 * HALO and basis * polar * BLOCK == rows * SPAN
-    assert reach == (SPAN - BLOCK) // 4
+    assert reach == (SPAN - BLOCK) // 4 and polar == HALO
     ahead, back = ring(lat_count, 1), ring(lat_count, -1)
-    other = lax.ppermute(fields, "lon", SWAP)
-    going = jnp.where(core == 0, fields[:HALO], fields[rows - HALO :])
+    head, tail = fields[:HALO], fields[rows - HALO :]
+    going = jnp.where(core == 0, head, tail)
+    staying = jnp.where(core == 0, tail, head)
     second = lax.ppermute(going, axes, back)
-    going, band_start = lax.optimization_barrier((going, band_start))
+    going, staying, band_start = lax.optimization_barrier((going, staying, band_start))
 
     vmem = pl.BlockSpec(memory_space=pltpu.VMEM)
     hbm = pl.BlockSpec(memory_space=pltpu.HBM)
@@ -366,56 +391,80 @@
     ext_cols = cols + SPAN - BLOCK
     limit = pltpu.CompilerParams(vmem_limit_bytes=32 * 1024 * 1024)
     small = pl.CostEstimate(flops=100_000, bytes_accessed=1_000, transcendentals=0)
-    halo_weights, own_weights, polar_weights, turns, whole, mix, turned = pl.pallas_call(
-        weight_kernel,
-        out_shape=(
-            sds((2, group // 2, HALO * SPAN), BF16),
-            sds((group, rows * SPAN), BF16),
-            sds((rows * BLOCK, rows * SPAN), BF16),
-            sds((basis, 2 * polar, cycle), BF16),
-            sds((rows, cols, chans), BF16),
-            sds((basis * chans, chans), BF16),
-            sds((polar, basis * cols, cycle), BF16),
-        ),
-        in_specs=[hbm] * 7,
-        out_specs=[vmem] * 7,
-        scratch_shapes=[
-            pltpu.SMEM((rows,), jnp.int32),
-            pltpu.SMEM((rows,), jnp.int32),
-            pltpu.VMEM((taps, basis, row_total), F32),
-            pltpu.VMEM((band, basis, rows), BF16),
-            pltpu.VMEM((128, -(-row_total // 128) * 128), F32),
-            pltpu.VMEM((128, 128), F32),
-            pltpu.SemaphoreType.DMA((7,)),
-        ],
-        compiler_params=limit,
-        cost_estimate=pl.CostEstimate(
-            flops=100_000, bytes_accessed=1_000, transcendentals=0
-        ),
-        name="filter_weights",
-    )(
-        *(
+    large = pl.CostEstimate(flops=1_600_000_000, bytes_accessed=1_000, transcendentals=0)
+    weight_shapes = (
+        sds((2, group // 2, HALO * SPAN), BF16),
+        sds((group, rows * SPAN), BF16),
+        sds((rows * BLOCK, rows * SPAN), BF16),
+        sds((basis, 2 * polar, cycle), BF16),
+        sds((basis * chans, chans), BF16),
+        sds((polar, basis * cols, cycle), BF16),
+    )
+
+    def weights(made):
+        operands = [
             pltpu.with_memory_space_constraint(x, pltpu.HBM)
             for x in (
                 band_start, band_width, jnp.transpose(lon_taps, (2, 1, 0)),
-                jnp.transpose(lat_taps, (2, 1, 0)), fields, cycle_taps,
+                jnp.transpose(lat_taps, (2, 1, 0)), cycle_taps,
                 mixing.reshape(basis * chans, chans),
             )
+        ]
+        return pl.pallas_call(
+            functools.partial(weight_kernel, bool(made)),
+            out_shape=weight_shapes,
+            in_specs=[hbm] * 6 + [vmem] * len(made),
+            out_specs=[vmem] * 6,
+            input_output_aliases={6 + n: n for n in range(len(made))},
+            scratch_shapes=[
+                pltpu.SMEM((rows,), jnp.int32),
+                pltpu.SMEM((rows,), jnp.int32),
+                pltpu.VMEM((taps, basis, row_total), F32),
+                pltpu.VMEM((band, basis, rows), BF16),
+                pltpu.VMEM((128, -(-row_total // 128) * 128), F32),
+                pltpu.VMEM((128, 128), F32),
+                pltpu.SemaphoreType.DMA((6,)),
+            ],
+            compiler_params=limit,
+            cost_estimate=small,
+            name="filter_weights" if made else "first_weights",
+        )(*operands, *made)
+
+    made = weights(())
+    going, made = lax.optimization_barrier((going, made))
+    whole, edges, polar_left, polar_right = pl.pallas_call(
+        stage_kernel,
+        out_shape=(
+            sds((rows, cols, chans), BF16),
+            sds((rows, 2 * reach, chans), BF16),
+            sds((polar, cols // 2, chans), BF16),
+            sds((polar, cols // 2, chans), BF16),
         ),
-    )
-    message = pl.pallas_call(
-        pack_kernel,
-        out_shape=sds((HALO, cols + 2 * reach, chans), BF16),
         in_specs=[vmem] * 2,
-        out_specs=vmem,
+        out_specs=[vmem] * 4,
         compiler_params=limit,
         cost_estimate=small,
-        name="late_message",
-    )(whole, other)
+        name="stage_rows",
+    )(going, staying)
+    edges = lax.ppermute(edges, "lon", SWAP)
+    polar_left = lax.ppermute(polar_left, "lon", SWAP)
+    polar_right = lax.ppermute(polar_right, "lon", SWAP)
+    message, corners = pl.pallas_call(
+        pack_kernel,
+        out_shape=(
+            sds((HALO, cols + 2 * reach, chans), BF16),
+            sds((HALO, 2 * reach, chans), BF16),
+        ),
+        in_specs=[vmem] * 2,
+        out_specs=(vmem, vmem),
+        compiler_params=limit,
+        cost_estimate=small,
+        name="pack_messages",
+    )(whole, edges)
     first = lax.ppermute(message, axes, ahead)
-    edges = jnp.concatenate([other[:, :reach], other[:, cols - reach :]], axis=1)
-    upper, lower = edges[:HALO], edges[rows - HALO :]
-    second_edges = lax.ppermute(jnp.where(core == 0, upper, lower), axes, back)
+    second_edges = lax.ppermute(corners, axes, back)
+    corners, made = lax.optimization_barrier((corners, made))
+    halo_weights, own_weights, polar_weights, turns, mix, turned = weights(made)
     acc, turned = pl.pallas_call(
         own_kernel,
         out_shape=(
@@ -439,7 +488,7 @@
     acc = pl.pallas_call(
         partner_kernel,
         out_shape=sds((rows, cols, chans), F32),
-        in_specs=[vmem] * 7,
+        in_specs=[vmem] * 9,
         out_specs=vmem,
         input_output_aliases={0: 0},
         scratch_shapes=[
@@ -452,7 +501,7 @@
             flops=100_000, bytes_accessed=1_000, transcendentals=0
         ),
         name="partner_columns",
-    )(acc, own_weights, polar_weights, turned, whole, mix, other)
+    )(acc, own_weights, polar_weights, turned, whole, mix, edges, polar_left, polar_right)
 
     half = rows // 2
     scratch = [
@@ -468,9 +517,7 @@
         out_specs=vmem,
         scratch_shapes=scratch,
         compiler_params=limit,
-        cost_estimate=pl.CostEstimate(
-            flops=300_000_000, bytes_accessed=1_000_000, transcendentals=0
-        ),
+        cost_estimate=large,
         name="early_side",
     )(second, second_edges, halo_weights, acc, mix)
     first, early = lax.optimization_barrier((first, early))

time: 12.6 us -> 12.6 us (level)
  waiting for transfers between devices: 0.83 us -> 0.55 us
  starting transfers between devices: 4.3 us -> 4.47 us
    ppermute x1, waiting for transfers between devices: 0.82 us -> 0.12 us  [shards(): first = lax.ppermute(message, axes, ahead)]
    ppermute x1, starting transfers between devices: 2.76 us -> 2.14 us  [shards(): second = lax.ppermute(going, axes, back)]
    ppermute x2 -> x4, starting transfers between devices: 1.52 us -> 2.04 us  [the longest x1 1.19 us: shards(): second_edges = lax.ppermute(corners, axes, back)]
    ppermute x2 -> x4, waiting for transfers between devices: 0.01 us -> 0.43 us  [the longest x1 0.42 us: shards(): edges = lax.ppermute(edges, 'lon', SWAP)]
    ppermute x1, starting transfers between devices: 0.02 us -> 0.29 us  [shards(): first = lax.ppermute(message, axes, ahead)]
    pallas_call x2 -> x4, Pallas kernels: 1.52 us -> 1.61 us  [the longest x2 1.51 us: weights(): pl.pallas_call(functools.partial(weight_kernel, bool(made)), out_shape=we...]
    select_n x2 -> x1, other arithmetic: 1.08 us -> 1.07 us  [shards(): staying = jnp.where(core == 0, tail, head)]
  transfers between devices with their start and end apart: 4 -> 6, of which waited for: 1 -> 2; matrix products, arithmetic and copies ran while one was open for 9% -> 0% of each run, Pallas kernels for 38% -> 39%
where the time goes in v14:
time: 12.6 us; the launch traced here: 12.4 us
  Pallas kernels  6.23 us (49%)
  starting transfers between devices  4.47 us (35%)
  other arithmetic  1.07 us (8%)
  waiting for transfers between devices  0.55 us (4%)
    ppermute x1, starting transfers between devices, shards(): second = lax.ppermute(going, axes, back)  2.14 us
    pallas_call x1, Pallas kernels, shards(): pl.pallas_call(partner_kernel, out_shape=sds((rows, cols, chans), F32), i...  1.66 us
    pallas_call x2, Pallas kernels, weights(): pl.pallas_call(functools.partial(weight_kernel, bool(made)), out_shape=we...  1.51 us
    pallas_call x1, Pallas kernels, shards(): pl.pallas_call(own_kernel, out_shape=(sds((rows, cols, chans), F32), sds(...  1.48 us
    pallas_call x1, Pallas kernels, shards(): pl.pallas_call(late_kernel, out_shape=sds((rows, cols, chans), BF16), in_...  1.42 us
    ppermute x1, starting transfers between devices, shards(): second_edges = lax.ppermute(corners, axes, back)  1.19 us
    select_n x1, other arithmetic, shards(): staying = jnp.where(core == 0, tail, head)  1.07 us
    ppermute x1, waiting for transfers between devices, shards(): edges = lax.ppermute(edges, 'lon', SWAP)  0.42 us
  transfers between devices with their start and end apart: 6, of which 2 were waited for; matrix products, arithmetic and copies ran while one was open for 0% of the time, Pallas kernels for 39%

profile of v14, /device:TPU:1, one launch (start us, length us, event | category | flops | bytes accessed | tf_op | source)
XLA Modules:
  0.0 12.4 jit_solution(14671557803141576055)
XLA Ops:
  0.0 1.1 %broadcast_select_fusion = (bf16[4,128,256]{2,1,0:T(8,128)(2,1)S(1)}, bf16[4,128,256]{2,1,0:T(8,128)(2,1)S(1)}) fusion(pred[]{:T(512)S(6)} %eq.4, bf16[8,128,256]{2,1,0:T(8,128)(2,1)} %param.7), kind=kLoop, calls=%fused_computation | loop fusion | flops 262144 | bytes 1048577 | tf_op jit(solution)/shard_map/jit(_where)/select_n | solution.py:383
  1.1 2.1 %collective-permute-start.2 = (bf16[4,128,256]{2,1,0:T(8,128)(2,1)S(1)}, bf16[4,128,256]{2,1,0:T(8,128)(2,1)S(1)}, u32[]{:S(2)}, u32[]{:S(2)}) collective-permute-start(bf16[4,128,256]{2,1,0:T(8,128)(2,1)S(1)} %get-tuple-element.54.going), channel_id=1, source_target_pairs={{0,4},{4,12},{8,0},{12,20},{16,8},{20,28},{24,16},{28,24},{1,5},{5... | collective-permute-start | bytes 786440 | tf_op jit(solution)/shard_map/ppermute | solution.py:384
  3.2 0.1 first_weights.1
  3.3 0.1 stage_rows.1
  3.4 0.3 %collective-permute-start = (bf16[8,8,256]{2,1,0:T(8,128)(2,1)S(1)}, bf16[8,8,256]{2,1,0:T(8,128)(2,1)S(1)}, u32[]{:S(2)}, u32[]{:S(2)}) collective-permute-start(bf16[8,8,256]{2,1,0:T(8,128)(2,1)S(1)} %get-tuple-element.57), channel_id=1, source_target_pairs={{0,4},{4,0},{1,5},{5,1},{2,6},{6,2},{3,7},{7,3},{8,12},{12,8},{9,1... | collective-permute-start | bytes 98312 | tf_op jit(solution)/shard_map/ppermute | solution.py:449
  3.7 0.2 %collective-permute-start.4 = (bf16[4,64,256]{2,1,0:T(8,128)(2,1)S(1)}, bf16[4,64,256]{2,1,0:T(8,128)(2,1)S(1)}, u32[]{:S(2)}, u32[]{:S(2)}) collective-permute-start(bf16[4,64,256]{2,1,0:T(8,128)(2,1)S(1)} %get-tuple-element.79), channel_id=1, source_target_pairs={{0,4},{4,0},{1,5},{5,1},{2,6},{6,2},{3,7},{7,3},{8,12},{12,8},{9,1... | collective-permute-start | bytes 393224 | tf_op jit(solution)/shard_map/ppermute | solution.py:450
  3.9 0.3 %collective-permute-start.5 = (bf16[4,64,256]{2,1,0:T(8,128)(2,1)S(1)}, bf16[4,64,256]{2,1,0:T(8,128)(2,1)S(1)}, u32[]{:S(2)}, u32[]{:S(2)}) collective-permute-start(bf16[4,64,256]{2,1,0:T(8,128)(2,1)S(1)} %get-tuple-element.80), channel_id=1, source_target_pairs={{0,4},{4,0},{1,5},{5,1},{2,6},{6,2},{3,7},{7,3},{8,12},{12,8},{9,1... | collective-permute-start | bytes 393224 | tf_op jit(solution)/shard_map/ppermute | solution.py:451
  4.2 0.4 %collective-permute-done.edges = bf16[8,8,256]{2,1,0:T(8,128)(2,1)S(1)} collective-permute-done((bf16[8,8,256]{2,1,0:T(8,128)(2,1)S(1)}, bf16[8,8,256]{2,1,0:T(8,128)(2,1)S(1)}, u32[]{:S(2)}, u32[]{:S(2)}) %collective-permute-start) | collective-permute-done | bytes 32800 | tf_op jit(solution)/shard_map/ppermute | solution.py:449
  4.7 0.3 %collective-permute-start.1 = (bf16[4,136,256]{2,1,0:T(8,128)(2,1)S(1)}, bf16[4,136,256]{2,1,0:T(8,128)(2,1)S(1)}, u32[]{:S(2)}, u32[]{:S(2)}) collective-permute-start(bf16[4,136,256]{2,1,0:T(8,128)(2,1)S(1)} %get-tuple-element.58), channel_id=1, source_target_pairs={{0,8},{4,0},{8,16},{12,4},{16,24},{20,12},{24,28},{28,20},{1,9},{5... | collective-permute-start | bytes 835592 | tf_op jit(solution)/shard_map/ppermute | solution.py:464
  5.0 1.2 %collective-permute-start.3 = (bf16[4,8,256]{2,1,0:T(8,128)(2,1)S(1)}, bf16[4,8,256]{2,1,0:T(8,128)(2,1)S(1)}, u32[]{:S(2)}, u32[]{:S(2)}) collective-permute-start(bf16[4,8,256]{2,1,0:T(8,128)(2,1)S(1)} %get-tuple-element.59), channel_id=1, source_target_pairs={{0,4},{4,12},{8,0},{12,20},{16,8},{20,28},{24,16},{28,24},{1,5},{5... | collective-permute-start | bytes 49160 | tf_op jit(solution)/shard_map/ppermute | solution.py:465
  6.1 1.5 %filter_weights.1 = (bf16[2,256,128]{2,1,0:T(8,128)(2,1)S(1)}, bf16[512,256]{1,0:T(8,128)(2,1)S(1)}, bf16[128,256]{1,0:T(8,128)(2,1)S(1)}, bf16[4,8,256]{2,1,0:T...) custom-call(s32[8]{0:T(128)} %start_in.1, ...), custom_call_target="tpu_custom_call", output_to_operand_aliasing={{0}: (6, {}), {1}: (7, {}), {2}: (8, {}), {3}: (9, {}), {4}... | custom-call | flops 100000 | bytes 1000 | tf_op jit(solution)/shard_map/filter_weights/pallas_call | solution.py:413
  7.6 1.5 %own_rows.1 = (f32[8,128,256]{2,1,0:T(8,128)S(1)}, bf16[4,512,256]{2,1,0:T(8,128)(2,1)S(1)}) custom-call(bf16[4,512,256]{2,1,0:T(8,128)(2,1)S(1)} %get-tuple-element.72.turned_in, bf16[512,256]{1,0:T(8,128)(2,1)S(1)} %get-tuple-element.73.own_weights, bf16[4,8,256]{2,1,0:T(8,128)(2,1)S(1)} %get-tuple-element.74.cycle_taps, ...), custom_call_target="tpu_custom_call", output_to_operand_aliasing={{1}: (0, {})} | custom-call | flops 100000 | bytes 1000 | tf_op jit(solution)/shard_map/own_rows/pallas_call | solution.py:468
  9.1 0.0 collective-permute-done.4.polar_left
  9.1 0.0 collective-permute-done.5.polar_right
  9.1 1.7 %partner_columns.1.acc = f32[8,128,256]{2,1,0:T(8,128)S(1)} custom-call(f32[8,128,256]{2,1,0:T(8,128)S(1)} %get-tuple-element.76.acc_in, bf16[512,256]{1,0:T(8,128)(2,1)S(1)} %get-tuple-element.73.own_weights, bf16[128,256]{1,0:T(8,128)(2,1)S(1)} %get-tuple-element.77.polar_weights, ...), custom_call_target="tpu_custom_call", output_to_operand_aliasing={{}: (0, {})} | custom-call | flops 100000 | bytes 1000 | tf_op jit(solution)/shard_map/partner_columns/pallas_call | solution.py:488
  10.8 0.0 collective-permute-done.3.edges
  10.8 0.0 collective-permute-done.2.halo
  10.9 0.1 collective-permute-done.1.halo
  11.0 1.4 %late_side.1 = bf16[8,128,256]{2,1,0:T(8,128)(2,1)} custom-call(bf16[4,128,256]{2,1,0:T(8,128)(2,1)S(1)} %early_side.1.early, bf16[4,136,256]{2,1,0:T(8,128)(2,1)S(1)} %collective-permute-done.1.halo, bf16[2,256,128]{2,1,0:T(8,128)(2,1)S(1)} %get-tuple-element.83.weights, f32[8,128,256]{2,1,0:T(8,128)S(1)} %partner_columns.1.acc, ...), custom_call_target="tpu_custom_call" | custom-call | tf_op jit(solution)/shard_map/late_side/pallas_call | solution.py:524
  (2 shorter events, 0.1 us)
Async XLA Ops:
  1.1 9.7 %collective-permute-start.2 = (bf16[4,128,256]{2,1,0:T(8,128)(2,1)S(1)}, bf16[4,128,256]{2,1,0:T(8,128)(2,1)S(1)}, u32[]{:S(2)}, u32[]{:S(2)}) collective-permute-start(bf16[4,128,256]{2,1,0:T(8,128)(2,1)S(1)} %get-tuple-element.54.going), channel_id=1, source_target_pairs={{0,4},{4,12},{8,0},{12,20},{16,8},{20,28},{24,16},{28,24},{1,5},{5... | collective-permute-start | bytes 786440 | tf_op jit(solution)/shard_map/ppermute | solution.py:384
  3.4 1.3 %collective-permute-start = (bf16[8,8,256]{2,1,0:T(8,128)(2,1)S(1)}, bf16[8,8,256]{2,1,0:T(8,128)(2,1)S(1)}, u32[]{:S(2)}, u32[]{:S(2)}) collective-permute-start(bf16[8,8,256]{2,1,0:T(8,128)(2,1)S(1)} %get-tuple-element.57), channel_id=1, source_target_pairs={{0,4},{4,0},{1,5},{5,1},{2,6},{6,2},{3,7},{7,3},{8,12},{12,8},{9,1... | collective-permute-start | bytes 98312 | tf_op jit(solution)/shard_map/ppermute | solution.py:449
  3.7 5.4 %collective-permute-start.4 = (bf16[4,64,256]{2,1,0:T(8,128)(2,1)S(1)}, bf16[4,64,256]{2,1,0:T(8,128)(2,1)S(1)}, u32[]{:S(2)}, u32[]{:S(2)}) collective-permute-start(bf16[4,64,256]{2,1,0:T(8,128)(2,1)S(1)} %get-tuple-element.79), channel_id=1, source_target_pairs={{0,4},{4,0},{1,5},{5,1},{2,6},{6,2},{3,7},{7,3},{8,12},{12,8},{9,1... | collective-permute-start | bytes 393224 | tf_op jit(solution)/shard_map/ppermute | solution.py:450
  3.9 5.2 %collective-permute-start.5 = (bf16[4,64,256]{2,1,0:T(8,128)(2,1)S(1)}, bf16[4,64,256]{2,1,0:T(8,128)(2,1)S(1)}, u32[]{:S(2)}, u32[]{:S(2)}) collective-permute-start(bf16[4,64,256]{2,1,0:T(8,128)(2,1)S(1)} %get-tuple-element.80), channel_id=1, source_target_pairs={{0,4},{4,0},{1,5},{5,1},{2,6},{6,2},{3,7},{7,3},{8,12},{12,8},{9,1... | collective-permute-start | bytes 393224 | tf_op jit(solution)/shard_map/ppermute | solution.py:451
  4.7 6.3 %collective-permute-start.1 = (bf16[4,136,256]{2,1,0:T(8,128)(2,1)S(1)}, bf16[4,136,256]{2,1,0:T(8,128)(2,1)S(1)}, u32[]{:S(2)}, u32[]{:S(2)}) collective-permute-start(bf16[4,136,256]{2,1,0:T(8,128)(2,1)S(1)} %get-tuple-element.58), channel_id=1, source_target_pairs={{0,8},{4,0},{8,16},{12,4},{16,24},{20,12},{24,28},{28,20},{1,9},{5... | collective-permute-start | bytes 835592 | tf_op jit(solution)/shard_map/ppermute | solution.py:464
  5.0 5.8 %collective-permute-start.3 = (bf16[4,8,256]{2,1,0:T(8,128)(2,1)S(1)}, bf16[4,8,256]{2,1,0:T(8,128)(2,1)S(1)}, u32[]{:S(2)}, u32[]{:S(2)}) collective-permute-start(bf16[4,8,256]{2,1,0:T(8,128)(2,1)S(1)} %get-tuple-element.59), channel_id=1, source_target_pairs={{0,4},{4,12},{8,0},{12,20},{16,8},{20,28},{24,16},{28,24},{1,5},{5... | collective-permute-start | bytes 49160 | tf_op jit(solution)/shard_map/ppermute | solution.py:465

commit v15 on v14

--- a/solution.py
+++ b/solution.py
@@ -80,7 +80,7 @@
     base = lat_pos * rows
     at_top = base == 0
 
-    is_early = at_top & (lax.axis_index("lon") == 0)
+    is_early = at_top & (lax.axis_index("lon") == 0) & (lax.axis_index("ens") == 0)
 
     @pl.when(jnp.logical_not(is_early) if late else is_early)
     def make():
@@ -166,10 +166,6 @@
             polar_weights[i * BLOCK : (i + 1) * BLOCK, :] = staircase(line[i : i + 1], BLOCK)
         copies[4].wait()
 
-        @pl.when(at_top & (lax.axis_index("lon") == 0))
-        def top():
-            polar_matrices(cycle_taps, turned, True)
-
         copies[5].wait()
 
 
@@ -207,7 +203,7 @@
 
     lat_pos = lax.axis_index("lat")
 
-    @pl.when((lat_pos == 0) & (lax.axis_index("lon") != 0))
+    @pl.when(lat_pos == 0)
     def top():
         polar_matrices(cycle_taps, turned, True)
 

time: 12.6 us -> 12.6 us (level)
  starting transfers between devices: 4.47 us -> 4.27 us
  waiting for transfers between devices: 0.55 us -> 0.75 us
    ppermute x1, starting transfers between devices: 0.34 us -> 0.07 us  [shards(): edges = lax.ppermute(edges, 'lon', SWAP)]
    ppermute x1, starting transfers between devices: 0.24 us -> 0.5 us  [shards(): polar_left = lax.ppermute(polar_left, 'lon', SWAP)]
    ppermute x1, starting transfers between devices: 0.27 us -> 0.08 us  [shards(): polar_right = lax.ppermute(polar_right, 'lon', SWAP)]
    ppermute x1, waiting for transfers between devices: 0.42 us -> 0.62 us  [shards(): edges = lax.ppermute(edges, 'lon', SWAP)]
where the time goes in v15:
time: 12.6 us; the launch traced here: 12.4 us
  Pallas kernels  6.23 us (49%)
  starting transfers between devices  4.27 us (34%)
  other arithmetic  1.07 us (8%)
  waiting for transfers between devices  0.75 us (6%)
    ppermute x1, starting transfers between devices, shards(): second = lax.ppermute(going, axes, back)  2.14 us
    pallas_call x1, Pallas kernels, shards(): pl.pallas_call(partner_kernel, out_shape=sds((rows, cols, chans), F32), i...  1.66 us
    pallas_call x2, Pallas kernels, weights(): pl.pallas_call(functools.partial(weight_kernel, bool(made)), out_shape=we...  1.51 us
    pallas_call x1, Pallas kernels, shards(): pl.pallas_call(own_kernel, out_shape=(sds((rows, cols, chans), F32), sds(...  1.48 us
    pallas_call x1, Pallas kernels, shards(): pl.pallas_call(late_kernel, out_shape=sds((rows, cols, chans), BF16), in_...  1.42 us
    ppermute x1, starting transfers between devices, shards(): second_edges = lax.ppermute(corners, axes, back)  1.3 us
    select_n x1, other arithmetic, shards(): staying = jnp.where(core == 0, tail, head)  1.07 us
    ppermute x1, waiting for transfers between devices, shards(): edges = lax.ppermute(edges, 'lon', SWAP)  0.62 us
  transfers between devices with their start and end apart: 6, of which 2 were waited for; matrix products, arithmetic and copies ran while one was open for 0% of the time, Pallas kernels for 39%

profile of v15, /device:TPU:1, one launch (start us, length us, event | category | flops | bytes accessed | tf_op | source)
XLA Modules:
  0.0 12.4 jit_solution(1243917405342511589)
XLA Ops:
  0.0 1.1 %broadcast_select_fusion = (bf16[4,128,256]{2,1,0:T(8,128)(2,1)S(1)}, bf16[4,128,256]{2,1,0:T(8,128)(2,1)S(1)}) fusion(pred[]{:T(512)S(6)} %eq.4, bf16[8,128,256]{2,1,0:T(8,128)(2,1)} %param.7), kind=kLoop, calls=%fused_computation | loop fusion | flops 262144 | bytes 1048577 | tf_op jit(solution)/shard_map/jit(_where)/select_n | solution.py:379
  1.1 2.1 %collective-permute-start.2 = (bf16[4,128,256]{2,1,0:T(8,128)(2,1)S(1)}, bf16[4,128,256]{2,1,0:T(8,128)(2,1)S(1)}, u32[]{:S(2)}, u32[]{:S(2)}) collective-permute-start(bf16[4,128,256]{2,1,0:T(8,128)(2,1)S(1)} %get-tuple-element.54.going), channel_id=1, source_target_pairs={{0,4},{4,12},{8,0},{12,20},{16,8},{20,28},{24,16},{28,24},{1,5},{5... | collective-permute-start | bytes 786440 | tf_op jit(solution)/shard_map/ppermute | solution.py:380
  3.2 0.1 first_weights.1
  3.3 0.1 stage_rows.1
  3.4 0.1 collective-permute-start
  3.4 0.5 %collective-permute-start.4 = (bf16[4,64,256]{2,1,0:T(8,128)(2,1)S(1)}, bf16[4,64,256]{2,1,0:T(8,128)(2,1)S(1)}, u32[]{:S(2)}, u32[]{:S(2)}) collective-permute-start(bf16[4,64,256]{2,1,0:T(8,128)(2,1)S(1)} %get-tuple-element.79), channel_id=1, source_target_pairs={{0,4},{4,0},{1,5},{5,1},{2,6},{6,2},{3,7},{7,3},{8,12},{12,8},{9,1... | collective-permute-start | bytes 393224 | tf_op jit(solution)/shard_map/ppermute | solution.py:446
  3.9 0.1 collective-permute-start.5
  4.0 0.6 %collective-permute-done.edges = bf16[8,8,256]{2,1,0:T(8,128)(2,1)S(1)} collective-permute-done((bf16[8,8,256]{2,1,0:T(8,128)(2,1)S(1)}, bf16[8,8,256]{2,1,0:T(8,128)(2,1)S(1)}, u32[]{:S(2)}, u32[]{:S(2)}) %collective-permute-start) | collective-permute-done | bytes 32800 | tf_op jit(solution)/shard_map/ppermute | solution.py:445
  4.7 0.2 %collective-permute-start.1 = (bf16[4,136,256]{2,1,0:T(8,128)(2,1)S(1)}, bf16[4,136,256]{2,1,0:T(8,128)(2,1)S(1)}, u32[]{:S(2)}, u32[]{:S(2)}) collective-permute-start(bf16[4,136,256]{2,1,0:T(8,128)(2,1)S(1)} %get-tuple-element.58), channel_id=1, source_target_pairs={{0,8},{4,0},{8,16},{12,4},{16,24},{20,12},{24,28},{28,20},{1,9},{5... | collective-permute-start | bytes 835592 | tf_op jit(solution)/shard_map/ppermute | solution.py:460
  4.8 1.3 %collective-permute-start.3 = (bf16[4,8,256]{2,1,0:T(8,128)(2,1)S(1)}, bf16[4,8,256]{2,1,0:T(8,128)(2,1)S(1)}, u32[]{:S(2)}, u32[]{:S(2)}) collective-permute-start(bf16[4,8,256]{2,1,0:T(8,128)(2,1)S(1)} %get-tuple-element.59), channel_id=1, source_target_pairs={{0,4},{4,12},{8,0},{12,20},{16,8},{20,28},{24,16},{28,24},{1,5},{5... | collective-permute-start | bytes 49160 | tf_op jit(solution)/shard_map/ppermute | solution.py:461
  6.1 1.5 %filter_weights.1 = (bf16[2,256,128]{2,1,0:T(8,128)(2,1)S(1)}, bf16[512,256]{1,0:T(8,128)(2,1)S(1)}, bf16[128,256]{1,0:T(8,128)(2,1)S(1)}, bf16[4,8,256]{2,1,0:T...) custom-call(s32[8]{0:T(128)} %start_in.1, ...), custom_call_target="tpu_custom_call", output_to_operand_aliasing={{0}: (6, {}), {1}: (7, {}), {2}: (8, {}), {3}: (9, {}), {4}... | custom-call | flops 100000 | bytes 1000 | tf_op jit(solution)/shard_map/filter_weights/pallas_call | solution.py:409
  7.6 1.5 %own_rows.1 = (f32[8,128,256]{2,1,0:T(8,128)S(1)}, bf16[4,512,256]{2,1,0:T(8,128)(2,1)S(1)}) custom-call(bf16[4,512,256]{2,1,0:T(8,128)(2,1)S(1)} %get-tuple-element.72.turned_in, bf16[512,256]{1,0:T(8,128)(2,1)S(1)} %get-tuple-element.73.own_weights, bf16[4,8,256]{2,1,0:T(8,128)(2,1)S(1)} %get-tuple-element.74.cycle_taps, ...), custom_call_target="tpu_custom_call", output_to_operand_aliasing={{1}: (0, {})} | custom-call | flops 100000 | bytes 1000 | tf_op jit(solution)/shard_map/own_rows/pallas_call | solution.py:464
  9.1 0.0 collective-permute-done.4.polar_left
  9.1 0.0 collective-permute-done.5.polar_right
  9.1 1.7 %partner_columns.1.acc = f32[8,128,256]{2,1,0:T(8,128)S(1)} custom-call(f32[8,128,256]{2,1,0:T(8,128)S(1)} %get-tuple-element.76.acc_in, bf16[512,256]{1,0:T(8,128)(2,1)S(1)} %get-tuple-element.73.own_weights, bf16[128,256]{1,0:T(8,128)(2,1)S(1)} %get-tuple-element.77.polar_weights, ...), custom_call_target="tpu_custom_call", output_to_operand_aliasing={{}: (0, {})} | custom-call | flops 100000 | bytes 1000 | tf_op jit(solution)/shard_map/partner_columns/pallas_call | solution.py:484
  10.8 0.0 collective-permute-done.3.edges
  10.8 0.0 collective-permute-done.2.halo
  10.9 0.1 collective-permute-done.1.halo
  11.0 1.4 %late_side.1 = bf16[8,128,256]{2,1,0:T(8,128)(2,1)} custom-call(bf16[4,128,256]{2,1,0:T(8,128)(2,1)S(1)} %early_side.1.early, bf16[4,136,256]{2,1,0:T(8,128)(2,1)S(1)} %collective-permute-done.1.halo, bf16[2,256,128]{2,1,0:T(8,128)(2,1)S(1)} %get-tuple-element.83.weights, f32[8,128,256]{2,1,0:T(8,128)S(1)} %partner_columns.1.acc, ...), custom_call_target="tpu_custom_call" | custom-call | tf_op jit(solution)/shard_map/late_side/pallas_call | solution.py:520
  (2 shorter events, 0.1 us)
Async XLA Ops:
  1.1 9.7 %collective-permute-start.2 = (bf16[4,128,256]{2,1,0:T(8,128)(2,1)S(1)}, bf16[4,128,256]{2,1,0:T(8,128)(2,1)S(1)}, u32[]{:S(2)}, u32[]{:S(2)}) collective-permute-start(bf16[4,128,256]{2,1,0:T(8,128)(2,1)S(1)} %get-tuple-element.54.going), channel_id=1, source_target_pairs={{0,4},{4,12},{8,0},{12,20},{16,8},{20,28},{24,16},{28,24},{1,5},{5... | collective-permute-start | bytes 786440 | tf_op jit(solution)/shard_map/ppermute | solution.py:380
  3.4 1.3 %collective-permute-start = (bf16[8,8,256]{2,1,0:T(8,128)(2,1)S(1)}, bf16[8,8,256]{2,1,0:T(8,128)(2,1)S(1)}, u32[]{:S(2)}, u32[]{:S(2)}) collective-permute-start(bf16[8,8,256]{2,1,0:T(8,128)(2,1)S(1)} %get-tuple-element.57), channel_id=1, source_target_pairs={{0,4},{4,0},{1,5},{5,1},{2,6},{6,2},{3,7},{7,3},{8,12},{12,8},{9,1... | collective-permute-start | bytes 98312 | tf_op jit(solution)/shard_map/ppermute | solution.py:445
  3.4 5.7 %collective-permute-start.4 = (bf16[4,64,256]{2,1,0:T(8,128)(2,1)S(1)}, bf16[4,64,256]{2,1,0:T(8,128)(2,1)S(1)}, u32[]{:S(2)}, u32[]{:S(2)}) collective-permute-start(bf16[4,64,256]{2,1,0:T(8,128)(2,1)S(1)} %get-tuple-element.79), channel_id=1, source_target_pairs={{0,4},{4,0},{1,5},{5,1},{2,6},{6,2},{3,7},{7,3},{8,12},{12,8},{9,1... | collective-permute-start | bytes 393224 | tf_op jit(solution)/shard_map/ppermute | solution.py:446
  3.9 5.2 %collective-permute-start.5 = (bf16[4,64,256]{2,1,0:T(8,128)(2,1)S(1)}, bf16[4,64,256]{2,1,0:T(8,128)(2,1)S(1)}, u32[]{:S(2)}, u32[]{:S(2)}) collective-permute-start(bf16[4,64,256]{2,1,0:T(8,128)(2,1)S(1)} %get-tuple-element.80), channel_id=1, source_target_pairs={{0,4},{4,0},{1,5},{5,1},{2,6},{6,2},{3,7},{7,3},{8,12},{12,8},{9,1... | collective-permute-start | bytes 393224 | tf_op jit(solution)/shard_map/ppermute | solution.py:447
  4.7 6.3 %collective-permute-start.1 = (bf16[4,136,256]{2,1,0:T(8,128)(2,1)S(1)}, bf16[4,136,256]{2,1,0:T(8,128)(2,1)S(1)}, u32[]{:S(2)}, u32[]{:S(2)}) collective-permute-start(bf16[4,136,256]{2,1,0:T(8,128)(2,1)S(1)} %get-tuple-element.58), channel_id=1, source_target_pairs={{0,8},{4,0},{8,16},{12,4},{16,24},{20,12},{24,28},{28,20},{1,9},{5... | collective-permute-start | bytes 835592 | tf_op jit(solution)/shard_map/ppermute | solution.py:460
  4.8 6.0 %collective-permute-start.3 = (bf16[4,8,256]{2,1,0:T(8,128)(2,1)S(1)}, bf16[4,8,256]{2,1,0:T(8,128)(2,1)S(1)}, u32[]{:S(2)}, u32[]{:S(2)}) collective-permute-start(bf16[4,8,256]{2,1,0:T(8,128)(2,1)S(1)} %get-tuple-element.59), channel_id=1, source_target_pairs={{0,4},{4,12},{8,0},{12,20},{16,8},{20,28},{24,16},{28,24},{1,5},{5... | collective-permute-start | bytes 49160 | tf_op jit(solution)/shard_map/ppermute | solution.py:461

commit v16 on v15

--- a/solution.py
+++ b/solution.py
@@ -169,7 +169,11 @@
         copies[5].wait()
 
 
-def stage_kernel(going, staying, whole, edges, polar_left, polar_right):
+def stage_kernel(
+    start_in, width_in, lon_in, lat_in, cycle_in, mixing_in, going, staying,
+    whole, edges, polar_left, polar_right, *refs,
+):
+    weight_kernel(False, start_in, width_in, lon_in, lat_in, cycle_in, mixing_in, *refs)
     cols = whole.shape[1]
     reach = edges.shape[1] // 2
     is_first = lax.axis_index("lon") == 0
@@ -397,51 +401,39 @@
         sds((polar, basis * cols, cycle), BF16),
     )
 
-    def weights(made):
-        operands = [
-            pltpu.with_memory_space_constraint(x, pltpu.HBM)
-            for x in (
-                band_start, band_width, jnp.transpose(lon_taps, (2, 1, 0)),
-                jnp.transpose(lat_taps, (2, 1, 0)), cycle_taps,
-                mixing.reshape(basis * chans, chans),
-            )
-        ]
-        return pl.pallas_call(
-            functools.partial(weight_kernel, bool(made)),
-            out_shape=weight_shapes,
-            in_specs=[hbm] * 6 + [vmem] * len(made),
-            out_specs=[vmem] * 6,
-            input_output_aliases={6 + n: n for n in range(len(made))},
-            scratch_shapes=[
-                pltpu.SMEM((rows,), jnp.int32),
-                pltpu.SMEM((rows,), jnp.int32),
-                pltpu.VMEM((taps, basis, row_total), F32),
-                pltpu.VMEM((band, basis, rows), BF16),
-                pltpu.VMEM((128, -(-row_total // 128) * 128), F32),
-                pltpu.VMEM((128, 128), F32),
-                pltpu.SemaphoreType.DMA((6,)),
-            ],
-            compiler_params=limit,
-            cost_estimate=small,
-            name="filter_weights" if made else "first_weights",
-        )(*operands, *made)
-
-    made = weights(())
-    going, made = lax.optimization_barrier((going, made))
-    whole, edges, polar_left, polar_right = pl.pallas_call(
+    operands = [
+        pltpu.with_memory_space_constraint(x, pltpu.HBM)
+        for x in (
+            band_start, band_width, jnp.transpose(lon_taps, (2, 1, 0)),
+            jnp.transpose(lat_taps, (2, 1, 0)), cycle_taps,
+            mixing.reshape(basis * chans, chans),
+        )
+    ]
+    weight_scratch = [
+        pltpu.SMEM((rows,), jnp.int32),
+        pltpu.SMEM((rows,), jnp.int32),
+        pltpu.VMEM((taps, basis, row_total), F32),
+        pltpu.VMEM((band, basis, rows), BF16),
+        pltpu.VMEM((128, -(-row_total // 128) * 128), F32),
+        pltpu.VMEM((128, 128), F32),
+        pltpu.SemaphoreType.DMA((6,)),
+    ]
+    whole, edges, polar_left, polar_right, *made = pl.pallas_call(
         stage_kernel,
         out_shape=(
             sds((rows, cols, chans), BF16),
             sds((rows, 2 * reach, chans), BF16),
             sds((polar, cols // 2, chans), BF16),
             sds((polar, cols // 2, chans), BF16),
+            *weight_shapes,
         ),
-        in_specs=[vmem] * 2,
-        out_specs=[vmem] * 4,
+        in_specs=[hbm] * 6 + [vmem] * 2,
+        out_specs=[vmem] * 10,
+        scratch_shapes=weight_scratch,
         compiler_params=limit,
         cost_estimate=small,
         name="stage_rows",
-    )(going, staying)
+    )(*operands, going, staying)
     edges = lax.ppermute(edges, "lon", SWAP)
     polar_left = lax.ppermute(polar_left, "lon", SWAP)
     polar_right = lax.ppermute(polar_right, "lon", SWAP)
@@ -460,7 +452,17 @@
     first = lax.ppermute(message, axes, ahead)
     second_edges = lax.ppermute(corners, axes, back)
     corners, made = lax.optimization_barrier((corners, made))
-    halo_weights, own_weights, polar_weights, turns, mix, turned = weights(made)
+    halo_weights, own_weights, polar_weights, turns, mix, turned = pl.pallas_call(
+        functools.partial(weight_kernel, True),
+        out_shape=weight_shapes,
+        in_specs=[hbm] * 6 + [vmem] * 6,
+        out_specs=[vmem] * 6,
+        input_output_aliases={6 + n: n for n in range(6)},
+        scratch_shapes=weight_scratch,
+        compiler_params=limit,
+        cost_estimate=small,
+        name="filter_weights",
+    )(*operands, *made)
     acc, turned = pl.pallas_call(
         own_kernel,
         out_shape=(

time: 12.6 us -> 12.6 us (level)
    pallas_call x2 -> x1, Pallas kernels: 1.51 us -> 1.46 us  [shards(): pl.pallas_call(functools.partial(weight_kernel, True), out_shape=weight_s...]
where the time goes in v16:
time: 12.6 us; the launch traced here: 12.4 us
  Pallas kernels  6.21 us (49%)
  starting transfers between devices  4.27 us (34%)
  other arithmetic  1.07 us (8%)
  waiting for transfers between devices  0.77 us (6%)
    ppermute x1, starting transfers between devices, shards(): second = lax.ppermute(going, axes, back)  2.14 us
    pallas_call x1, Pallas kernels, shards(): pl.pallas_call(partner_kernel, out_shape=sds((rows, cols, chans), F32), i...  1.66 us
    pallas_call x1, Pallas kernels, shards(): pl.pallas_call(own_kernel, out_shape=(sds((rows, cols, chans), F32), sds(...  1.48 us
    pallas_call x1, Pallas kernels, shards(): pl.pallas_call(functools.partial(weight_kernel, True), out_shape=weight_s...  1.46 us
    pallas_call x1, Pallas kernels, shards(): pl.pallas_call(late_kernel, out_shape=sds((rows, cols, chans), BF16), in_...  1.42 us
    ppermute x1, starting transfers between devices, shards(): second_edges = lax.ppermute(corners, axes, back)  1.3 us
    select_n x1, other arithmetic, shards(): staying = jnp.where(core == 0, tail, head)  1.07 us
    ppermute x1, waiting for transfers between devices, shards(): edges = lax.ppermute(edges, 'lon', SWAP)  0.62 us
  transfers between devices with their start and end apart: 6, of which 2 were waited for; matrix products, arithmetic and copies ran while one was open for 0% of the time, Pallas kernels for 39%

profile of v16, /device:TPU:1, one launch (start us, length us, event | category | flops | bytes accessed | tf_op | source)
XLA Modules:
  0.0 12.4 jit_solution(9973663940331299256)
XLA Ops:
  0.0 1.1 %broadcast_select_fusion = (bf16[4,128,256]{2,1,0:T(8,128)(2,1)S(1)}, bf16[4,128,256]{2,1,0:T(8,128)(2,1)S(1)}) fusion(pred[]{:T(512)S(6)} %eq.4, bf16[8,128,256]{2,1,0:T(8,128)(2,1)} %param.7), kind=kLoop, calls=%fused_computation | loop fusion | flops 262144 | bytes 1048577 | tf_op jit(solution)/shard_map/jit(_where)/select_n | solution.py:383
  1.1 2.1 %collective-permute-start.2 = (bf16[4,128,256]{2,1,0:T(8,128)(2,1)S(1)}, bf16[4,128,256]{2,1,0:T(8,128)(2,1)S(1)}, u32[]{:S(2)}, u32[]{:S(2)}) collective-permute-start(bf16[4,128,256]{2,1,0:T(8,128)(2,1)S(1)} %get-tuple-element.40.going), channel_id=1, source_target_pairs={{0,4},{4,12},{8,0},{12,20},{16,8},{20,28},{24,16},{28,24},{1,5},{5... | collective-permute-start | bytes 786440 | tf_op jit(solution)/shard_map/ppermute | solution.py:384
  3.2 0.1 stage_rows.1
  3.3 0.1 collective-permute-start
  3.4 0.5 %collective-permute-start.4 = (bf16[4,64,256]{2,1,0:T(8,128)(2,1)S(1)}, bf16[4,64,256]{2,1,0:T(8,128)(2,1)S(1)}, u32[]{:S(2)}, u32[]{:S(2)}) collective-permute-start(bf16[4,64,256]{2,1,0:T(8,128)(2,1)S(1)} %get-tuple-element.65), channel_id=1, source_target_pairs={{0,4},{4,0},{1,5},{5,1},{2,6},{6,2},{3,7},{7,3},{8,12},{12,8},{9,1... | collective-permute-start | bytes 393224 | tf_op jit(solution)/shard_map/ppermute | solution.py:438
  3.9 0.1 collective-permute-start.5
  4.0 0.6 %collective-permute-done.edges = bf16[8,8,256]{2,1,0:T(8,128)(2,1)S(1)} collective-permute-done((bf16[8,8,256]{2,1,0:T(8,128)(2,1)S(1)}, bf16[8,8,256]{2,1,0:T(8,128)(2,1)S(1)}, u32[]{:S(2)}, u32[]{:S(2)}) %collective-permute-start) | collective-permute-done | bytes 32800 | tf_op jit(solution)/shard_map/ppermute | solution.py:437
  4.6 0.2 %collective-permute-start.1 = (bf16[4,136,256]{2,1,0:T(8,128)(2,1)S(1)}, bf16[4,136,256]{2,1,0:T(8,128)(2,1)S(1)}, u32[]{:S(2)}, u32[]{:S(2)}) collective-permute-start(bf16[4,136,256]{2,1,0:T(8,128)(2,1)S(1)} %get-tuple-element.44), channel_id=1, source_target_pairs={{0,8},{4,0},{8,16},{12,4},{16,24},{20,12},{24,28},{28,20},{1,9},{5... | collective-permute-start | bytes 835592 | tf_op jit(solution)/shard_map/ppermute | solution.py:452
  4.8 1.3 %collective-permute-start.3 = (bf16[4,8,256]{2,1,0:T(8,128)(2,1)S(1)}, bf16[4,8,256]{2,1,0:T(8,128)(2,1)S(1)}, u32[]{:S(2)}, u32[]{:S(2)}) collective-permute-start(bf16[4,8,256]{2,1,0:T(8,128)(2,1)S(1)} %get-tuple-element.45), channel_id=1, source_target_pairs={{0,4},{4,12},{8,0},{12,20},{16,8},{20,28},{24,16},{28,24},{1,5},{5... | collective-permute-start | bytes 49160 | tf_op jit(solution)/shard_map/ppermute | solution.py:453
  6.1 1.5 %filter_weights.1 = (bf16[2,256,128]{2,1,0:T(8,128)(2,1)S(1)}, bf16[512,256]{1,0:T(8,128)(2,1)S(1)}, bf16[128,256]{1,0:T(8,128)(2,1)S(1)}, bf16[4,8,256]{2,1,0:T...) custom-call(s32[8]{0:T(128)} %start_in.1, ...), custom_call_target="tpu_custom_call", output_to_operand_aliasing={{0}: (6, {}), {1}: (7, {}), {2}: (8, {}), {3}: (9, {}), {4}... | custom-call | flops 100000 | bytes 1000 | tf_op jit(solution)/shard_map/filter_weights/pallas_call | solution.py:455
  7.6 1.5 %own_rows.1 = (f32[8,128,256]{2,1,0:T(8,128)S(1)}, bf16[4,512,256]{2,1,0:T(8,128)(2,1)S(1)}) custom-call(bf16[4,512,256]{2,1,0:T(8,128)(2,1)S(1)} %get-tuple-element.58.turned_in, bf16[512,256]{1,0:T(8,128)(2,1)S(1)} %get-tuple-element.59.own_weights, bf16[4,8,256]{2,1,0:T(8,128)(2,1)S(1)} %get-tuple-element.60.cycle_taps, ...), custom_call_target="tpu_custom_call", output_to_operand_aliasing={{1}: (0, {})} | custom-call | flops 100000 | bytes 1000 | tf_op jit(solution)/shard_map/own_rows/pallas_call | solution.py:466
  9.1 0.0 collective-permute-done.4.polar_left
  9.1 0.0 collective-permute-done.5.polar_right
  9.1 1.7 %partner_columns.1.acc = f32[8,128,256]{2,1,0:T(8,128)S(1)} custom-call(f32[8,128,256]{2,1,0:T(8,128)S(1)} %get-tuple-element.62.acc_in, bf16[512,256]{1,0:T(8,128)(2,1)S(1)} %get-tuple-element.59.own_weights, bf16[128,256]{1,0:T(8,128)(2,1)S(1)} %get-tuple-element.63.polar_weights, ...), custom_call_target="tpu_custom_call", output_to_operand_aliasing={{}: (0, {})} | custom-call | flops 100000 | bytes 1000 | tf_op jit(solution)/shard_map/partner_columns/pallas_call | solution.py:486
  10.8 0.0 collective-permute-done.3.edges
  10.8 0.0 collective-permute-done.2.halo
  10.8 0.1 %collective-permute-done.1.halo = bf16[4,136,256]{2,1,0:T(8,128)(2,1)S(1)} collective-permute-done((bf16[4,136,256]{2,1,0:T(8,128)(2,1)S(1)}, bf16[4,136,256]{2,1,0:T(8,128)(2,1)S(1)}, u32[]{:S(2)}, u32[]{:S(2)}) %collective-permute-start.1) | collective-permute-done | bytes 278560 | tf_op jit(solution)/shard_map/ppermute | solution.py:452
  11.0 1.4 %late_side.1 = bf16[8,128,256]{2,1,0:T(8,128)(2,1)} custom-call(bf16[4,128,256]{2,1,0:T(8,128)(2,1)S(1)} %early_side.1.early, bf16[4,136,256]{2,1,0:T(8,128)(2,1)S(1)} %collective-permute-done.1.halo, bf16[2,256,128]{2,1,0:T(8,128)(2,1)S(1)} %get-tuple-element.69.weights, f32[8,128,256]{2,1,0:T(8,128)S(1)} %partner_columns.1.acc, ...), custom_call_target="tpu_custom_call" | custom-call | tf_op jit(solution)/shard_map/late_side/pallas_call | solution.py:522
  (2 shorter events, 0.1 us)
Async XLA Ops:
  1.1 9.7 %collective-permute-start.2 = (bf16[4,128,256]{2,1,0:T(8,128)(2,1)S(1)}, bf16[4,128,256]{2,1,0:T(8,128)(2,1)S(1)}, u32[]{:S(2)}, u32[]{:S(2)}) collective-permute-start(bf16[4,128,256]{2,1,0:T(8,128)(2,1)S(1)} %get-tuple-element.40.going), channel_id=1, source_target_pairs={{0,4},{4,12},{8,0},{12,20},{16,8},{20,28},{24,16},{28,24},{1,5},{5... | collective-permute-start | bytes 786440 | tf_op jit(solution)/shard_map/ppermute | solution.py:384
  3.3 1.3 %collective-permute-start = (bf16[8,8,256]{2,1,0:T(8,128)(2,1)S(1)}, bf16[8,8,256]{2,1,0:T(8,128)(2,1)S(1)}, u32[]{:S(2)}, u32[]{:S(2)}) collective-permute-start(bf16[8,8,256]{2,1,0:T(8,128)(2,1)S(1)} %get-tuple-element.43), channel_id=1, source_target_pairs={{0,4},{4,0},{1,5},{5,1},{2,6},{6,2},{3,7},{7,3},{8,12},{12,8},{9,1... | collective-permute-start | bytes 98312 | tf_op jit(solution)/shard_map/ppermute | solution.py:437
  3.4 5.7 %collective-permute-start.4 = (bf16[4,64,256]{2,1,0:T(8,128)(2,1)S(1)}, bf16[4,64,256]{2,1,0:T(8,128)(2,1)S(1)}, u32[]{:S(2)}, u32[]{:S(2)}) collective-permute-start(bf16[4,64,256]{2,1,0:T(8,128)(2,1)S(1)} %get-tuple-element.65), channel_id=1, source_target_pairs={{0,4},{4,0},{1,5},{5,1},{2,6},{6,2},{3,7},{7,3},{8,12},{12,8},{9,1... | collective-permute-start | bytes 393224 | tf_op jit(solution)/shard_map/ppermute | solution.py:438
  3.9 5.2 %collective-permute-start.5 = (bf16[4,64,256]{2,1,0:T(8,128)(2,1)S(1)}, bf16[4,64,256]{2,1,0:T(8,128)(2,1)S(1)}, u32[]{:S(2)}, u32[]{:S(2)}) collective-permute-start(bf16[4,64,256]{2,1,0:T(8,128)(2,1)S(1)} %get-tuple-element.66), channel_id=1, source_target_pairs={{0,4},{4,0},{1,5},{5,1},{2,6},{6,2},{3,7},{7,3},{8,12},{12,8},{9,1... | collective-permute-start | bytes 393224 | tf_op jit(solution)/shard_map/ppermute | solution.py:439
  4.6 6.3 %collective-permute-start.1 = (bf16[4,136,256]{2,1,0:T(8,128)(2,1)S(1)}, bf16[4,136,256]{2,1,0:T(8,128)(2,1)S(1)}, u32[]{:S(2)}, u32[]{:S(2)}) collective-permute-start(bf16[4,136,256]{2,1,0:T(8,128)(2,1)S(1)} %get-tuple-element.44), channel_id=1, source_target_pairs={{0,8},{4,0},{8,16},{12,4},{16,24},{20,12},{24,28},{28,20},{1,9},{5... | collective-permute-start | bytes 835592 | tf_op jit(solution)/shard_map/ppermute | solution.py:452
  4.8 6.0 %collective-permute-start.3 = (bf16[4,8,256]{2,1,0:T(8,128)(2,1)S(1)}, bf16[4,8,256]{2,1,0:T(8,128)(2,1)S(1)}, u32[]{:S(2)}, u32[]{:S(2)}) collective-permute-start(bf16[4,8,256]{2,1,0:T(8,128)(2,1)S(1)} %get-tuple-element.45), channel_id=1, source_target_pairs={{0,4},{4,12},{8,0},{12,20},{16,8},{20,28},{24,16},{28,24},{1,5},{5... | collective-permute-start | bytes 49160 | tf_op jit(solution)/shard_map/ppermute | solution.py:453

commit v17 on v16

--- a/solution.py
+++ b/solution.py
@@ -299,14 +299,11 @@
 
     @pl.when(present)
     def arrived():
-        for p in range(HALO):
-            cells = halo(p)
-            pad = jnp.zeros((ext.shape[1] - cells.shape[0], chans), BF16)
-            ext[p] = jnp.concatenate([cells, pad], axis=0)
+        window = halo()
         groups = [(i, k) for k in range(basis) for i in range(half)]
         for n, part in enumerate(parts):
             for at in range(0, wide, BLOCK):
-                cells = ext[:, part.start + at : part.start + at + SPAN, :]
+                cells = window(part.start + at)
                 window_products(
                     weights.at[side], cells, hidden.at[n], groups, wide, at, chans
                 )
@@ -335,11 +332,15 @@
     side, present = from_side(0)
     reach = edges.shape[1] // 2
 
-    def cells(p):
-        edge = edges[p]
-        return jnp.concatenate([edge[reach:], halo[p], edge[:reach]], axis=0)
-
-    side_rows(side, cells, weights, acc, mix, ext, hidden, present, result)
+    def windows():
+        cols, chans = halo.shape[1:]
+        pad = jnp.zeros((ext.shape[1] - cols - 2 * reach, chans), BF16)
+        for p in range(HALO):
+            edge = edges[p]
+            ext[p] = jnp.concatenate([edge[reach:], halo[p], edge[:reach], pad], axis=0)
+        return lambda start: ext[:, start : start + SPAN, :]
+
+    side_rows(side, windows, weights, acc, mix, ext, hidden, present, result)
 
 
 def late_kernel(early, halo, weights, acc, mix, out, ext, hidden, result, sems):
@@ -348,6 +349,17 @@
     rows = pl.ds(side * half, half)
     other_rows = pl.ds((1 - side) * half, half)
 
+    def windows():
+        def window(start):
+            here = min(SPAN, halo.shape[1] - start)
+            cells = halo[:, start : start + here, :]
+            if here == SPAN:
+                return cells
+            pad = jnp.zeros((HALO, SPAN - here, halo.shape[2]), BF16)
+            return jnp.concatenate([cells, pad], axis=1)
+
+        return window
+
     def copy_of(part):
         n = 0 if part.start == 0 else 1
         return pltpu.make_async_copy(
@@ -357,7 +369,7 @@
     first = pltpu.make_async_copy(early, out.at[other_rows], sems.at[2])
     first.start()
     side_rows(
-        side, lambda p: halo[p], weights, acc, mix, ext, hidden, present, result,
+        side, windows, weights, acc, mix, ext, hidden, present, result,
         lambda part: copy_of(part).start(),
     )
     first.wait()

time: 12.6 us -> 12.6 us (level)
  no operation moved by 1% of the time
where the time goes in v17:
time: 12.6 us; the launch traced here: 12.4 us
  Pallas kernels  6.21 us (49%)
  starting transfers between devices  4.27 us (34%)
  other arithmetic  1.07 us (8%)
  waiting for transfers between devices  0.77 us (6%)
    ppermute x1, starting transfers between devices, shards(): second = lax.ppermute(going, axes, back)  2.14 us
    pallas_call x1, Pallas kernels, shards(): pl.pallas_call(partner_kernel, out_shape=sds((rows, cols, chans), F32), i...  1.66 us
    pallas_call x1, Pallas kernels, shards(): pl.pallas_call(own_kernel, out_shape=(sds((rows, cols, chans), F32), sds(...  1.48 us
    pallas_call x1, Pallas kernels, shards(): pl.pallas_call(functools.partial(weight_kernel, True), out_shape=weight_s...  1.46 us
    pallas_call x1, Pallas kernels, shards(): pl.pallas_call(late_kernel, out_shape=sds((rows, cols, chans), BF16), in_...  1.42 us
    ppermute x1, starting transfers between devices, shards(): second_edges = lax.ppermute(corners, axes, back)  1.3 us
    select_n x1, other arithmetic, shards(): staying = jnp.where(core == 0, tail, head)  1.07 us
    ppermute x1, waiting for transfers between devices, shards(): edges = lax.ppermute(edges, 'lon', SWAP)  0.62 us
  transfers between devices with their start and end apart: 6, of which 2 were waited for; matrix products, arithmetic and copies ran while one was open for 0% of the time, Pallas kernels for 39%

profile of v17, /device:TPU:1, one launch (start us, length us, event | category | flops | bytes accessed | tf_op | source)
XLA Modules:
  0.0 12.4 jit_solution(5142999556096468322)
XLA Ops:
  0.0 1.1 %broadcast_select_fusion = (bf16[4,128,256]{2,1,0:T(8,128)(2,1)S(1)}, bf16[4,128,256]{2,1,0:T(8,128)(2,1)S(1)}) fusion(pred[]{:T(512)S(6)} %eq.4, bf16[8,128,256]{2,1,0:T(8,128)(2,1)} %param.7), kind=kLoop, calls=%fused_computation | loop fusion | flops 262144 | bytes 1048577 | tf_op jit(solution)/shard_map/jit(_where)/select_n | solution.py:395
  1.1 2.1 %collective-permute-start.2 = (bf16[4,128,256]{2,1,0:T(8,128)(2,1)S(1)}, bf16[4,128,256]{2,1,0:T(8,128)(2,1)S(1)}, u32[]{:S(2)}, u32[]{:S(2)}) collective-permute-start(bf16[4,128,256]{2,1,0:T(8,128)(2,1)S(1)} %get-tuple-element.40.going), channel_id=1, source_target_pairs={{0,4},{4,12},{8,0},{12,20},{16,8},{20,28},{24,16},{28,24},{1,5},{5... | collective-permute-start | bytes 786440 | tf_op jit(solution)/shard_map/ppermute | solution.py:396
  3.2 0.1 stage_rows.1
  3.3 0.1 collective-permute-start
  3.4 0.5 %collective-permute-start.4 = (bf16[4,64,256]{2,1,0:T(8,128)(2,1)S(1)}, bf16[4,64,256]{2,1,0:T(8,128)(2,1)S(1)}, u32[]{:S(2)}, u32[]{:S(2)}) collective-permute-start(bf16[4,64,256]{2,1,0:T(8,128)(2,1)S(1)} %get-tuple-element.65), channel_id=1, source_target_pairs={{0,4},{4,0},{1,5},{5,1},{2,6},{6,2},{3,7},{7,3},{8,12},{12,8},{9,1... | collective-permute-start | bytes 393224 | tf_op jit(solution)/shard_map/ppermute | solution.py:450
  3.9 0.1 collective-permute-start.5
  4.0 0.6 %collective-permute-done.edges = bf16[8,8,256]{2,1,0:T(8,128)(2,1)S(1)} collective-permute-done((bf16[8,8,256]{2,1,0:T(8,128)(2,1)S(1)}, bf16[8,8,256]{2,1,0:T(8,128)(2,1)S(1)}, u32[]{:S(2)}, u32[]{:S(2)}) %collective-permute-start) | collective-permute-done | bytes 32800 | tf_op jit(solution)/shard_map/ppermute | solution.py:449
  4.6 0.2 %collective-permute-start.1 = (bf16[4,136,256]{2,1,0:T(8,128)(2,1)S(1)}, bf16[4,136,256]{2,1,0:T(8,128)(2,1)S(1)}, u32[]{:S(2)}, u32[]{:S(2)}) collective-permute-start(bf16[4,136,256]{2,1,0:T(8,128)(2,1)S(1)} %get-tuple-element.44), channel_id=1, source_target_pairs={{0,8},{4,0},{8,16},{12,4},{16,24},{20,12},{24,28},{28,20},{1,9},{5... | collective-permute-start | bytes 835592 | tf_op jit(solution)/shard_map/ppermute | solution.py:464
  4.8 1.3 %collective-permute-start.3 = (bf16[4,8,256]{2,1,0:T(8,128)(2,1)S(1)}, bf16[4,8,256]{2,1,0:T(8,128)(2,1)S(1)}, u32[]{:S(2)}, u32[]{:S(2)}) collective-permute-start(bf16[4,8,256]{2,1,0:T(8,128)(2,1)S(1)} %get-tuple-element.45), channel_id=1, source_target_pairs={{0,4},{4,12},{8,0},{12,20},{16,8},{20,28},{24,16},{28,24},{1,5},{5... | collective-permute-start | bytes 49160 | tf_op jit(solution)/shard_map/ppermute | solution.py:465
  6.1 1.5 %filter_weights.1 = (bf16[2,256,128]{2,1,0:T(8,128)(2,1)S(1)}, bf16[512,256]{1,0:T(8,128)(2,1)S(1)}, bf16[128,256]{1,0:T(8,128)(2,1)S(1)}, bf16[4,8,256]{2,1,0:T...) custom-call(s32[8]{0:T(128)} %start_in.1, ...), custom_call_target="tpu_custom_call", output_to_operand_aliasing={{0}: (6, {}), {1}: (7, {}), {2}: (8, {}), {3}: (9, {}), {4}... | custom-call | flops 100000 | bytes 1000 | tf_op jit(solution)/shard_map/filter_weights/pallas_call | solution.py:467
  7.6 1.5 %own_rows.1 = (f32[8,128,256]{2,1,0:T(8,128)S(1)}, bf16[4,512,256]{2,1,0:T(8,128)(2,1)S(1)}) custom-call(bf16[4,512,256]{2,1,0:T(8,128)(2,1)S(1)} %get-tuple-element.58.turned_in, bf16[512,256]{1,0:T(8,128)(2,1)S(1)} %get-tuple-element.59.own_weights, bf16[4,8,256]{2,1,0:T(8,128)(2,1)S(1)} %get-tuple-element.60.cycle_taps, ...), custom_call_target="tpu_custom_call", output_to_operand_aliasing={{1}: (0, {})} | custom-call | flops 100000 | bytes 1000 | tf_op jit(solution)/shard_map/own_rows/pallas_call | solution.py:478
  9.1 0.0 collective-permute-done.4.polar_left
  9.1 0.0 collective-permute-done.5.polar_right
  9.1 1.7 %partner_columns.1.acc = f32[8,128,256]{2,1,0:T(8,128)S(1)} custom-call(f32[8,128,256]{2,1,0:T(8,128)S(1)} %get-tuple-element.62.acc_in, bf16[512,256]{1,0:T(8,128)(2,1)S(1)} %get-tuple-element.59.own_weights, bf16[128,256]{1,0:T(8,128)(2,1)S(1)} %get-tuple-element.63.polar_weights, ...), custom_call_target="tpu_custom_call", output_to_operand_aliasing={{}: (0, {})} | custom-call | flops 100000 | bytes 1000 | tf_op jit(solution)/shard_map/partner_columns/pallas_call | solution.py:498
  10.8 0.0 collective-permute-done.3.edges
  10.8 0.0 collective-permute-done.2.halo
  10.8 0.1 %collective-permute-done.1.halo = bf16[4,136,256]{2,1,0:T(8,128)(2,1)S(1)} collective-permute-done((bf16[4,136,256]{2,1,0:T(8,128)(2,1)S(1)}, bf16[4,136,256]{2,1,0:T(8,128)(2,1)S(1)}, u32[]{:S(2)}, u32[]{:S(2)}) %collective-permute-start.1) | collective-permute-done | bytes 278560 | tf_op jit(solution)/shard_map/ppermute | solution.py:464
  11.0 1.4 %late_side.1 = bf16[8,128,256]{2,1,0:T(8,128)(2,1)} custom-call(bf16[4,128,256]{2,1,0:T(8,128)(2,1)S(1)} %early_side.1.early, bf16[4,136,256]{2,1,0:T(8,128)(2,1)S(1)} %collective-permute-done.1.halo, bf16[2,256,128]{2,1,0:T(8,128)(2,1)S(1)} %get-tuple-element.69.weights, f32[8,128,256]{2,1,0:T(8,128)S(1)} %partner_columns.1.acc, ...), custom_call_target="tpu_custom_call" | custom-call | tf_op jit(solution)/shard_map/late_side/pallas_call | solution.py:534
  (2 shorter events, 0.1 us)
Async XLA Ops:
  1.1 9.7 %collective-permute-start.2 = (bf16[4,128,256]{2,1,0:T(8,128)(2,1)S(1)}, bf16[4,128,256]{2,1,0:T(8,128)(2,1)S(1)}, u32[]{:S(2)}, u32[]{:S(2)}) collective-permute-start(bf16[4,128,256]{2,1,0:T(8,128)(2,1)S(1)} %get-tuple-element.40.going), channel_id=1, source_target_pairs={{0,4},{4,12},{8,0},{12,20},{16,8},{20,28},{24,16},{28,24},{1,5},{5... | collective-permute-start | bytes 786440 | tf_op jit(solution)/shard_map/ppermute | solution.py:396
  3.3 1.3 %collective-permute-start = (bf16[8,8,256]{2,1,0:T(8,128)(2,1)S(1)}, bf16[8,8,256]{2,1,0:T(8,128)(2,1)S(1)}, u32[]{:S(2)}, u32[]{:S(2)}) collective-permute-start(bf16[8,8,256]{2,1,0:T(8,128)(2,1)S(1)} %get-tuple-element.43), channel_id=1, source_target_pairs={{0,4},{4,0},{1,5},{5,1},{2,6},{6,2},{3,7},{7,3},{8,12},{12,8},{9,1... | collective-permute-start | bytes 98312 | tf_op jit(solution)/shard_map/ppermute | solution.py:449
  3.4 5.7 %collective-permute-start.4 = (bf16[4,64,256]{2,1,0:T(8,128)(2,1)S(1)}, bf16[4,64,256]{2,1,0:T(8,128)(2,1)S(1)}, u32[]{:S(2)}, u32[]{:S(2)}) collective-permute-start(bf16[4,64,256]{2,1,0:T(8,128)(2,1)S(1)} %get-tuple-element.65), channel_id=1, source_target_pairs={{0,4},{4,0},{1,5},{5,1},{2,6},{6,2},{3,7},{7,3},{8,12},{12,8},{9,1... | collective-permute-start | bytes 393224 | tf_op jit(solution)/shard_map/ppermute | solution.py:450
  3.9 5.2 %collective-permute-start.5 = (bf16[4,64,256]{2,1,0:T(8,128)(2,1)S(1)}, bf16[4,64,256]{2,1,0:T(8,128)(2,1)S(1)}, u32[]{:S(2)}, u32[]{:S(2)}) collective-permute-start(bf16[4,64,256]{2,1,0:T(8,128)(2,1)S(1)} %get-tuple-element.66), channel_id=1, source_target_pairs={{0,4},{4,0},{1,5},{5,1},{2,6},{6,2},{3,7},{7,3},{8,12},{12,8},{9,1... | collective-permute-start | bytes 393224 | tf_op jit(solution)/shard_map/ppermute | solution.py:451
  4.6 6.3 %collective-permute-start.1 = (bf16[4,136,256]{2,1,0:T(8,128)(2,1)S(1)}, bf16[4,136,256]{2,1,0:T(8,128)(2,1)S(1)}, u32[]{:S(2)}, u32[]{:S(2)}) collective-permute-start(bf16[4,136,256]{2,1,0:T(8,128)(2,1)S(1)} %get-tuple-element.44), channel_id=1, source_target_pairs={{0,8},{4,0},{8,16},{12,4},{16,24},{20,12},{24,28},{28,20},{1,9},{5... | collective-permute-start | bytes 835592 | tf_op jit(solution)/shard_map/ppermute | solution.py:464
  4.8 6.0 %collective-permute-start.3 = (bf16[4,8,256]{2,1,0:T(8,128)(2,1)S(1)}, bf16[4,8,256]{2,1,0:T(8,128)(2,1)S(1)}, u32[]{:S(2)}, u32[]{:S(2)}) collective-permute-start(bf16[4,8,256]{2,1,0:T(8,128)(2,1)S(1)} %get-tuple-element.45), channel_id=1, source_target_pairs={{0,4},{4,12},{8,0},{12,20},{16,8},{20,28},{24,16},{28,24},{1,5},{5... | collective-permute-start | bytes 49160 | tf_op jit(solution)/shard_map/ppermute | solution.py:465

commit v18 on v16

--- a/solution.py
+++ b/solution.py
@@ -169,13 +169,23 @@
         copies[5].wait()
 
 
-def stage_kernel(
-    start_in, width_in, lon_in, lat_in, cycle_in, mixing_in, going, staying,
-    whole, edges, polar_left, polar_right, *refs,
+def edge_kernel(
+    start_in, width_in, lon_in, lat_in, cycle_in, mixing_in, going, staying, edges, *refs,
 ):
     weight_kernel(False, start_in, width_in, lon_in, lat_in, cycle_in, mixing_in, *refs)
+    cols = going.shape[1]
+    reach = edges.shape[1] // 2
+    is_first = lax.axis_index("lon") == 0
+    for p in range(HALO):
+        for r, first, second in ((p, going, staying), (HALO + p, staying, going)):
+            for n, at in enumerate((slice(0, reach), slice(cols - reach, cols))):
+                edges[r, n * reach : (n + 1) * reach, :] = jnp.where(
+                    is_first, first[p, at, :], second[p, at, :]
+                )
+
+
+def stage_kernel(going, staying, whole, polar_left, polar_right):
     cols = whole.shape[1]
-    reach = edges.shape[1] // 2
     is_first = lax.axis_index("lon") == 0
     at_top = lax.axis_index("lat") == 0
     for p in range(HALO):
@@ -183,9 +193,7 @@
         lower = jnp.where(is_first, staying[p], going[p])
         polar = jnp.where(at_top, upper, lower)
         polar_left[p], polar_right[p] = polar[: cols // 2], polar[cols // 2 :]
-        for r, row in ((p, upper), (HALO + p, lower)):
-            whole[r] = row
-            edges[r] = jnp.concatenate([row[:reach], row[cols - reach :]], axis=0)
+        whole[p], whole[HALO + p] = upper, lower
 
 
 def pack_kernel(whole, edges, message, corners):
@@ -418,22 +426,30 @@
         pltpu.VMEM((128, 128), F32),
         pltpu.SemaphoreType.DMA((6,)),
     ]
-    whole, edges, polar_left, polar_right, *made = pl.pallas_call(
+    edges, *made = pl.pallas_call(
+        edge_kernel,
+        out_shape=(sds((rows, 2 * reach, chans), BF16), *weight_shapes),
+        in_specs=[hbm] * 6 + [vmem] * 2,
+        out_specs=[vmem] * 7,
+        scratch_shapes=weight_scratch,
+        compiler_params=limit,
+        cost_estimate=small,
+        name="stage_edges",
+    )(*operands, going, staying)
+    going, staying, edges = lax.optimization_barrier((going, staying, edges))
+    whole, polar_left, polar_right = pl.pallas_call(
         stage_kernel,
         out_shape=(
             sds((rows, cols, chans), BF16),
-            sds((rows, 2 * reach, chans), BF16),
             sds((polar, cols // 2, chans), BF16),
             sds((polar, cols // 2, chans), BF16),
-            *weight_shapes,
         ),
-        in_specs=[hbm] * 6 + [vmem] * 2,
-        out_specs=[vmem] * 10,
-        scratch_shapes=weight_scratch,
+        in_specs=[vmem] * 2,
+        out_specs=[vmem] * 3,
         compiler_params=limit,
         cost_estimate=small,
         name="stage_rows",
-    )(*operands, going, staying)
+    )(going, staying)
     edges = lax.ppermute(edges, "lon", SWAP)
     polar_left = lax.ppermute(polar_left, "lon", SWAP)
     polar_right = lax.ppermute(polar_right, "lon", SWAP)

time: 12.6 us -> 12.6 us (level)
    ppermute x1, waiting for transfers between devices: 0.62 us -> 0.49 us  [shards(): edges = lax.ppermute(edges, 'lon', SWAP)]
where the time goes in v18:
time: 12.6 us; the launch traced here: 12.4 us
  Pallas kernels  6.23 us (49%)
  starting transfers between devices  4.32 us (34%)
  other arithmetic  1.07 us (8%)
  waiting for transfers between devices  0.69 us (5%)
    ppermute x1, starting transfers between devices, shards(): second = lax.ppermute(going, axes, back)  2.14 us
    pallas_call x1, Pallas kernels, shards(): pl.pallas_call(partner_kernel, out_shape=sds((rows, cols, chans), F32), i...  1.66 us
    pallas_call x1, Pallas kernels, shards(): pl.pallas_call(own_kernel, out_shape=(sds((rows, cols, chans), F32), sds(...  1.48 us
    pallas_call x1, Pallas kernels, shards(): pl.pallas_call(functools.partial(weight_kernel, True), out_shape=weight_s...  1.46 us
    pallas_call x1, Pallas kernels, shards(): pl.pallas_call(late_kernel, out_shape=sds((rows, cols, chans), BF16), in_...  1.42 us
    ppermute x1, starting transfers between devices, shards(): second_edges = lax.ppermute(corners, axes, back)  1.3 us
    select_n x1, other arithmetic, shards(): staying = jnp.where(core == 0, tail, head)  1.07 us
    ppermute x1, starting transfers between devices, shards(): polar_left = lax.ppermute(polar_left, 'lon', SWAP)  0.55 us
  transfers between devices with their start and end apart: 6, of which 2 were waited for; matrix products, arithmetic and copies ran while one was open for 0% of the time, Pallas kernels for 39%

profile of v18, /device:TPU:1, one launch (start us, length us, event | category | flops | bytes accessed | tf_op | source)
XLA Modules:
  0.0 12.4 jit_solution(17275552961457879243)
XLA Ops:
  0.0 1.1 %broadcast_select_fusion = (bf16[4,128,256]{2,1,0:T(8,128)(2,1)S(1)}, bf16[4,128,256]{2,1,0:T(8,128)(2,1)S(1)}) fusion(pred[]{:T(512)S(6)} %eq.4, bf16[8,128,256]{2,1,0:T(8,128)(2,1)} %param.7), kind=kLoop, calls=%fused_computation | loop fusion | flops 262144 | bytes 1048577 | tf_op jit(solution)/shard_map/jit(_where)/select_n | solution.py:391
  1.1 2.1 %collective-permute-start.2 = (bf16[4,128,256]{2,1,0:T(8,128)(2,1)S(1)}, bf16[4,128,256]{2,1,0:T(8,128)(2,1)S(1)}, u32[]{:S(2)}, u32[]{:S(2)}) collective-permute-start(bf16[4,128,256]{2,1,0:T(8,128)(2,1)S(1)} %get-tuple-element.46.going), channel_id=1, source_target_pairs={{0,4},{4,12},{8,0},{12,20},{16,8},{20,28},{24,16},{28,24},{1,5},{5... | collective-permute-start | bytes 786440 | tf_op jit(solution)/shard_map/ppermute | solution.py:392
  3.2 0.1 stage_edges.1
  3.3 0.1 collective-permute-start
  3.4 0.1 stage_rows.1
  3.4 0.5 %collective-permute-start.4 = (bf16[4,64,256]{2,1,0:T(8,128)(2,1)S(1)}, bf16[4,64,256]{2,1,0:T(8,128)(2,1)S(1)}, u32[]{:S(2)}, u32[]{:S(2)}) collective-permute-start(bf16[4,64,256]{2,1,0:T(8,128)(2,1)S(1)} %get-tuple-element.71), channel_id=1, source_target_pairs={{0,4},{4,0},{1,5},{5,1},{2,6},{6,2},{3,7},{7,3},{8,12},{12,8},{9,1... | collective-permute-start | bytes 393224 | tf_op jit(solution)/shard_map/ppermute | solution.py:454
  4.0 0.1 collective-permute-start.5
  4.1 0.5 %collective-permute-done.edges = bf16[8,8,256]{2,1,0:T(8,128)(2,1)S(1)} collective-permute-done((bf16[8,8,256]{2,1,0:T(8,128)(2,1)S(1)}, bf16[8,8,256]{2,1,0:T(8,128)(2,1)S(1)}, u32[]{:S(2)}, u32[]{:S(2)}) %collective-permute-start) | collective-permute-done | bytes 32800 | tf_op jit(solution)/shard_map/ppermute | solution.py:453
  4.6 0.2 %collective-permute-start.1 = (bf16[4,136,256]{2,1,0:T(8,128)(2,1)S(1)}, bf16[4,136,256]{2,1,0:T(8,128)(2,1)S(1)}, u32[]{:S(2)}, u32[]{:S(2)}) collective-permute-start(bf16[4,136,256]{2,1,0:T(8,128)(2,1)S(1)} %get-tuple-element.50), channel_id=1, source_target_pairs={{0,8},{4,0},{8,16},{12,4},{16,24},{20,12},{24,28},{28,20},{1,9},{5... | collective-permute-start | bytes 835592 | tf_op jit(solution)/shard_map/ppermute | solution.py:468
  4.8 1.3 %collective-permute-start.3 = (bf16[4,8,256]{2,1,0:T(8,128)(2,1)S(1)}, bf16[4,8,256]{2,1,0:T(8,128)(2,1)S(1)}, u32[]{:S(2)}, u32[]{:S(2)}) collective-permute-start(bf16[4,8,256]{2,1,0:T(8,128)(2,1)S(1)} %get-tuple-element.51), channel_id=1, source_target_pairs={{0,4},{4,12},{8,0},{12,20},{16,8},{20,28},{24,16},{28,24},{1,5},{5... | collective-permute-start | bytes 49160 | tf_op jit(solution)/shard_map/ppermute | solution.py:469
  6.1 1.5 %filter_weights.1 = (bf16[2,256,128]{2,1,0:T(8,128)(2,1)S(1)}, bf16[512,256]{1,0:T(8,128)(2,1)S(1)}, bf16[128,256]{1,0:T(8,128)(2,1)S(1)}, bf16[4,8,256]{2,1,0:T...) custom-call(s32[8]{0:T(128)} %start_in.1, ...), custom_call_target="tpu_custom_call", output_to_operand_aliasing={{0}: (6, {}), {1}: (7, {}), {2}: (8, {}), {3}: (9, {}), {4}... | custom-call | flops 100000 | bytes 1000 | tf_op jit(solution)/shard_map/filter_weights/pallas_call | solution.py:471
  7.5 1.5 %own_rows.1 = (f32[8,128,256]{2,1,0:T(8,128)S(1)}, bf16[4,512,256]{2,1,0:T(8,128)(2,1)S(1)}) custom-call(bf16[4,512,256]{2,1,0:T(8,128)(2,1)S(1)} %get-tuple-element.64.turned_in, bf16[512,256]{1,0:T(8,128)(2,1)S(1)} %get-tuple-element.65.own_weights, bf16[4,8,256]{2,1,0:T(8,128)(2,1)S(1)} %get-tuple-element.66.cycle_taps, ...), custom_call_target="tpu_custom_call", output_to_operand_aliasing={{1}: (0, {})} | custom-call | flops 100000 | bytes 1000 | tf_op jit(solution)/shard_map/own_rows/pallas_call | solution.py:482
  9.0 0.0 collective-permute-done.4.polar_left
  9.0 0.0 collective-permute-done.5.polar_right
  9.1 1.7 %partner_columns.1.acc = f32[8,128,256]{2,1,0:T(8,128)S(1)} custom-call(f32[8,128,256]{2,1,0:T(8,128)S(1)} %get-tuple-element.68.acc_in, bf16[512,256]{1,0:T(8,128)(2,1)S(1)} %get-tuple-element.65.own_weights, bf16[128,256]{1,0:T(8,128)(2,1)S(1)} %get-tuple-element.69.polar_weights, ...), custom_call_target="tpu_custom_call", output_to_operand_aliasing={{}: (0, {})} | custom-call | flops 100000 | bytes 1000 | tf_op jit(solution)/shard_map/partner_columns/pallas_call | solution.py:502
  10.7 0.0 collective-permute-done.3.edges
  10.7 0.0 collective-permute-done.2.halo
  10.8 0.2 %collective-permute-done.1.halo = bf16[4,136,256]{2,1,0:T(8,128)(2,1)S(1)} collective-permute-done((bf16[4,136,256]{2,1,0:T(8,128)(2,1)S(1)}, bf16[4,136,256]{2,1,0:T(8,128)(2,1)S(1)}, u32[]{:S(2)}, u32[]{:S(2)}) %collective-permute-start.1) | collective-permute-done | bytes 278560 | tf_op jit(solution)/shard_map/ppermute | solution.py:468
  11.0 1.4 %late_side.1 = bf16[8,128,256]{2,1,0:T(8,128)(2,1)} custom-call(bf16[4,128,256]{2,1,0:T(8,128)(2,1)S(1)} %early_side.1.early, bf16[4,136,256]{2,1,0:T(8,128)(2,1)S(1)} %collective-permute-done.1.halo, bf16[2,256,128]{2,1,0:T(8,128)(2,1)S(1)} %get-tuple-element.75.weights, f32[8,128,256]{2,1,0:T(8,128)S(1)} %partner_columns.1.acc, ...), custom_call_target="tpu_custom_call" | custom-call | tf_op jit(solution)/shard_map/late_side/pallas_call | solution.py:538
  (2 shorter events, 0.1 us)
Async XLA Ops:
  1.1 9.7 %collective-permute-start.2 = (bf16[4,128,256]{2,1,0:T(8,128)(2,1)S(1)}, bf16[4,128,256]{2,1,0:T(8,128)(2,1)S(1)}, u32[]{:S(2)}, u32[]{:S(2)}) collective-permute-start(bf16[4,128,256]{2,1,0:T(8,128)(2,1)S(1)} %get-tuple-element.46.going), channel_id=1, source_target_pairs={{0,4},{4,12},{8,0},{12,20},{16,8},{20,28},{24,16},{28,24},{1,5},{5... | collective-permute-start | bytes 786440 | tf_op jit(solution)/shard_map/ppermute | solution.py:392
  3.3 1.3 %collective-permute-start = (bf16[8,8,256]{2,1,0:T(8,128)(2,1)S(1)}, bf16[8,8,256]{2,1,0:T(8,128)(2,1)S(1)}, u32[]{:S(2)}, u32[]{:S(2)}) collective-permute-start(bf16[8,8,256]{2,1,0:T(8,128)(2,1)S(1)} %get-tuple-element.49), channel_id=1, source_target_pairs={{0,4},{4,0},{1,5},{5,1},{2,6},{6,2},{3,7},{7,3},{8,12},{12,8},{9,1... | collective-permute-start | bytes 98312 | tf_op jit(solution)/shard_map/ppermute | solution.py:453
  3.4 5.6 %collective-permute-start.4 = (bf16[4,64,256]{2,1,0:T(8,128)(2,1)S(1)}, bf16[4,64,256]{2,1,0:T(8,128)(2,1)S(1)}, u32[]{:S(2)}, u32[]{:S(2)}) collective-permute-start(bf16[4,64,256]{2,1,0:T(8,128)(2,1)S(1)} %get-tuple-element.71), channel_id=1, source_target_pairs={{0,4},{4,0},{1,5},{5,1},{2,6},{6,2},{3,7},{7,3},{8,12},{12,8},{9,1... | collective-permute-start | bytes 393224 | tf_op jit(solution)/shard_map/ppermute | solution.py:454
  4.0 5.1 %collective-permute-start.5 = (bf16[4,64,256]{2,1,0:T(8,128)(2,1)S(1)}, bf16[4,64,256]{2,1,0:T(8,128)(2,1)S(1)}, u32[]{:S(2)}, u32[]{:S(2)}) collective-permute-start(bf16[4,64,256]{2,1,0:T(8,128)(2,1)S(1)} %get-tuple-element.72), channel_id=1, source_target_pairs={{0,4},{4,0},{1,5},{5,1},{2,6},{6,2},{3,7},{7,3},{8,12},{12,8},{9,1... | collective-permute-start | bytes 393224 | tf_op jit(solution)/shard_map/ppermute | solution.py:455
  4.6 6.4 %collective-permute-start.1 = (bf16[4,136,256]{2,1,0:T(8,128)(2,1)S(1)}, bf16[4,136,256]{2,1,0:T(8,128)(2,1)S(1)}, u32[]{:S(2)}, u32[]{:S(2)}) collective-permute-start(bf16[4,136,256]{2,1,0:T(8,128)(2,1)S(1)} %get-tuple-element.50), channel_id=1, source_target_pairs={{0,8},{4,0},{8,16},{12,4},{16,24},{20,12},{24,28},{28,20},{1,9},{5... | collective-permute-start | bytes 835592 | tf_op jit(solution)/shard_map/ppermute | solution.py:468
  4.8 6.0 %collective-permute-start.3 = (bf16[4,8,256]{2,1,0:T(8,128)(2,1)S(1)}, bf16[4,8,256]{2,1,0:T(8,128)(2,1)S(1)}, u32[]{:S(2)}, u32[]{:S(2)}) collective-permute-start(bf16[4,8,256]{2,1,0:T(8,128)(2,1)S(1)} %get-tuple-element.51), channel_id=1, source_target_pairs={{0,4},{4,12},{8,0},{12,20},{16,8},{20,28},{24,16},{28,24},{1,5},{5... | collective-permute-start | bytes 49160 | tf_op jit(solution)/shard_map/ppermute | solution.py:469
